TPU v7x, 32 devices: a whole 2x2x4 slice. The times are simulated.
32 devices in a mesh: dp: 2 (over y), seq: 16 (over z, x, core).
Axes of the slice: x: 2, y: 2, z: 4, core: 2. Of those that a mesh axis runs over, the one named last changes fastest.
Arguments:
- frames_in: bfloat16 [2, 32, 256, 1024], P(None, ('dp', 'seq')), may hold values from -6 to 6
- cotangent: bfloat16 [2, 32, 256, 1024], P(None, ('dp', 'seq')), may hold values from -6 to 6
- lengths: int32 [2, 2], P(None, 'dp'), may hold values from 4 to 16, as said below
- actions: int32 [2, 32], P(None, ('dp', 'seq')), may hold values from 0 to 7
- spatial_in: bfloat16 [1024, 3072], P('seq', 'dp'), may hold values from -0.1875 to 0.1875
- spatial_out: bfloat16 [1024, 1024], P('seq', 'dp'), may hold values from -1 to 1
- temporal_in: bfloat16 [1024, 3072], P('seq', 'dp'), may hold values from -0.1875 to 0.1875
- temporal_out: bfloat16 [1024, 1024], P('seq', 'dp'), may hold values from -0.375 to 0.375
- hidden_in: bfloat16 [1024, 4096], P('seq', 'dp'), may hold values from -0.1875 to 0.1875
- hidden_out: bfloat16 [4096, 1024], P('seq', 'dp'), may hold values from -0.09375 to 0.09375
- norm_gains: bfloat16 [3, 1024], P(None, 'seq'), may hold values from 0.25 to 1.75
- norm_shifts: bfloat16 [3, 1024], P(None, 'seq'), may hold values from -4 to 4
- bias_up: bfloat16 [4096], P('seq'), may hold values from -6 to 6
- bias_down: bfloat16 [1024], P('seq'), may hold values from -4 to 4
- action_table: bfloat16 [8, 1024], P(None, 'seq'), may hold values from -6 to 6
Outputs:
- layer_out: bfloat16 [2, 32, 256, 1024], P(None, ('dp', 'seq'))
- frames_gradient: bfloat16 [2, 32, 256, 1024], P(None, ('dp', 'seq'))
- spatial_in_gradient: float32 [1024, 3072], P('seq', 'dp')
- spatial_out_gradient: float32 [1024, 1024], P('seq', 'dp')
- temporal_in_gradient: float32 [1024, 3072], P('seq', 'dp')
- temporal_out_gradient: float32 [1024, 1024], P('seq', 'dp')
- hidden_in_gradient: float32 [1024, 4096], P('seq', 'dp')
- hidden_out_gradient: float32 [4096, 1024], P('seq', 'dp')
- gains_gradient: float32 [3, 1024], P(None, 'seq')
- shifts_gradient: float32 [3, 1024], P(None, 'seq')
- bias_up_gradient: float32 [4096], P('seq')
- bias_down_gradient: float32 [1024], P('seq')
- table_gradient: float32 [8, 1024], P(None, 'seq')
Inputs may be any that keep to these rules, and one draw needn't show every extreme that they name: `lengths`: frames at or past a video's length are padding. In each micro-batch, among the 1 videos of each index of dp, exactly one has 16 live frames.
All inputs are finite; a program needn't handle non-finite values.
Results may differ from a plain program's by a relative error of at most 0.018.
Values may be sent and summed in bfloat16 or wider, within the bound.
A program may use at most 256 MiB of HBM per device.

v0:
```python
from functools import partial

import jax
import jax.numpy as jnp
from jax import lax
from jax.sharding import PartitionSpec as P

HEADS = 16
HDIM = 64
ACTIONS = 8
FRAMES = 16
MB = 2


EPS = 1e-05
NEG = -1e30
HIGH = lax.Precision.HIGHEST
SPACE_FORMS = ("fqhd,fkhd->fhqk", "fhqk,fkhd->fqhd", "fhqk,fqhd->fkhd")
TIME_FORMS = ("vqshd,vkshd->vshqk", "vshqk,vkshd->vqshd", "vshqk,vqshd->vkshd")


def layer_norm(value, gain_row, shift_row):
    centre = jnp.mean(value, axis=-1, keepdims=True)
    offset = value - centre
    spread = jnp.mean(offset * offset, axis=-1, keepdims=True)
    return offset * lax.rsqrt(spread + EPS) * gain_row + shift_row


def norm_back(value, gain_row, shift_row, upstream):
    result, pullback = jax.vjp(layer_norm, value, gain_row, shift_row)
    return pullback(upstream)


def dot_out(rows, weight):
    return jnp.dot(rows, weight, preferred_element_type=jnp.float32)


def dot_back(upstream, weight):
    return lax.dot_general(
        upstream,
        weight,
        (((upstream.ndim - 1,), (1,)), ((), ())),
        preferred_element_type=jnp.float32,
    )


def weight_grad(rows, upstream):
    flat_rows = rows.reshape(-1, rows.shape[-1])
    flat_up = upstream.reshape(-1, upstream.shape[-1])
    return lax.dot_general(
        flat_rows, flat_up, (((0,), (0,)), ((), ())), preferred_element_type=jnp.float32
    )


def masked_scores(queries, key_rows, allowed, forms, scale):
    scores = jnp.einsum(forms[0], queries, key_rows, preferred_element_type=jnp.float32) * scale
    if allowed is None:
        return scores
    return jnp.where(allowed, scores, NEG)


def attend_fwd(queries, key_rows, values, allowed, forms, scale):
    scores = masked_scores(queries, key_rows, allowed, forms, scale)
    peak = jnp.max(scores, axis=-1, keepdims=True)
    raised = jnp.exp(scores - peak)
    total = jnp.sum(raised, axis=-1, keepdims=True)
    prob_rows = (raised / total).astype(jnp.bfloat16)
    mixed = jnp.einsum(forms[1], prob_rows, values, preferred_element_type=jnp.float32).astype(
        jnp.bfloat16
    )
    return (mixed, peak + jnp.log(total))


def attend_back(queries, key_rows, values, allowed, log_total, upstream, forms, scale):
    scores = masked_scores(queries, key_rows, allowed, forms, scale)
    prob_full = jnp.exp(scores - log_total)
    prob_rows = prob_full.astype(jnp.bfloat16)
    prob_grad = jnp.einsum(forms[0], upstream, values, preferred_element_type=jnp.float32)
    value_grad = jnp.einsum(forms[2], prob_rows, upstream, preferred_element_type=jnp.float32)
    inner = jnp.sum(prob_full * prob_grad, axis=-1, keepdims=True)
    score_grad = (prob_full * (prob_grad - inner) * scale).astype(jnp.bfloat16)
    query_grad = jnp.einsum(forms[1], score_grad, key_rows, preferred_element_type=jnp.float32)
    key_grad = jnp.einsum(forms[2], score_grad, queries, preferred_element_type=jnp.float32)
    return (query_grad, key_grad, value_grad)


def collect(
    spatial_in,
    spatial_out,
    temporal_in,
    temporal_out,
    hidden_in,
    hidden_out,
    norm_gains,
    norm_shifts,
    bias_up,
    bias_down,
    action_table,
):
    wide = (
        lax.all_gather(spatial_in, "dp", axis=1, tiled=True),
        lax.all_gather(spatial_out, "dp", axis=1, tiled=True),
        lax.all_gather(temporal_in, "dp", axis=1, tiled=True),
        lax.all_gather(temporal_out, "dp", axis=1, tiled=True),
        lax.all_gather(hidden_in, "dp", axis=1, tiled=True),
        lax.all_gather(hidden_out, "dp", axis=1, tiled=True),
    )
    return (
        lax.all_gather(wide[0], "seq", axis=0, tiled=True),
        lax.all_gather(wide[1], "seq", axis=0, tiled=True),
        lax.all_gather(wide[2], "seq", axis=0, tiled=True),
        lax.all_gather(wide[3], "seq", axis=0, tiled=True),
        lax.all_gather(wide[4], "seq", axis=0, tiled=True),
        lax.all_gather(wide[5], "seq", axis=0, tiled=True),
        lax.all_gather(norm_gains, "seq", axis=1, tiled=True),
        lax.all_gather(norm_shifts, "seq", axis=1, tiled=True),
        lax.all_gather(bias_up, "seq", axis=0, tiled=True),
        lax.all_gather(bias_down, "seq", axis=0, tiled=True),
        lax.all_gather(action_table, "seq", axis=1, tiled=True),
    )


def body(
    frames_in,
    cotangent,
    lengths,
    actions,
    spatial_in,
    spatial_out,
    temporal_in,
    temporal_out,
    hidden_in,
    hidden_out,
    norm_gains,
    norm_shifts,
    bias_up,
    bias_down,
    action_table,
):
    scale = HDIM ** (-0.5)
    seq_count = lax.axis_size("seq")
    seq_place = lax.axis_index("seq")
    micro_count, frame_count, spatial_count, width = frames_in.shape
    video_count = frame_count * seq_count // FRAMES
    place_count = spatial_count // seq_count
    frame_rows = seq_place * frame_count + jnp.arange(frame_count, dtype=jnp.int32)
    frame_of = frame_rows % FRAMES
    video_of = frame_rows // FRAMES
    frame_ids = jnp.arange(FRAMES, dtype=jnp.int32)
    video_ids = jnp.arange(video_count, dtype=jnp.int32)
    shards = (
        spatial_in,
        spatial_out,
        temporal_in,
        temporal_out,
        hidden_in,
        hidden_out,
        norm_gains,
        norm_shifts,
        bias_up,
        bias_down,
        action_table,
    )
    totals = [
        jnp.zeros(
            piece.shape[:-2] + (piece.shape[-2] * seq_count, piece.shape[-1] * lax.axis_size("dp")),
            jnp.float32,
        )
        for piece in shards[:6]
    ]
    totals = totals + [
        jnp.zeros((3, width), jnp.float32),
        jnp.zeros((3, width), jnp.float32),
        jnp.zeros((bias_up.shape[0] * seq_count,), jnp.float32),
        jnp.zeros((width,), jnp.float32),
        jnp.zeros((ACTIONS, width), jnp.float32),
    ]
    out_list = []
    grad_list = []
    for micro_step in range(MB):
        forward_set = collect(
            spatial_in,
            spatial_out,
            temporal_in,
            temporal_out,
            hidden_in,
            hidden_out,
            norm_gains,
            norm_shifts,
            bias_up,
            bias_down,
            action_table,
        )
        (
            w_sin,
            w_sout,
            w_tin,
            w_tout,
            w_hin,
            w_hout,
            gain_set,
            shift_set,
            up_set,
            down_set,
            table_set,
        ) = forward_set
        gain_rows = gain_set.astype(jnp.float32)
        shift_rows = shift_set.astype(jnp.float32)
        up_shift = up_set.astype(jnp.float32)
        down_shift = down_set.astype(jnp.float32)
        table_rows = table_set.astype(jnp.float32)
        span_now = lengths[micro_step]
        live_span = jnp.sum(
            jnp.where(video_of[:, None] == video_ids[None, :], span_now[None, :], 0), axis=1
        )
        frame_live = (frame_of < live_span).astype(jnp.float32)[:, None, None]
        allowed = (
            (frame_ids[None, :] <= frame_ids[:, None])[None, :, :]
            & (frame_ids[None, None, :] < span_now[:, None, None])
        )[:, None, None, :, :]
        onehot = (actions[micro_step][:, None] == jnp.arange(ACTIONS)[None, :]).astype(jnp.float32)
        stream_in = (
            frames_in[micro_step].astype(jnp.float32)
            + jnp.dot(onehot, table_rows, precision=HIGH)[:, None, :]
        )
        normed_one = layer_norm(stream_in, gain_rows[0], shift_rows[0]).astype(jnp.bfloat16)
        packed_one = dot_out(normed_one, w_sin).astype(jnp.bfloat16)
        split_one = packed_one.reshape(frame_count, spatial_count, 3, HEADS, HDIM)
        mixed_one, total_one = attend_fwd(
            split_one[:, :, 0], split_one[:, :, 1], split_one[:, :, 2], None, SPACE_FORMS, scale
        )
        mixed_one = mixed_one.reshape(frame_count, spatial_count, width)
        stream_one = stream_in + dot_out(mixed_one, w_sout)
        normed_two = layer_norm(stream_one, gain_rows[1], shift_rows[1]).astype(jnp.bfloat16)
        packed_two = dot_out(normed_two, w_tin).astype(jnp.bfloat16)
        timed = lax.all_to_all(packed_two, "seq", split_axis=1, concat_axis=0, tiled=True)
        split_two = timed.reshape(video_count, FRAMES, place_count, 3, HEADS, HDIM)
        mixed_two, total_two = attend_fwd(
            split_two[:, :, :, 0],
            split_two[:, :, :, 1],
            split_two[:, :, :, 2],
            allowed,
            TIME_FORMS,
            scale,
        )
        back_two = lax.all_to_all(
            mixed_two.reshape(video_count * FRAMES, place_count, width),
            "seq",
            split_axis=0,
            concat_axis=1,
            tiled=True,
        )
        stream_two = stream_one + dot_out(back_two, w_tout)
        normed_three = layer_norm(stream_two, gain_rows[2], shift_rows[2]).astype(jnp.bfloat16)
        expand = dot_out(normed_three, w_hin) + up_shift
        active = jax.nn.gelu(expand, approximate=True).astype(jnp.bfloat16)
        stream_end = stream_two + dot_out(active, w_hout) + down_shift
        out_list.append((stream_end * frame_live).astype(jnp.bfloat16))
        backward_set = collect(
            spatial_in,
            spatial_out,
            temporal_in,
            temporal_out,
            hidden_in,
            hidden_out,
            norm_gains,
            norm_shifts,
            bias_up,
            bias_down,
            action_table,
        )
        (
            w_sin,
            w_sout,
            w_tin,
            w_tout,
            w_hin,
            w_hout,
            gain_set,
            shift_set,
            up_set,
            down_set,
            table_set,
        ) = backward_set
        gain_rows = gain_set.astype(jnp.float32)
        shift_rows = shift_set.astype(jnp.float32)
        upstream = cotangent[micro_step].astype(jnp.float32) * frame_live
        down_grad = jnp.sum(upstream, axis=(0, 1))
        end_low = upstream.astype(jnp.bfloat16)
        hout_grad = weight_grad(active, end_low)
        active_grad = dot_back(end_low, w_hout)
        result, gelu_pull = jax.vjp(partial(jax.nn.gelu, approximate=True), expand)
        expand_grad = gelu_pull(active_grad)[0]
        up_grad = jnp.sum(expand_grad, axis=(0, 1))
        expand_low = expand_grad.astype(jnp.bfloat16)
        hin_grad = weight_grad(normed_three, expand_low)
        three_in, three_gain, three_shift = norm_back(
            stream_two, gain_rows[2], shift_rows[2], dot_back(expand_low, w_hin)
        )
        stream_two_grad = upstream + three_in
        two_low = stream_two_grad.astype(jnp.bfloat16)
        tout_grad = weight_grad(back_two, two_low)
        mixed_two_grad = dot_back(two_low, w_tout).astype(jnp.bfloat16)
        timed_grad = lax.all_to_all(mixed_two_grad, "seq", split_axis=1, concat_axis=0, tiled=True)
        timed_grad = timed_grad.reshape(video_count, FRAMES, place_count, HEADS, HDIM)
        query_two, key_two, value_two = attend_back(
            split_two[:, :, :, 0],
            split_two[:, :, :, 1],
            split_two[:, :, :, 2],
            allowed,
            total_two,
            timed_grad,
            TIME_FORMS,
            scale,
        )
        packed_back = jnp.stack([query_two, key_two, value_two], axis=3).astype(jnp.bfloat16)
        packed_back = packed_back.reshape(video_count * FRAMES, place_count, 3 * width)
        packed_two_grad = lax.all_to_all(
            packed_back, "seq", split_axis=0, concat_axis=1, tiled=True
        )
        tin_grad = weight_grad(normed_two, packed_two_grad)
        two_in, two_gain, two_shift = norm_back(
            stream_one, gain_rows[1], shift_rows[1], dot_back(packed_two_grad, w_tin)
        )
        stream_one_grad = stream_two_grad + two_in
        one_low = stream_one_grad.astype(jnp.bfloat16)
        sout_grad = weight_grad(mixed_one, one_low)
        mixed_one_grad = dot_back(one_low, w_sout).astype(jnp.bfloat16)
        mixed_one_grad = mixed_one_grad.reshape(frame_count, spatial_count, HEADS, HDIM)
        query_one, key_one, value_one = attend_back(
            split_one[:, :, 0],
            split_one[:, :, 1],
            split_one[:, :, 2],
            None,
            total_one,
            mixed_one_grad,
            SPACE_FORMS,
            scale,
        )
        packed_one_grad = jnp.stack([query_one, key_one, value_one], axis=2).astype(jnp.bfloat16)
        packed_one_grad = packed_one_grad.reshape(frame_count, spatial_count, 3 * width)
        sin_grad = weight_grad(normed_one, packed_one_grad)
        one_in, one_gain, one_shift = norm_back(
            stream_in, gain_rows[0], shift_rows[0], dot_back(packed_one_grad, w_sin)
        )
        stream_in_grad = stream_one_grad + one_in
        grad_list.append(stream_in_grad.astype(jnp.bfloat16))
        frame_sums = jnp.sum(stream_in_grad, axis=1)
        table_grad = lax.dot_general(onehot, frame_sums, (((0,), (0,)), ((), ())), precision=HIGH)
        updates = [
            sin_grad,
            sout_grad,
            tin_grad,
            tout_grad,
            hin_grad,
            hout_grad,
            jnp.stack([one_gain, two_gain, three_gain]),
            jnp.stack([one_shift, two_shift, three_shift]),
            up_grad,
            down_grad,
            table_grad,
        ]
        totals = [old + new for old, new in zip(totals, updates)]
    summed = (
        lax.psum_scatter(
            totals[0].astype(jnp.bfloat16), "seq", scatter_dimension=0, tiled=True
        ).astype(jnp.float32),
        lax.psum_scatter(
            totals[1].astype(jnp.bfloat16), "seq", scatter_dimension=0, tiled=True
        ).astype(jnp.float32),
        lax.psum_scatter(
            totals[2].astype(jnp.bfloat16), "seq", scatter_dimension=0, tiled=True
        ).astype(jnp.float32),
        lax.psum_scatter(
            totals[3].astype(jnp.bfloat16), "seq", scatter_dimension=0, tiled=True
        ).astype(jnp.float32),
        lax.psum_scatter(
            totals[4].astype(jnp.bfloat16), "seq", scatter_dimension=0, tiled=True
        ).astype(jnp.float32),
        lax.psum_scatter(
            totals[5].astype(jnp.bfloat16), "seq", scatter_dimension=0, tiled=True
        ).astype(jnp.float32),
        lax.psum_scatter(
            totals[6].astype(jnp.bfloat16), "seq", scatter_dimension=1, tiled=True
        ).astype(jnp.float32),
        lax.psum_scatter(
            totals[7].astype(jnp.bfloat16), "seq", scatter_dimension=1, tiled=True
        ).astype(jnp.float32),
        lax.psum_scatter(
            totals[8].astype(jnp.bfloat16), "seq", scatter_dimension=0, tiled=True
        ).astype(jnp.float32),
        lax.psum_scatter(
            totals[9].astype(jnp.bfloat16), "seq", scatter_dimension=0, tiled=True
        ).astype(jnp.float32),
        lax.psum_scatter(
            totals[10].astype(jnp.bfloat16), "seq", scatter_dimension=1, tiled=True
        ).astype(jnp.float32),
    )
    matrices = (
        lax.psum_scatter(
            summed[0].astype(jnp.bfloat16), "dp", scatter_dimension=1, tiled=True
        ).astype(jnp.float32),
        lax.psum_scatter(
            summed[1].astype(jnp.bfloat16), "dp", scatter_dimension=1, tiled=True
        ).astype(jnp.float32),
        lax.psum_scatter(
            summed[2].astype(jnp.bfloat16), "dp", scatter_dimension=1, tiled=True
        ).astype(jnp.float32),
        lax.psum_scatter(
            summed[3].astype(jnp.bfloat16), "dp", scatter_dimension=1, tiled=True
        ).astype(jnp.float32),
        lax.psum_scatter(
            summed[4].astype(jnp.bfloat16), "dp", scatter_dimension=1, tiled=True
        ).astype(jnp.float32),
        lax.psum_scatter(
            summed[5].astype(jnp.bfloat16), "dp", scatter_dimension=1, tiled=True
        ).astype(jnp.float32),
    )
    smalls = lax.psum((summed[6], summed[7], summed[8], summed[9], summed[10]), "dp")
    layer_out = jnp.stack(out_list)
    frames_gradient = jnp.stack(grad_list)
    return (
        layer_out,
        frames_gradient,
        matrices[0],
        matrices[1],
        matrices[2],
        matrices[3],
        matrices[4],
        matrices[5],
        smalls[0],
        smalls[1],
        smalls[2],
        smalls[3],
        smalls[4],
    )


def solution(mesh):
    in_specs = (
        P(None, ("dp", "seq"), None, None),
        P(None, ("dp", "seq"), None, None),
        P(None, "dp"),
        P(None, ("dp", "seq")),
        P("seq", "dp"),
        P("seq", "dp"),
        P("seq", "dp"),
        P("seq", "dp"),
        P("seq", "dp"),
        P("seq", "dp"),
        P(None, "seq"),
        P(None, "seq"),
        P("seq"),
        P("seq"),
        P(None, "seq"),
    )
    out_specs = (
        P(None, ("dp", "seq"), None, None),
        P(None, ("dp", "seq"), None, None),
        P("seq", "dp"),
        P("seq", "dp"),
        P("seq", "dp"),
        P("seq", "dp"),
        P("seq", "dp"),
        P("seq", "dp"),
        P(None, "seq"),
        P(None, "seq"),
        P("seq"),
        P("seq"),
        P(None, "seq"),
    )
    return jax.shard_map(body, mesh=mesh, in_specs=in_specs, out_specs=out_specs, check_vma=False)
```

profile of v0, /device:TPU:0, one launch (start us, length us, event | category | flops | bytes accessed | tf_op | source)
XLA Modules:
  0.0 1483.0 jit_solution(7199377856118581986)
XLA Ops:
  53.1 21.9 %all-gather.1 = bf16[16,64,3]{1,2,0:T(4,128)(2,1)S(1)} all-gather(bf16[1,64,3]{1,2,0:T(4,128)(2,1)S(1)} %bitcast.544), channel_id=1, replica_groups=mesh['dp'=2,'seq'=16] {'seq'}, dimensions={0}, use_global_device_ids=true | all-gather | bytes 6528 | tf_op jit(solution)/shard_map/all_gather | solution.py:115
  75.1 17.4 %all-gather.2 = bf16[16,64,3]{1,2,0:T(4,128)(2,1)S(1)} all-gather(bf16[1,64,3]{1,2,0:T(4,128)(2,1)S(1)} %bitcast.545), channel_id=1, replica_groups=mesh['dp'=2,'seq'=16] {'seq'}, dimensions={0}, use_global_device_ids=true | all-gather | bytes 6528 | tf_op jit(solution)/shard_map/all_gather | solution.py:116
  92.5 19.1 %all-gather = bf16[16,64,8]{1,2,0:T(8,128)(2,1)S(1)} all-gather(bf16[1,64,8]{1,2,0:T(8,128)(2,1)S(1)} %bitcast.543), channel_id=1, replica_groups=mesh['dp'=2,'seq'=16] {'seq'}, dimensions={0}, use_global_device_ids=true | all-gather | bytes 17408 | tf_op jit(solution)/shard_map/all_gather | solution.py:119
  129.6 55.8 %all-gather.15.cloned.1.call-done = bf16[1024,3072]{1,0:T(8,128)(2,1)} async-done(((bf16[64,3072]{1,0:T(8,128)(2,1)}), bf16[1024,3072]{1,0:T(8,128)(2,1)}) %all-gather.15.cloned.1.call-update) | async-done | bytes 6291472 | tf_op jit(solution)/shard_map/all_gather | solution.py:111
  258.0 20.5 %all-to-all-start.2 = ((bf16[16,2,24576]{2,1,0:T(2,128)(2,1)}), bf16[16,2,24576]{2,1,0:T(2,128)(2,1)}, u32[]{:S(2)}, u32[]{:S(2)}) async-start(bf16[16,2,24576]{2,1,0:T(2,128)(2,1)} %reshape.1895), calls=%async_computation.2 | async-start | bytes 3145728 | tf_op jit(solution)/shard_map/all_to_all | solution.py:236
  316.2 18.6 %all-to-all-done.2 = bf16[16,2,24576]{2,1,0:T(2,128)(2,1)} async-done(((bf16[16,2,24576]{2,1,0:T(2,128)(2,1)}), bf16[16,2,24576]{2,1,0:T(2,128)(2,1)}, u32[]{:S(2)}, u32[]{:S(2)}) %all-to-all-start.2) | async-done | bytes 1572896 | tf_op jit(solution)/shard_map/all_to_all | solution.py:236
  334.9 18.5 %all-to-all-start.1 = ((bf16[16,16,1024]{2,1,0:T(8,128)(2,1)}), bf16[16,16,1024]{2,1,0:T(8,128)(2,1)S(1)}, u32[]{:S(2)}, u32[]{:S(2)}) async-start(bf16[16,16,1024]{2,1,0:T(8,128)(2,1)} %reshape.1838), calls=%async_computation.1 | async-start | bytes 1048576 | tf_op jit(solution)/shard_map/all_to_all | solution.py:246
  397.9 32.0 %all-gather.3 = bf16[16,1,256]{2,1,0:T(2,128)(2,1)S(1)} all-gather(bf16[1,1,256]{2,1,0:T(2,128)(2,1)S(1)} %reshape.1872), channel_id=1, replica_groups=mesh['dp'=2,'seq'=16] {'seq'}, dimensions={0}, use_global_device_ids=true | all-gather | bytes 8704 | tf_op jit(solution)/shard_map/all_gather | solution.py:117
  564.7 31.9 %all-to-all-done.5 = bf16[16,16,3072]{2,1,0:T(8,128)(2,1)} async-done(((bf16[16,16,3072]{2,1,0:T(8,128)(2,1)}), bf16[16,16,3072]{2,1,0:T(8,128)(2,1)}, u32[]{:S(2)}, u32[]{:S(2)}) %all-to-all-start.5) | async-done | bytes 1572896 | tf_op jit(solution)/shard_map/all_to_all | solution.py:318
  624.4 14.5 all-to-all-done.6
  693.0 22.6 %all-to-all-done.7 = bf16[16,16,3072]{2,1,0:T(8,128)(2,1)} async-done(((bf16[16,16,3072]{2,1,0:T(8,128)(2,1)}), bf16[16,16,3072]{2,1,0:T(8,128)(2,1)}, u32[]{:S(2)}, u32[]{:S(2)}) %all-to-all-start.7) | async-done | bytes 1572896 | tf_op jit(solution)/shard_map/all_to_all | solution.py:318
  737.4 14.1 add_convert_fusion
  883.0 42.1 %reduce-scatter.42.cloned.1.call-done = bf16[256,1024]{1,0:T(8,128)(2,1)} async-done(((bf16[4096,1024]{1,0:T(8,128)(2,1)}), bf16[256,1024]{1,0:T(8,128)(2,1)}) %reduce-scatter.42.cloned.1.call-update) | async-done | bytes 524304 | tf_op jit(solution)/shard_map/reduce_scatter | solution.py:380
  925.2 108.2 %reduce-scatter.38.cloned.1.call-done = bf16[64,4096]{1,0:T(8,128)(2,1)} async-done(((bf16[1024,4096]{1,0:T(8,128)(2,1)}), bf16[64,4096]{1,0:T(8,128)(2,1)}) %reduce-scatter.38.cloned.1.call-update) | async-done | bytes 524304 | tf_op jit(solution)/shard_map/reduce_scatter | solution.py:377
  1036.8 62.1 %all-reduce.4 = (bf16[1024]{0:T(1024)(128)(2,1)S(1)}, bf16[4096]{0:T(1024)(128)(2,1)S(1)}, bf16[1024]{0:T(1024)(128)(2,1)S(1)}) all-reduce(bf16[1024]{0:T(1024)(128)(2,1)S(1)} %dynamic-update-slice, bf16[4096]{0:T(1024)(128)(2,1)S(1)} %add_convert_fusion.11, bf16[1024]{0:T(1024)(128)(2,1)S(1)} %add_convert_fusion.12), channel_id=1, replica_groups=mesh['dp'=2,'seq'=16] {'seq'}, use_global_device_ids=true, to_apply=%add | all-reduce | flops 6144 | bytes 24576
  1098.9 23.8 %reduce-scatter.30.cloned.1.call-done = bf16[64,3072]{1,0:T(8,128)(2,1)} async-done(((bf16[1024,3072]{1,0:T(8,128)(2,1)}), bf16[64,3072]{1,0:T(8,128)(2,1)}) %reduce-scatter.30.cloned.1.call-update) | async-done | bytes 393232 | tf_op jit(solution)/shard_map/reduce_scatter | solution.py:371
  1131.1 80.3 %reduce-scatter.22.cloned.1.call-done = bf16[64,3072]{1,0:T(8,128)(2,1)} async-done(((bf16[1024,3072]{1,0:T(8,128)(2,1)}), bf16[64,3072]{1,0:T(8,128)(2,1)}) %reduce-scatter.22.cloned.1.call-update) | async-done | bytes 393232 | tf_op jit(solution)/shard_map/reduce_scatter | solution.py:365
  1225.7 56.7 %reduce-scatter.46.cloned.1.call-done = bf16[64,3]{1,0:T(8,128)(2,1)} async-done(((bf16[1024,3]{1,0:T(8,128)(2,1)}), bf16[64,3]{1,0:T(8,128)(2,1)}) %reduce-scatter.46.cloned.1.call-update) | async-done | bytes 400
  1283.2 57.5 %reduce-scatter.48.cloned.1.call-done = bf16[64,3]{1,0:T(8,128)(2,1)} async-done(((bf16[1024,3]{1,0:T(8,128)(2,1)}), bf16[64,3]{1,0:T(8,128)(2,1)}) %reduce-scatter.48.cloned.1.call-update) | async-done | bytes 400
  1341.5 56.9 %reduce-scatter.50.cloned.1.call-done = bf16[64,8]{1,0:T(8,128)(2,1)} async-done(((bf16[1024,8]{1,0:T(8,128)(2,1)}), bf16[64,8]{1,0:T(8,128)(2,1)}) %reduce-scatter.50.cloned.1.call-update) | async-done | bytes 1040
  1411.3 15.2 %reduce-scatter.44.cloned.1.call-done = bf16[256,512]{1,0:T(8,128)(2,1)} async-done(((bf16[256,1024]{1,0:T(8,128)(2,1)}), bf16[256,512]{1,0:T(8,128)(2,1)}) %reduce-scatter.44.cloned.1.call-update) | async-done | bytes 262160 | tf_op jit(solution)/shard_map/reduce_scatter | solution.py:415
  1428.3 15.1 %reduce-scatter.40.cloned.1.call-done = bf16[64,2048]{1,0:T(8,128)(2,1)} async-done(((bf16[64,4096]{1,0:T(8,128)(2,1)}), bf16[64,2048]{1,0:T(8,128)(2,1)}) %reduce-scatter.40.cloned.1.call-update) | async-done | bytes 262160 | tf_op jit(solution)/shard_map/reduce_scatter | solution.py:412
  1445.2 13.5 reduce-scatter.32.cloned.1.call-done
  1460.4 13.8 reduce-scatter.24.cloned.1.call-done
  (565 shorter events, 630.9 us)
Async XLA Ops:
  7.2 107.6 %all-gather.11.cloned.1.call-start = ((), (), s32[]{:S(2)}) async-start(), calls=%async_computation.23 | async-start | bytes 6684672 | tf_op jit(solution)/shard_map/all_gather | solution.py:109
  17.9 108.8 %all-gather.13.cloned.1.call-start = ((), (), s32[]{:S(2)}) async-start(), calls=%async_computation.24 | async-start | bytes 2228224 | tf_op jit(solution)/shard_map/all_gather | solution.py:110
  23.2 162.2 %all-gather.15.cloned.1.call-start = ((), (), s32[]{:S(2)}) async-start(), calls=%async_computation.25 | async-start | bytes 6684672 | tf_op jit(solution)/shard_map/all_gather | solution.py:111
  31.0 399.5 %all-gather.17.cloned.1.call-start = ((), (), s32[]{:S(2)}) async-start(), calls=%async_computation.26 | async-start | bytes 2228224 | tf_op jit(solution)/shard_map/all_gather | solution.py:112
  36.3 402.7 %all-gather.19.cloned.1.call-start = ((), (), s32[]{:S(2)}) async-start(), calls=%async_computation.27 | async-start | bytes 8912896 | tf_op jit(solution)/shard_map/all_gather | solution.py:113
  44.8 406.9 %all-gather.21.cloned.1.call-start = ((), (), s32[]{:S(2)}) async-start(), calls=%async_computation.28 | async-start | bytes 8912896 | tf_op jit(solution)/shard_map/all_gather | solution.py:114
  212.4 45.6 %all-to-all-start = ((bf16[16,2,24576]{2,1,0:T(2,128)(2,1)}), bf16[16,2,24576]{2,1,0:T(2,128)(2,1)}, u32[]{:S(2)}, u32[]{:S(2)}) async-start(bf16[16,2,24576]{2,1,0:T(2,128)(2,1)} %reshape.1897), calls=%async_computation | async-start | bytes 3145728 | tf_op jit(solution)/shard_map/all_to_all | solution.py:236
  258.0 76.9 %all-to-all-start.2 = ((bf16[16,2,24576]{2,1,0:T(2,128)(2,1)}), bf16[16,2,24576]{2,1,0:T(2,128)(2,1)}, u32[]{:S(2)}, u32[]{:S(2)}) async-start(bf16[16,2,24576]{2,1,0:T(2,128)(2,1)} %reshape.1895), calls=%async_computation.2 | async-start | bytes 3145728 | tf_op jit(solution)/shard_map/all_to_all | solution.py:236
  334.9 55.6 %all-to-all-start.1 = ((bf16[16,16,1024]{2,1,0:T(8,128)(2,1)}), bf16[16,16,1024]{2,1,0:T(8,128)(2,1)S(1)}, u32[]{:S(2)}, u32[]{:S(2)}) async-start(bf16[16,16,1024]{2,1,0:T(8,128)(2,1)} %reshape.1838), calls=%async_computation.1 | async-start | bytes 1048576 | tf_op jit(solution)/shard_map/all_to_all | solution.py:246
  683.7 179.7 %reduce-scatter.34.cloned.1.call-start = ((), (), s32[]{:S(2)}) async-start(), calls=%async_computation.35 | async-start | bytes 2228224 | tf_op jit(solution)/shard_map/reduce_scatter | solution.py:374
  688.9 193.5 %reduce-scatter.26.cloned.1.call-start = ((), (), s32[]{:S(2)}) async-start(), calls=%async_computation.31 | async-start | bytes 2228224 | tf_op jit(solution)/shard_map/reduce_scatter | solution.py:368
  726.2 198.8 %reduce-scatter.42.cloned.1.call-start = ((), (), s32[]{:S(2)}) async-start(), calls=%async_computation.39 | async-start | bytes 8912896 | tf_op jit(solution)/shard_map/reduce_scatter | solution.py:380
  751.5 281.9 %reduce-scatter.38.cloned.1.call-start = ((), (), s32[]{:S(2)}) async-start(), calls=%async_computation.37 | async-start | bytes 8912896 | tf_op jit(solution)/shard_map/reduce_scatter | solution.py:377
  774.2 348.5 %reduce-scatter.30.cloned.1.call-start = ((), (), s32[]{:S(2)}) async-start(), calls=%async_computation.33 | async-start | bytes 6684672 | tf_op jit(solution)/shard_map/reduce_scatter | solution.py:371
  784.4 427.0 %reduce-scatter.22.cloned.1.call-start = ((), (), s32[]{:S(2)}) async-start(), calls=%async_computation.29 | async-start | bytes 6684672 | tf_op jit(solution)/shard_map/reduce_scatter | solution.py:365
  862.0 361.1 %reduce-scatter.36.cloned.1.call-start = ((), (), s32[]{:S(2)}) async-start(), calls=%async_computation.36 | async-start | bytes 196608 | tf_op jit(solution)/shard_map/reduce_scatter | solution.py:409
  863.4 419.0 %reduce-scatter.46.cloned.1.call-start = ((), (), s32[]{:S(2)}) async-start(), calls=%async_computation.41 | async-start | bytes 278528
  880.3 460.4 %reduce-scatter.48.cloned.1.call-start = ((), (), s32[]{:S(2)}) async-start(), calls=%async_computation.42 | async-start | bytes 278528
  881.3 517.1 %reduce-scatter.50.cloned.1.call-start = ((), (), s32[]{:S(2)}) async-start(), calls=%async_computation.43 | async-start | bytes 278528
  882.3 527.5 %reduce-scatter.28.cloned.1.call-start = ((), (), s32[]{:S(2)}) async-start(), calls=%async_computation.32 | async-start | bytes 196608 | tf_op jit(solution)/shard_map/reduce_scatter | solution.py:403
  882.9 543.6 %reduce-scatter.44.cloned.1.call-start = ((), (), s32[]{:S(2)}) async-start(), calls=%async_computation.40 | async-start | bytes 786432 | tf_op jit(solution)/shard_map/reduce_scatter | solution.py:415
  925.1 518.3 %reduce-scatter.40.cloned.1.call-start = ((), (), s32[]{:S(2)}) async-start(), calls=%async_computation.38 | async-start | bytes 786432 | tf_op jit(solution)/shard_map/reduce_scatter | solution.py:412
  1033.4 425.3 %reduce-scatter.32.cloned.1.call-start = ((), (), s32[]{:S(2)}) async-start(), calls=%async_computation.34 | async-start | bytes 589824 | tf_op jit(solution)/shard_map/reduce_scatter | solution.py:406
  1122.8 351.4 %reduce-scatter.24.cloned.1.call-start = ((), (), s32[]{:S(2)}) async-start(), calls=%async_computation.30 | async-start | bytes 589824 | tf_op jit(solution)/shard_map/reduce_scatter | solution.py:400
  (156 other events, 3730.1 us)
Sparse Core Ops, SparseCore 0:
  18.0 62.2 all-gather.10
  82.5 39.9 all-gather.12
  124.8 60.6 all-gather.14
  187.5 49.3 all-gather.16
  238.9 112.6 all-gather.18
  353.6 86.6 all-gather.20
  689.1 63.3 reduce-scatter.33
  756.6 60.5 reduce-scatter.25
  821.3 103.7 reduce-scatter.41
  929.0 104.3 reduce-scatter.37
  1037.3 85.3 reduce-scatter.29
  1127.1 84.3 reduce-scatter.21
  1213.7 9.4 reduce-scatter.35
  1227.1 55.3 reduce-scatter.45
  1286.4 54.3 reduce-scatter.47
  1344.1 54.2 reduce-scatter.49
  1400.5 9.2 reduce-scatter.27
  1411.9 14.5 reduce-scatter.43
  1428.8 14.5 reduce-scatter.39
  1445.5 13.1 reduce-scatter.31
  1461.0 13.1 reduce-scatter.23
where the time goes:
time: 1490 us; the launch traced here: 1480 us
  waiting for transfers between devices  648 us (43%)
  matrix products  301 us (20%)
  blocking collectives  203 us (14%)
  local copies, waits for them, and re-layouts  156 us (10%)
  starting transfers between devices  79.2 us (5%)
  other arithmetic  76.4 us (5%)
  between operations  19.9 us (1%)
    unnamed x24, waiting for transfers between devices  172 us
    reduce_scatter x1, waiting for transfers between devices, body(): lax.psum_scatter(totals[4].astype(jnp.bfloat16), 'seq', scatter_dimension...  108 us
    dot_general x12, matrix products, weight_grad(): lax.dot_general(flat_rows, flat_up, (((0,), (0,)), ((), ())), preferred_e...  83.9 us
    reduce_scatter x1, waiting for transfers between devices, body(): lax.psum_scatter(totals[0].astype(jnp.bfloat16), 'seq', scatter_dimension...  80.3 us
    unnamed x1, blocking collectives  62.1 us
    unnamed x322, local copies, waits for them, and re-layouts  59.8 us
    dot_general x12, matrix products, dot_back(): lax.dot_general(upstream, weight, (((upstream.ndim - 1,), (1,)), ((), ())...  56 us
    all_gather x1, waiting for transfers between devices, collect(): lax.all_gather(wide[2], 'seq', axis=0, tiled=True)  55.8 us
  transfers between devices with their start and end apart: 29, of which 19 were waited for; matrix products, arithmetic and copies ran while one was open for 26% of the time, Pallas kernels for 0%

commit v1 on v0

v1 whole, which is shorter than its diff:
```python
import functools
import jax
import jax.numpy as jnp
from jax import lax
from jax.experimental import pallas as pl
from jax.experimental.pallas import tpu as pltpu
from jax.sharding import PartitionSpec as P

MESH = pl.DeviceIdType.MESH


class Place:
    def __init__(self, seq_count, dp_count):
        self.size = {"z": 4, "x": seq_count // 8, "y": dp_count}
        seq = lax.axis_index("seq")
        self.core = lax.rem(seq, 2)
        self.at = {
            "z": seq // (2 * self.size["x"]),
            "x": lax.rem(seq // 2, self.size["x"]),
            "y": lax.axis_index("dp"),
        }

    def device(self, core=None, **moved):
        at = dict(self.at, **moved)
        core = self.core if core is None else core
        return (at["y"], (at["z"] * self.size["x"] + at["x"]) * 2 + core)

    def sibling(self):
        return self.device(core=1 - self.core)


def when(condition, action):
    if condition is True:
        action()
    elif condition is not False:
        pl.when(condition)(action)


def entry_barrier(place):
    barrier = pltpu.get_barrier_semaphore()

    def greet(device):
        pl.semaphore_signal(barrier, inc=1, device_id=device, device_id_type=MESH)

    count = 1
    greet(place.sibling())
    for axis in ("x", "y", "z"):
        here, size = place.at[axis], place.size[axis]
        if size == 2:
            greet(place.device(**{axis: 1 - here}))
            count = count + 1
            continue
        pl.when(here > 0)(lambda axis=axis, here=here: greet(place.device(**{axis: here - 1})))
        pl.when(here < size - 1)(lambda axis=axis, here=here: greet(place.device(**{axis: here + 1})))
        count = count + (here > 0).astype(jnp.int32) + (here < size - 1).astype(jnp.int32)
    pl.semaphore_wait(barrier, count)


def line_steps(here, size, distance):
    if size == 2:
        return [(1 - here, True, False, 0)]
    return [
        (here - distance, here - distance >= 0, here < size - 1, 1),
        (here + distance, here + distance < size, here > 0, -1),
    ]


class Gather:
    def __init__(self, place, order, shard, whole, rows, sems):
        self.place, self.order = place, order
        self.shard, self.whole, self.rows = shard, whole, rows
        self.n = [place.size[axis] for axis in order]
        self.me = [place.at[axis] for axis in order]
        self.recv, self.send, self.sib_send, self.sib_recv, self.own_sem = sems
        self.sent = []
        n1, n2, n3 = self.n
        self.ticks = n1 - 1 + n2 + max(n3 - 1, 1)

    @staticmethod
    def sem_shapes(n):
        n1, n2, n3 = n
        count = n1 + n2 + n2 * n3
        return (
            pltpu.SemaphoreType.DMA((count,)),
            pltpu.SemaphoreType.DMA((2, count)),
            pltpu.SemaphoreType.DMA((n2, n3)),
            pltpu.SemaphoreType.DMA((n2, n3)),
            pltpu.SemaphoreType.DMA((1,)),
        )

    def block(self, first, second, third, core=None):
        at = dict(zip(self.order, (first, second, third)))
        core = self.place.core if core is None else core
        return self.whole.at[at["y"], at["z"], at["x"], core, self.rows]

    def own(self):
        return pltpu.make_async_copy(
            self.shard.at[self.rows], self.block(*self.me), self.own_sem.at[0]
        )

    def pass_on(self, stage, slot, src, dst, direction, condition):
        axis, here = self.order[stage], self.me[stage]
        target = self.place.device(**{axis: here + direction})
        sem = self.send.at[(direction + 1) // 2, slot]

        def copy():
            return pltpu.make_async_remote_copy(
                src_ref=src, dst_ref=dst, send_sem=sem, recv_sem=self.recv.at[slot],
                device_id=target, device_id_type=MESH,
            )

        when(condition, lambda: copy().start())
        self.sent.append((condition, copy))

    def spread(self, stage, slot, src, dst):
        here, size = self.me[stage], self.n[stage]
        if size == 2:
            axis = self.order[stage]
            target = self.place.device(**{axis: 1 - here})

            def copy():
                return pltpu.make_async_remote_copy(
                    src_ref=src, dst_ref=dst, send_sem=self.send.at[0, slot],
                    recv_sem=self.recv.at[slot], device_id=target, device_id_type=MESH,
                )

            copy().start()
            self.sent.append((True, copy))
            return
        self.pass_on(stage, slot, src, dst, 1, here < size - 1)
        self.pass_on(stage, slot, src, dst, -1, here > 0)

    def arrive(self, slot, ref):
        pltpu.make_async_copy(ref, ref, self.recv.at[slot]).wait()

    def to_sibling(self, second, third):
        ref = self.block(slice(None), second, third)

        def copy():
            return pltpu.make_async_remote_copy(
                src_ref=ref, dst_ref=ref, send_sem=self.sib_send.at[second, third],
                recv_sem=self.sib_recv.at[second, third],
                device_id=self.place.sibling(), device_id_type=MESH,
            )

        return copy

    def hand(self, second, third, condition=True):
        copy = self.to_sibling(second, third)
        when(condition, lambda: copy().start())

    def tick(self, now):
        n1, n2, n3 = self.n
        me1, me2, me3 = self.me
        if now == 0:
            self.own().start()
            src = self.shard.at[self.rows]
            self.spread(0, me1, src, self.block(*self.me))
        if 1 <= now <= n1 - 1:
            for index, here, go, way in line_steps(me1, n1, now):
                self.step_one(index, here, go, way)
        base = n1 - 1
        if now == base:
            self.own().wait()
            self.group_ready(me2)
            ref = self.block(slice(None), me2, me3)
            self.spread(1, n1 + me2, ref, ref)
        for distance in range(1, n2):
            if now == base + distance:
                for index, here, go, way in line_steps(me2, n2, distance):
                    self.step_two(index, here, go, way)
        for far in range(1, n3):
            for distance in range(0, n2):
                if now == base + distance + far:
                    choices = [(me2, True)] if distance == 0 else [
                        (index, here) for index, here, _, _ in line_steps(me2, n2, distance)
                    ]
                    for second, there in choices:
                        for index, here, go, way in line_steps(me3, n3, far):
                            self.step_three(second, there, index, here, go, way)

    def step_one(self, index, here, go, way):
        ref = self.block(index, *self.me[1:])
        both = here if go is True or go is False else jnp.logical_and(here, go)

        when(here, lambda: self.arrive(index, ref))
        if go is not False:
            self.pass_on(0, index, ref, ref, way, both)

    def group_ready(self, second, condition=True):
        self.hand(second, self.me[2], condition)
        ref = self.block(slice(None), second, self.me[2])
        slot = self.n[0] + self.n[1] + second * self.n[2] + self.me[2]
        if condition is True:
            self.spread(2, slot, ref, ref)
            return
        here, size = self.me[2], self.n[2]
        if size == 2:
            axis = self.order[2]
            target = self.place.device(**{axis: 1 - here})

            def copy():
                return pltpu.make_async_remote_copy(
                    src_ref=ref, dst_ref=ref, send_sem=self.send.at[0, slot],
                    recv_sem=self.recv.at[slot], device_id=target, device_id_type=MESH,
                )

            when(condition, lambda: copy().start())
            self.sent.append((condition, copy))
            return
        self.pass_on(2, slot, ref, ref, 1, jnp.logical_and(condition, here < size - 1))
        self.pass_on(2, slot, ref, ref, -1, jnp.logical_and(condition, here > 0))

    def step_two(self, index, here, go, way):
        slot = self.n[0] + index
        ref = self.block(slice(None), index, self.me[2])
        when(here, lambda: self.arrive(slot, ref))
        if go is not False:
            both = here if go is True else jnp.logical_and(here, go)
            self.pass_on(1, slot, ref, ref, way, both)
        self.group_ready(index, here)

    def step_three(self, second, there, index, here, go, way):
        slot = self.n[0] + self.n[1] + second * self.n[2] + index
        ref = self.block(slice(None), second, index)
        here = here if there is True else (there if here is True else jnp.logical_and(here, there))
        when(here, lambda: self.arrive(slot, ref))
        if go is not False:
            both = here if go is True else (go if here is True else jnp.logical_and(here, go))
            self.pass_on(2, slot, ref, ref, way, both)
        self.hand(second, index, here)

    def finish_recv(self):
        other = 1 - self.place.core
        for second in range(self.n[1]):
            for third in range(self.n[2]):
                ref = self.block(slice(None), second, third, core=other)
                pltpu.make_async_copy(ref, ref, self.sib_recv.at[second, third]).wait()

    def finish_send(self):
        for condition, copy in self.sent:
            when(condition, lambda copy=copy: copy().wait_send())
        for second in range(self.n[1]):
            for third in range(self.n[2]):
                self.to_sibling(second, third)().wait_send()


ORDERS = (("x", "z", "y"), ("y", "z", "x"))
ORDERS_LOW = (("z", "x", "y"), ("z", "y", "x"))


def piece_plan(weights):
    plan = []
    for index in range(weights):
        orders = ORDERS if index % 2 == 0 else ORDERS_LOW
        for half in range(2):
            plan.append((index, half, orders[half]))
    return plan


def gather_kernel(seq_count, dp_count, plan, skew, count, *refs):
    shards, wholes, sems = refs[:count], refs[count : 2 * count], refs[2 * count :]
    place = Place(seq_count, dp_count)
    entry_barrier(place)
    pieces = []
    for number, (index, half, order) in enumerate(plan):
        rows = shards[index].shape[0] // 2
        pieces.append(
            Gather(place, order, shards[index], wholes[index], pl.ds(half * rows, rows),
                   sems[5 * number : 5 * number + 5])
        )
    last = max(p.ticks + i * skew for i, p in enumerate(pieces))
    for now in range(last + 1):
        for i, piece in enumerate(pieces):
            if 0 <= now - i * skew <= piece.ticks:
                piece.tick(now - i * skew)
    for piece in pieces:
        piece.finish_recv()
        piece.finish_send()


def gather_all(shards, seq_count, dp_count, skew=1, collective_id=0):
    plan = piece_plan(len(shards))
    size = {"z": 4, "x": seq_count // 8, "y": dp_count}
    scratch = []
    for index, half, order in plan:
        scratch += list(Gather.sem_shapes([size[a] for a in order]))
    out_shape = [
        jax.ShapeDtypeStruct((dp_count, 4, size["x"], 2) + s.shape, s.dtype) for s in shards
    ]
    return pl.pallas_call(
        functools.partial(gather_kernel, seq_count, dp_count, plan, skew, len(shards)),
        out_shape=out_shape,
        in_specs=[pl.BlockSpec(memory_space=pltpu.HBM)] * len(shards),
        out_specs=[pl.BlockSpec(memory_space=pltpu.HBM)] * len(shards),
        scratch_shapes=scratch,
        compiler_params=pltpu.CompilerParams(collective_id=collective_id, has_side_effects=True),
        name="gather_weights",
    )(*shards)

D_EPS = 1e-05
NEG = -1e30
HEADS = 16
HDIM = 64
SCALE = HDIM ** (-0.5)
NT = (((1,), (1,)), ((), ()))
TN = (((0,), (0,)), ((), ()))
ROWS = 32
VMEM_LIMIT = 60 * 1024 * 1024


def dot(left, right, dims=(((1,), (0,)), ((), ()))):
    return lax.dot_general(left, right, dims, preferred_element_type=jnp.float32)


def tile_of(size, largest=512):
    return max(t for t in (128, 256, 384, 512, 1024) if t <= largest and size % t == 0)


def loop(count, action):
    def step(index, carry):
        action(index)
        return carry

    lax.fori_loop(0, count, step, 0)


def at_rows(index, size):
    return pl.ds(pl.multiple_of(index * size, size), size)


def moments(value):
    width = value.shape[-1]
    centre = jnp.sum(value, axis=-1, keepdims=True) * (1.0 / width)
    offset = value - centre
    spread = jnp.sum(offset * offset, axis=-1, keepdims=True) * (1.0 / width)
    return offset, lax.rsqrt(spread + D_EPS)


def norm_forward(read, gain, shift, out):
    def step(index):
        rows = at_rows(index, ROWS)
        offset, rate = moments(read(rows))
        out[rows, :] = (offset * rate * gain[...] + shift[...]).astype(jnp.bfloat16)

    loop(out.shape[0] // ROWS, step)


def fold8(value):
    return jnp.sum(value.reshape(-1, 8, value.shape[-1]), axis=0)


def norm_backward(read, gain, grad, upstream, write, gain_out, shift_out):
    tokens, width = grad.shape

    def step(index, carry):
        gain_sum, shift_sum = carry
        rows = at_rows(index, ROWS)
        offset, rate = moments(read(rows))
        unit = offset * rate
        dy = grad[rows, :]
        gain_sum = gain_sum + fold8(dy * unit)
        shift_sum = shift_sum + fold8(dy)
        scaled = dy * gain[...]
        mean = jnp.sum(scaled, axis=-1, keepdims=True) * (1.0 / width)
        slope = jnp.sum(scaled * unit, axis=-1, keepdims=True) * (1.0 / width)
        write(index, rows, upstream(rows) + rate * (scaled - mean - unit * slope))
        return gain_sum, shift_sum

    zero = jnp.zeros((8, width), jnp.float32)
    gain_sum, shift_sum = lax.fori_loop(0, tokens // ROWS, step, (zero, zero))
    gain_out[...] = jnp.sum(gain_sum, axis=0, keepdims=True)
    shift_out[...] = jnp.sum(shift_sum, axis=0, keepdims=True)


def project(rows, weight, emit, tile_max=512):
    parts, _, size = weight.shape
    tile = tile_of(size, tile_max)
    for part in range(parts):

        def step(index, part=part):
            inner = at_rows(index, tile)
            columns = pl.ds(pl.multiple_of(part * size + index * tile, 128), tile)
            emit(columns, dot(rows[...], weight[part, :, inner]))

        loop(size // tile, step)


def project_back(grad, weight, emit, tile_max=512):
    parts, depth, size = weight.shape
    tile = tile_of(depth, tile_max)

    def step(index):
        inner = at_rows(index, tile)
        total = None
        for part in range(parts):
            term = dot(grad[:, part * size : (part + 1) * size], weight[part, inner, :], NT)
            total = term if total is None else total + term
        emit(inner, total)

    loop(depth // tile, step)


def outer(rows, grad, out, tile_max=512):
    parts, depth, size = out.shape
    tile = tile_of(depth, tile_max)

    def step(index):
        inner = at_rows(index, tile)
        left = rows[:, inner]
        for part in range(parts):
            out[part, inner, :] = dot(
                left, grad[:, part * size : (part + 1) * size], TN
            ).astype(out.dtype)

    loop(depth // tile, step)


def head_mask(shape, axis, head):
    lane = lax.broadcasted_iota(jnp.int32, shape, axis)
    return (lane // HDIM) == head


def pick(value, head):
    return jnp.where(head_mask(value.shape, 1, head), value, jnp.zeros_like(value))


def pick_rows(value, head):
    return jnp.where(head_mask(value.shape, 0, head), value, jnp.zeros_like(value))


def pair_slices(index, width, tokens):
    pairs = width // 128
    micro, pair = index // pairs, lax.rem(index, pairs)
    rows = pl.ds(pl.multiple_of(micro * tokens, tokens), tokens)
    return micro, rows, [
        pl.ds(pl.multiple_of(part * width + pair * 128, 128), 128) for part in range(3)
    ]


def attention_forward(packed, allowed, probs, mixed, tokens):
    width = mixed.shape[1]

    def step(index):
        micro, rows, (q_at, k_at, v_at) = pair_slices(index, width, tokens)
        queries = packed[rows, q_at] * jnp.bfloat16(SCALE)
        keys, values = packed[rows, k_at], packed[rows, v_at]
        values_t = values.astype(jnp.float32).T.astype(jnp.bfloat16)
        total = None
        for head in range(2):
            scores = dot(keys, pick(queries, head), NT)
            if allowed is not None:
                scores = jnp.where(allowed[micro] > 0, scores, NEG)
            raised = jnp.exp(scores - jnp.max(scores, axis=0, keepdims=True))
            prob = raised * (1.0 / jnp.sum(raised, axis=0, keepdims=True))
            prob = prob.astype(jnp.bfloat16)
            probs[2 * index + head] = prob
            term = dot(pick_rows(values_t, head), prob)
            total = term if total is None else total + term
        mixed[rows, q_at] = total.T.astype(jnp.bfloat16)

    loop(mixed.shape[0] // tokens * (width // 128), step)


def attention_backward(packed, probs, grad, packed_grad, tokens):
    width = grad.shape[1]

    def step(index):
        _, rows, (q_at, k_at, v_at) = pair_slices(index, width, tokens)
        queries, keys, values = packed[rows, q_at], packed[rows, k_at], packed[rows, v_at]
        upstream = grad[rows, q_at]
        keys_t = keys.astype(jnp.float32).T.astype(jnp.bfloat16)
        query_grad = key_grad = value_grad = None
        for head in range(2):
            low = probs[2 * index + head]
            prob = low.astype(jnp.float32)
            up = pick(upstream, head)
            prob_grad = dot(values, up, NT)
            inner = jnp.sum(prob * prob_grad, axis=0, keepdims=True)
            score_grad = (prob * (prob_grad - inner) * SCALE).astype(jnp.bfloat16)
            terms = (
                dot(pick_rows(keys_t, head), score_grad),
                dot(score_grad, pick(queries, head)),
                dot(low, up),
            )
            if head == 0:
                query_grad, key_grad, value_grad = terms
            else:
                query_grad = query_grad + terms[0]
                key_grad = key_grad + terms[1]
                value_grad = value_grad + terms[2]
        packed_grad[rows, q_at] = query_grad.T.astype(jnp.bfloat16)
        packed_grad[rows, k_at] = key_grad.astype(jnp.bfloat16)
        packed_grad[rows, v_at] = value_grad.astype(jnp.bfloat16)

    loop(grad.shape[0] // tokens * (width // 128), step)


class Fetch:
    def __init__(self, src, dst, sem):
        self.copy = pltpu.make_async_copy(src, dst, sem)

    def start(self):
        self.copy.start()
        return self

    def wait(self):
        self.copy.wait()


def spatial_reader(frames, row_pair, tokens):
    def read(rows):
        micro = rows.start // tokens
        return frames[rows, :].astype(jnp.float32) + row_pair[pl.ds(micro, 1), :]

    return read


def attend_forward_kernel(spatial, tokens, *refs):
    if spatial:
        stream, row_pair, gain, shift, w_in, w_out, out, packed, probs, mixed, *rest = refs
        allowed = None
        read = spatial_reader(stream, row_pair, tokens)
    else:
        stream, allowed, gain, shift, w_in, w_out, out, packed, probs, mixed, *rest = refs
        read = lambda rows: stream[rows, :].astype(jnp.float32)
    normed, v_in, v_out, sems = rest
    first = Fetch(w_in, v_in, sems.at[0]).start()
    second = Fetch(w_out, v_out, sems.at[1]).start()
    norm_forward(read, gain, shift, normed)
    first.wait()

    def emit(columns, value):
        packed[:, columns] = value.astype(jnp.bfloat16)

    project(normed, v_in, emit)
    attention_forward(packed, allowed, probs, mixed, tokens)
    second.wait()

    def emit_out(columns, value):
        if spatial:
            for micro in range(stream.shape[0] // tokens):
                rows = slice(micro * tokens, (micro + 1) * tokens)
                base = stream[rows, columns].astype(jnp.float32) + row_pair[micro : micro + 1, columns]
                out[rows, columns] = (base + value[rows]).astype(out.dtype)
        else:
            out[:, columns] = (stream[:, columns].astype(jnp.float32) + value).astype(out.dtype)

    project(mixed, v_out, emit_out)


def vmem(count):
    return [pl.BlockSpec(memory_space=pltpu.VMEM)] * count


def hbm(count):
    return [pl.BlockSpec(memory_space=pltpu.HBM)] * count


def attend_forward(spatial, tokens, stream, extra, gain, shift, w_in, w_out):
    total, width = stream.shape
    heads = total // tokens * HEADS
    low = jnp.bfloat16
    return pl.pallas_call(
        functools.partial(attend_forward_kernel, spatial, tokens),
        out_shape=(
            jax.ShapeDtypeStruct((total, width), low if spatial else jnp.float32),
            jax.ShapeDtypeStruct((total, 3 * width), low),
            jax.ShapeDtypeStruct((heads, tokens, tokens), low),
            jax.ShapeDtypeStruct((total, width), low),
        ),
        in_specs=vmem(4) + hbm(2),
        out_specs=vmem(4),
        scratch_shapes=[
            pltpu.VMEM((total, width), low),
            pltpu.VMEM(w_in.shape, low),
            pltpu.VMEM(w_out.shape, low),
            pltpu.SemaphoreType.DMA((2,)),
        ],
        compiler_params=pltpu.CompilerParams(vmem_limit_bytes=VMEM_LIMIT),
        name="space_forward" if spatial else "time_forward",
    )(stream, extra, gain, shift, w_in, w_out)


def attend_backward_kernel(spatial, tokens, *refs):
    if spatial:
        (up, stream, row_pair, gain, shift, packed_h, probs_h, mixed, w_in_h, w_out_h,
         down, w_in_grad, w_out_grad, gain_out, shift_out, sums, *rest) = refs
        read = spatial_reader(stream, row_pair, tokens)
    else:
        (up, stream, gain, shift, packed_h, probs_h, mixed, w_in_h, w_out_h,
         down, w_in_grad, w_out_grad, gain_out, shift_out, *rest) = refs
        read = lambda rows: stream[rows, :].astype(jnp.float32)
    normed, up_low, mixed_grad, packed_grad, normed_grad, packed, probs, w_in, w_out, sems = rest
    fetches = [
        Fetch(src, dst, sems.at[i]).start()
        for i, (src, dst) in enumerate(
            ((w_out_h, w_out), (packed_h, packed), (probs_h, probs), (w_in_h, w_in))
        )
    ]

    def lower(index):
        rows = at_rows(index, ROWS)
        up_low[rows, :] = up[rows, :].astype(jnp.bfloat16)

    loop(up.shape[0] // ROWS, lower)
    norm_forward(read, gain, shift, normed)
    fetches[0].wait()

    def emit_mixed(columns, value):
        mixed_grad[:, columns] = value.astype(jnp.bfloat16)

    project_back(up_low, w_out, emit_mixed)
    outer(mixed, up_low, w_out_grad)
    fetches[1].wait()
    fetches[2].wait()
    attention_backward(packed, probs, mixed_grad, packed_grad, tokens)
    fetches[3].wait()
    outer(normed, packed_grad, w_in_grad)

    def emit_normed(columns, value):
        normed_grad[:, columns] = value

    project_back(packed_grad, w_in, emit_normed)
    if spatial:
        sums[...] = jnp.zeros_like(sums)

        def write(index, rows, value):
            down[rows, :] = value.astype(down.dtype)
            micro = rows.start // tokens
            sums[pl.ds(micro, 1), :] += jnp.sum(fold8(value), axis=0, keepdims=True)
    else:

        def write(index, rows, value):
            down[rows, :] = value.astype(down.dtype)

    norm_backward(
        read, gain, normed_grad, lambda rows: up[rows, :].astype(jnp.float32), write, gain_out, shift_out
    )


def attend_backward(spatial, tokens, up, stream, extra, gain, shift, packed, probs, mixed, w_in, w_out):
    total, width = stream.shape
    low, full = jnp.bfloat16, jnp.float32
    shape = jax.ShapeDtypeStruct
    outs = [
        shape((total, width), low),
        shape(w_in.shape, low),
        shape(w_out.shape, low),
        shape((1, width), full),
        shape((1, width), full),
    ]
    if spatial:
        outs.append(shape((total // tokens, width), full))
    front = (up, stream) + ((extra,) if spatial else ()) + (gain, shift)
    return pl.pallas_call(
        functools.partial(attend_backward_kernel, spatial, tokens),
        out_shape=tuple(outs),
        in_specs=vmem(len(front)) + hbm(2) + vmem(1) + hbm(2),
        out_specs=vmem(len(outs)),
        scratch_shapes=[
            pltpu.VMEM((total, width), low),
            pltpu.VMEM((total, width), low),
            pltpu.VMEM((total, width), low),
            pltpu.VMEM((total, 3 * width), low),
            pltpu.VMEM((total, width), full),
            pltpu.VMEM(packed.shape, low),
            pltpu.VMEM(probs.shape, low),
            pltpu.VMEM(w_in.shape, low),
            pltpu.VMEM(w_out.shape, low),
            pltpu.SemaphoreType.DMA((4,)),
        ],
        compiler_params=pltpu.CompilerParams(vmem_limit_bytes=VMEM_LIMIT),
        name="space_backward" if spatial else "time_backward",
    )(*front, packed, probs, mixed, w_in, w_out)


GELU_A = 0.7978845608028654
GELU_B = 0.044715


def gelu_pair(value):
    square = value * value
    bent = jnp.tanh(GELU_A * value * (1.0 + GELU_B * square))
    half = 0.5 * (1.0 + bent)
    slope = half + 0.5 * value * (1.0 - bent * bent) * (GELU_A * (1.0 + 3.0 * GELU_B * square))
    return value * half, slope


def hidden_kernel(stream, cotangent, live, gain, shift, up_bias, down_bias, w_up_h, w_down_h,
                  out, down, up_grad_h, down_grad_h, gain_out, shift_out, up_bias_out, down_bias_out,
                  normed, end_low, active, slope, expand_low, normed_grad, w_up, w_down, up_stage, down_stage, sems):
    low = jnp.bfloat16
    first = Fetch(w_up_h, w_up, sems.at[0]).start()
    second = Fetch(w_down_h, w_down, sems.at[1]).start()
    tokens, width = stream.shape
    parts = w_up.shape[0]
    norm_forward(lambda rows: stream[rows, :], gain, shift, normed)

    def lower(index, total):
        rows = at_rows(index, ROWS)
        value = cotangent[rows, :].astype(jnp.float32) * live[rows, :]
        end_low[rows, :] = value.astype(low)
        return total + fold8(value)

    total = lax.fori_loop(0, tokens // ROWS, lower, jnp.zeros((8, width), jnp.float32))
    down_bias_out[...] = jnp.sum(total, axis=0, keepdims=True)
    first.wait()

    def emit_expand(columns, value):
        act, rate = gelu_pair(value + up_bias[:, columns])
        active[:, columns] = act.astype(low)
        slope[:, columns] = rate.astype(low)

    project(normed, w_up, emit_expand, 256)
    second.wait()

    def emit_out(columns, value):
        end = stream[:, columns] + value + down_bias[:, columns]
        out[:, columns] = (end * live[...]).astype(out.dtype)

    project(active, w_down, emit_out, 256)

    def emit_active(columns, value):
        grad = value * slope[:, columns].astype(jnp.float32)
        up_bias_out[:, columns] = jnp.sum(grad, axis=0, keepdims=True)
        expand_low[:, columns] = grad.astype(low)

    project_back(end_low, w_down, emit_active, 256)

    hidden, size = w_down.shape[1], w_down.shape[2]
    tile = down_stage.shape[2]

    def send_down(index, slot):
        return pltpu.make_async_copy(
            down_stage.at[slot], down_grad_h.at[:, at_rows(index, tile), :], sems.at[2 + slot]
        )

    def step_down(index):
        slot = lax.rem(index, 2)
        pl.when(index >= 2)(lambda: send_down(index - 2, slot).wait())
        left = active[:, at_rows(index, tile)]
        for part in range(parts):
            down_stage[slot, part] = dot(
                left, end_low[:, part * size : (part + 1) * size], TN
            ).astype(low)
        send_down(index, slot).start()

    count = hidden // tile
    loop(count, step_down)
    send_down(count - 2, (count - 2) % 2).wait()
    send_down(count - 1, (count - 1) % 2).wait()

    size_up = w_up.shape[2]
    tile_up = up_stage.shape[2]

    def send_up(index, slot):
        return pltpu.make_async_copy(
            up_stage.at[slot], up_grad_h.at[:, at_rows(index, tile_up), :], sems.at[4 + slot]
        )

    def step_up(index):
        slot = lax.rem(index, 2)
        pl.when(index >= 2)(lambda: send_up(index - 2, slot).wait())
        left = normed[:, at_rows(index, tile_up)]
        for part in range(parts):
            up_stage[slot, part] = dot(
                left, expand_low[:, part * size_up : (part + 1) * size_up], TN
            ).astype(low)
        send_up(index, slot).start()

    count_up = width // tile_up
    loop(count_up, step_up)

    def emit_normed(columns, value):
        normed_grad[:, columns] = value

    project_back(expand_low, w_up, emit_normed, 256)
    send_up(count_up - 2, (count_up - 2) % 2).wait()
    send_up(count_up - 1, (count_up - 1) % 2).wait()

    def write(index, rows, value):
        down[rows, :] = value

    def upstream(rows):
        return cotangent[rows, :].astype(jnp.float32) * live[rows, :]

    norm_backward(lambda rows: stream[rows, :], gain, normed_grad, upstream, write, gain_out, shift_out)


def hidden_layer(stream, cotangent, live, gain, shift, up_bias, down_bias, w_up, w_down):
    tokens, width = stream.shape
    hidden = up_bias.shape[1]
    parts = w_up.shape[0]
    low, full = jnp.bfloat16, jnp.float32
    shape = jax.ShapeDtypeStruct
    return pl.pallas_call(
        hidden_kernel,
        out_shape=(
            shape((tokens, width), low),
            shape((tokens, width), full),
            shape(w_up.shape, low),
            shape(w_down.shape, low),
            shape((1, width), full),
            shape((1, width), full),
            shape((1, hidden), full),
            shape((1, width), full),
        ),
        in_specs=vmem(7) + hbm(2),
        out_specs=vmem(2) + hbm(2) + vmem(4),
        scratch_shapes=[
            pltpu.VMEM((tokens, width), low),
            pltpu.VMEM((tokens, width), low),
            pltpu.VMEM((tokens, hidden), low),
            pltpu.VMEM((tokens, hidden), low),
            pltpu.VMEM((tokens, hidden), low),
            pltpu.VMEM((tokens, width), full),
            pltpu.VMEM(w_up.shape, low),
            pltpu.VMEM(w_down.shape, low),
            pltpu.VMEM((2, parts, 256, w_up.shape[2]), low),
            pltpu.VMEM((2, parts, 256, w_down.shape[2]), low),
            pltpu.SemaphoreType.DMA((6,)),
        ],
        compiler_params=pltpu.CompilerParams(vmem_limit_bytes=VMEM_LIMIT),
        name="hidden_layer",
    )(stream, cotangent, live, gain, shift, up_bias, down_bias, w_up, w_down)

class Reduce:
    def __init__(self, place, order, partial_sum, rows, out, bufs, sems):
        self.place, self.order, self.rows = place, order, rows
        self.partial, self.out = partial_sum, out
        self.kept, self.from_core, self.from_third, self.from_second, self.from_first = bufs
        self.core_sems, self.third_sems, self.second_sems, self.first_sems = sems
        self.n = [place.size[axis] for axis in order]
        self.me = [place.at[axis] for axis in order]
        self.sent = []
        n1, n2, n3 = self.n
        self.pair = n3 == 2
        self.third_ticks = 0 if self.pair else n3
        self.ticks = 1 + self.third_ticks + n2 + (1 if n1 == 2 else n1)

    @staticmethod
    def scratch(n, sizes, rows, columns, dtype):
        n1, n2, n3 = n
        slots = lambda count: 1 if count == 2 else count + 1
        return (
            [
                pltpu.VMEM(sizes + (rows, columns), dtype),
                pltpu.VMEM(sizes + (rows, columns), dtype),
                pltpu.VMEM((slots(n3), n2, n1, rows, columns), dtype),
                pltpu.VMEM((slots(n2), n1, rows, columns), dtype),
                pltpu.VMEM((slots(n1), rows, columns), dtype),
            ],
            [
                pltpu.SemaphoreType.DMA((3,)),
                pltpu.SemaphoreType.DMA((2, n3 + 1, n2)),
                pltpu.SemaphoreType.DMA((2, n2 + 1)),
                pltpu.SemaphoreType.DMA((2, n1 + 1)),
            ],
        )

    def block(self, first, second, third):
        at = dict(zip(self.order, (first, second, third)))
        return self.kept.at[at["y"], at["z"], at["x"]]

    def core_copy(self):
        return pltpu.make_async_remote_copy(
            src_ref=self.partial.at[:, :, :, 1 - self.place.core, self.rows],
            dst_ref=self.from_core,
            send_sem=self.core_sems.at[0], recv_sem=self.core_sems.at[1],
            device_id=self.place.sibling(), device_id_type=MESH,
        )

    def own_copy(self):
        return pltpu.make_async_copy(
            self.partial.at[:, :, :, self.place.core, self.rows], self.kept, self.core_sems.at[2]
        )

    def add_rows(self, dst, src, index):
        rows = dst.shape[-2]

        def step(i):
            at = index + (at_rows(i, 16),)
            dst[at] = dst[at] + src[at]

        loop(rows // 16, step)

    def send(self, stage, slot_sem, src, dst, moved, recv_sem, condition=True):
        axis = self.order[stage]

        def copy():
            return pltpu.make_async_remote_copy(
                src_ref=src, dst_ref=dst, send_sem=slot_sem, recv_sem=recv_sem,
                device_id=self.place.device(**{axis: moved}), device_id_type=MESH,
            )

        when(condition, lambda: copy().start())
        self.sent.append((condition, copy))

    def arrived(self, sem, ref):
        pltpu.make_async_copy(ref, ref, sem).wait()

    def second_order(self):
        order = []
        for step in range(1, self.n[1] + 1):
            for index in (self.n[1] - step, step - 1):
                if index not in order:
                    order.append(index)
        return order

    def tick(self, now):
        n1, n2, n3 = self.n
        if now == 0:
            self.core_copy().start()
            self.own_copy().start()
            return
        if now == 1:
            self.own_copy().wait()
            self.arrived(self.core_sems.at[1], self.from_core)
            sizes = self.kept.shape[:3]

            def add(index):
                y, rest = index // (sizes[1] * sizes[2]), lax.rem(index, sizes[1] * sizes[2])
                at = (y, rest // sizes[2], lax.rem(rest, sizes[2]))
                self.add_rows(self.kept, self.from_core, at)

            loop(sizes[0] * sizes[1] * sizes[2], add)
            if self.pair:
                other = 1 - self.me[2]
                for second in self.second_order():
                    self.send(
                        2, self.third_sems.at[0, 0, second], self.block(slice(None), second, other),
                        self.from_third.at[0, second], other, self.third_sems.at[1, 0, second],
                    )
        now = now - 1
        if not self.pair:
            if now < n3:
                self.line(2, now)
        now = now - self.third_ticks
        if 0 <= now < n2:
            self.line(1, now)
        now = now - n2
        if 0 <= now and now < (1 if n1 == 2 else n1):
            self.line(0, now)
        if now == (1 if n1 == 2 else n1):
            pass

    def stage_ref(self, stage, index):
        if stage == 2:
            return self.block(slice(None), slice(None), index)
        if stage == 1:
            return self.block(slice(None), index, self.me[2])
        return self.block(index, self.me[1], self.me[2])

    def buffers(self, stage):
        if stage == 2:
            return self.from_third, self.third_sems.at[0, :, 0], self.third_sems.at[1, :, 0]
        if stage == 1:
            return self.from_second, self.second_sems.at[0], self.second_sems.at[1]
        return self.from_first, self.first_sems.at[0], self.first_sems.at[1]

    def absorb(self, stage, index, buffer_slot):
        buffer, sems = (
            (self.from_third, lambda s: self.third_sems.at[1, s, 0]),
            (self.from_second, lambda s: self.second_sems.at[1, s]),
            (self.from_first, lambda s: self.first_sems.at[1, s]),
        )[2 - stage]
        self.arrived(sems(buffer_slot), buffer.at[buffer_slot])
        target = self.stage_ref(stage, index)
        source = buffer.at[buffer_slot]
        self.add_all(target, source)

    def add_all(self, target, source):
        lead = target.shape[:-2]
        count = 1
        for size in lead:
            count *= size

        def add(index):
            at, rest = (), index
            for size in reversed(lead):
                at = (lax.rem(rest, size),) + at
                rest = rest // size
            self.add_rows(target, source, at)

        if count == 1 and not lead:
            self.add_rows(target, source, ())
        else:
            loop(count, add)

    def third_ready(self, second):
        if not self.pair:
            return
        self.arrived(self.third_sems.at[1, 0, second], self.from_third.at[0, second])
        self.add_all(self.block(slice(None), second, self.me[2]), self.from_third.at[0, second])

    def line(self, stage, now):
        size, here = self.n[stage], self.me[stage]
        sems = (self.first_sems, self.second_sems, None)[stage]
        send_sem = lambda s: self.third_sems.at[0, s, 0] if stage == 2 else sems.at[0, s]
        recv_sem = lambda s: self.third_sems.at[1, s, 0] if stage == 2 else sems.at[1, s]
        buffer = (self.from_first, self.from_second, self.from_third)[stage]
        if size == 2:
            if stage == 1:
                if now == 0:
                    for second in range(2):
                        self.third_ready(second)
                    self.send(stage, send_sem(0), self.stage_ref(stage, 1 - here), buffer.at[0], 1 - here, recv_sem(0))
                if now == 1:
                    self.absorb(stage, here, 0)
                    self.start_first()
            if stage == 0:
                self.arrived(recv_sem(0), buffer.at[0])
                self.finish(buffer.at[0])
            return
        if now < size - 1:
            up = size - 1 - now + here
            goes_up = jnp.logical_and(here <= now, here < size - 1)

            def go_up():
                if stage == 1:
                    self.third_ready(up)
                pl.when(here > 0)(lambda: self.absorb(stage, up, up))

            up = jnp.minimum(up, size - 1)
            pl.when(goes_up)(go_up)
            self.send(stage, send_sem(up), self.stage_ref(stage, up), buffer.at[up], here + 1, recv_sem(up), goes_up)
            down = jnp.maximum(now + here - (size - 1), 0)
            goes_down = jnp.logical_and(size - 1 - here <= now, here > 0)

            def go_down():
                if stage == 1:
                    self.third_ready(down)
                pl.when(here < size - 1)(lambda: self.absorb(stage, down, down))

            pl.when(goes_down)(go_down)
            self.send(stage, send_sem(down), self.stage_ref(stage, down), buffer.at[self.down_slot(stage, down)],
                      here - 1, recv_sem(self.down_slot(stage, down)), goes_down)
            return
        if stage == 1:
            self.third_ready(here)
        pl.when(here > 0)(lambda: self.absorb(stage, here, here))
        pl.when(here < size - 1)(lambda: self.absorb(stage, here, size))
        if stage == 1:
            self.start_first()
        if stage == 0:
            self.finish(None)

    def down_slot(self, stage, target):
        here, size = self.me[stage], self.n[stage]
        return jnp.where(target == here - 1, size, target)

    def start_first(self):
        if self.n[0] == 2:
            other = 1 - self.me[0]
            self.send(0, self.first_sems.at[0, 0], self.stage_ref(0, other), self.from_first.at[0], other,
                      self.first_sems.at[1, 0])

    def finish(self, extra):
        own = self.stage_ref(0, self.me[0])

        def step(i):
            rows = at_rows(i, 16)
            value = own[rows, :].astype(jnp.float32)
            if extra is not None:
                value = value + extra[rows, :].astype(jnp.float32)
            self.out[pl.ds(pl.multiple_of(self.rows.start + i * 16, 16), 16), :] = value

        loop(own.shape[0] // 16, step)

    def finish_send(self):
        self.core_copy().wait_send()
        for condition, copy in self.sent:
            when(condition, lambda copy=copy: copy().wait_send())


def split_plan(heights, parts_of, orders_of):
    plan = []
    for index, height in enumerate(heights):
        parts = min(parts_of, height // 16)
        rows = height // parts
        for part in range(parts):
            plan.append((index, part * rows, rows, orders_of(index)[part]))
    return plan


def run_pieces(pieces, offsets, skew, work=()):
    events = []
    for i, piece in enumerate(pieces):
        for e in range(piece.ticks + 1):
            own = offsets[piece.order[2]] if isinstance(offsets, dict) else offsets
            when_at = own[e] if e < len(own) else own[-1] + e - len(own) + 1
            events.append((when_at + i * skew, i, e))
    events.sort()
    for _, i, e in events:
        pieces[i].tick(e)


def reduce_kernel(seq_count, dp_count, plan, offsets, skew, count, *refs):
    partials, outs, rest = refs[:count], refs[count : 2 * count], refs[2 * count :]
    place = Place(seq_count, dp_count)
    entry_barrier(place)
    pieces = []
    for number, (index, first, rows, order) in enumerate(plan):
        own = rest[9 * number : 9 * number + 9]
        pieces.append(Reduce(place, order, partials[index], pl.ds(first, rows), outs[index], own[:5], own[5:]))
    run_pieces(pieces, offsets, skew)
    for piece in pieces:
        piece.finish_send()


def weight_orders(index):
    if index in (0, 1, 4):
        return (("z", "x", "y"), ("z", "y", "x"), ("x", "y", "z"), ("x", "z", "y"))
    return (("z", "x", "y"), ("z", "y", "x"), ("y", "x", "z"), ("y", "z", "x"))


def reduce_all(partials, seq_count, dp_count, parts=2, offsets=(0, 1, 3, 4, 5, 6, 7), skew=1, collective_id=0, orders=weight_orders):
    size = {"z": 4, "x": seq_count // 8, "y": dp_count}
    sizes = (dp_count, 4, size["x"])
    scratch = []
    blocked, outs = [], []
    for p in partials:
        rows = p.shape[1] // seq_count
        blocked.append(p.reshape((dp_count, 4, size["x"], 2, rows, p.shape[2])))
        outs.append(jax.ShapeDtypeStruct((rows, p.shape[2]), jnp.float32))
    plan = split_plan([o.shape[0] for o in outs], parts, orders)
    for index, first, rows, order in plan:
        bufs, sems = Reduce.scratch(
            [size[a] for a in order], sizes, rows, outs[index].shape[1], partials[index].dtype
        )
        scratch += bufs + sems
    return pl.pallas_call(
        functools.partial(reduce_kernel, seq_count, dp_count, plan, offsets, skew, len(partials)),
        out_shape=outs,
        in_specs=hbm(len(partials)),
        out_specs=vmem(len(partials)),
        scratch_shapes=scratch,
        compiler_params=pltpu.CompilerParams(
            collective_id=collective_id, has_side_effects=True, vmem_limit_bytes=VMEM_LIMIT
        ),
        name="reduce_gradients",
    )(*blocked)

ACTIONS = 8
FRAMES = 16


def body(
    frames_in,
    cotangent,
    lengths,
    actions,
    spatial_in,
    spatial_out,
    temporal_in,
    temporal_out,
    hidden_in,
    hidden_out,
    norm_gains,
    norm_shifts,
    bias_up,
    bias_down,
    action_table,
):
    seq_count, dp_count = lax.axis_size("seq"), lax.axis_size("dp")
    micro, frame_count, spatial, width = frames_in.shape
    tokens = micro * frame_count * spatial
    frames = seq_count * frame_count
    places = spatial // seq_count
    group = frames * places
    cut = norm_gains.shape[1]
    low, full = jnp.bfloat16, jnp.float32

    up_rows = bias_up.shape[0] // cut
    small = jnp.concatenate(
        [norm_gains, norm_shifts, action_table, bias_down[None], bias_up.reshape(up_rows, cut)], axis=0
    )
    used = small.shape[0]
    small = jnp.pad(small, ((0, 32 - used), (0, 128 - cut)))
    shards = [spatial_in, spatial_out, temporal_in, temporal_out, hidden_in, hidden_out, small]
    wholes = gather_all(shards, seq_count, dp_count, skew=0, collective_id=1)
    weights = [
        whole.reshape(dp_count, shard.shape[0] * seq_count, shard.shape[1])
        for whole, shard in zip(wholes[:6], shards)
    ]
    w_sin, w_sout, w_tin, w_tout, w_hin, w_hout = weights
    small = wholes[6][0].reshape(seq_count, 32, 128)[:, :, :cut].astype(full)
    rows = small[:, : used - up_rows].transpose(1, 0, 2).reshape(used - up_rows, width)
    gain, shift = [rows[i : i + 1] for i in range(3)], [rows[i : i + 1] for i in range(3, 6)]
    table, down_bias = rows[6:14], rows[14:15]
    up_bias = small[:, used - up_rows : used].reshape(1, -1)

    at = jnp.arange(group, dtype=jnp.int32)
    frame, place = at // places, at % places
    video, frame = frame // FRAMES, frame % FRAMES
    span = lengths[:, video]
    alive = frame[None] < span
    allowed = (
        (place[:, None] == place[None]) & (video[:, None] == video[None]) & (frame[:, None] <= frame[None])
    )[None] & alive[:, :, None]
    allowed = allowed.astype(full)
    live = alive.astype(full).reshape(tokens, 1)
    onehot = (actions.reshape(-1)[:, None] == jnp.arange(ACTIONS)[None, :]).astype(full)
    row_pair = jnp.dot(onehot, table, precision=lax.Precision.HIGHEST)

    def to_places(value):
        value = value.reshape(micro, frame_count, seq_count, places, width)
        value = lax.all_to_all(value, "seq", split_axis=2, concat_axis=2, tiled=True)
        return value.transpose(0, 2, 1, 3, 4).reshape(tokens, width)

    def to_frames(value):
        value = value.reshape(micro, seq_count, frame_count, places, width)
        value = lax.all_to_all(value, "seq", split_axis=1, concat_axis=1, tiled=True)
        return value.transpose(0, 2, 1, 3, 4).reshape(tokens, width)

    frames_flat = frames_in.reshape(tokens, width)
    end_grad = to_places(cotangent)
    stream_one, packed_one, probs_one, mixed_one = attend_forward(
        True, spatial, frames_flat, row_pair, gain[0], shift[0], w_sin, w_sout
    )
    stream_one = to_places(stream_one)
    stream_two, packed_two, probs_two, mixed_two = attend_forward(
        False, group, stream_one, allowed, gain[1], shift[1], w_tin, w_tout
    )
    out, two_grad, hin_grad, hout_grad, gain_three, shift_three, up_grad, down_grad = hidden_layer(
        stream_two, end_grad, live, gain[2], shift[2], up_bias, down_bias, w_hin, w_hout
    )
    layer_out = to_frames(out).reshape(frames_in.shape)
    one_grad, tin_grad, tout_grad, gain_two, shift_two = attend_backward(
        False, group, two_grad, stream_one, None, gain[1], shift[1], packed_two, probs_two, mixed_two, w_tin, w_tout
    )
    one_grad = to_frames(one_grad)
    in_grad, sin_grad, sout_grad, gain_one, shift_one, sums = attend_backward(
        True, spatial, one_grad, frames_flat, row_pair, gain[0], shift[0], packed_one, probs_one, mixed_one, w_sin, w_sout
    )
    table_grad = lax.dot_general(onehot, sums, (((0,), (0,)), ((), ())), precision=lax.Precision.HIGHEST)

    rows = jnp.concatenate(
        [gain_one, gain_two, gain_three, shift_one, shift_two, shift_three, table_grad, down_grad], axis=0
    )
    rows = rows.reshape(used - up_rows, seq_count, cut).transpose(1, 0, 2)
    rows = jnp.concatenate([rows, up_grad.reshape(seq_count, up_rows, cut)], axis=1)
    rows = jnp.pad(rows, ((0, 0), (0, 32 - used), (0, 128 - cut))).astype(low).reshape(1, seq_count * 32, 128)
    rows = jnp.broadcast_to(rows, (dp_count,) + rows.shape[1:])
    first = reduce_all([hin_grad, hout_grad], seq_count, dp_count, collective_id=2)
    second = reduce_all([sin_grad, sout_grad, tin_grad, tout_grad, rows], seq_count, dp_count, collective_id=3)
    small = second[4][:, :cut]
    return (
        layer_out,
        in_grad.reshape(frames_in.shape),
        second[0],
        second[1],
        second[2],
        second[3],
        first[0],
        first[1],
        small[0:3],
        small[3:6],
        small[15:used].reshape(-1),
        small[14],
        small[6:14],
    )


def solution(mesh):
    rows = P(None, ("dp", "seq"), None, None)
    matrix = P("seq", "dp")
    cut = P(None, "seq")
    in_specs = (rows, rows, P(None, "dp"), P(None, ("dp", "seq"))) + (matrix,) * 6 + (cut, cut, P("seq"), P("seq"), cut)
    out_specs = (rows, rows) + (matrix,) * 6 + (cut, cut, P("seq"), P("seq"), cut)
    return jax.shard_map(body, mesh=mesh, in_specs=in_specs, out_specs=out_specs, check_vma=False)
```

time: 1490 us -> 798 us (0.54)
  Pallas kernels: 0 us -> 686 us
  waiting for transfers between devices: 648 us -> 43.7 us
  matrix products: 301 us -> 2.41 us
  blocking collectives: 203 us -> 0 us
  local copies, waits for them, and re-layouts: 156 us -> 36.9 us
  other arithmetic: 76.4 us -> 2.72 us
  starting transfers between devices: 79.2 us -> 23.6 us
  between operations: 19.9 us -> 1.09 us
    pallas_call x0 -> x8, Pallas kernels: none -> 686 us  [the longest x2 360 us: reduce_all(): pl.pallas_call(functools.partial(reduce_kernel, seq_count, dp_count, plan...]
    reduce_scatter x12 -> x0, waiting for transfers between devices: 320 us -> none  [the longest x1 108 us: body(): lax.psum_scatter(totals[4].astype(jnp.bfloat16), 'seq', scatter_dimension...]
    dot_general x62 -> x2, matrix products: 301 us -> 2.41 us  [the longest x1 1.44 us: body(): row_pair = jnp.dot(onehot, table, precision=lax.Precision.HIGHEST)]
    unnamed x24 -> x0, waiting for transfers between devices: 172 us -> none
    all_gather x10 -> x0, blocking collectives: 135 us -> none  [the longest x1 32 us: collect(): lax.all_gather(bias_up, 'seq', axis=0, tiled=True)]
    unnamed x1 -> x0, blocking collectives: 62.1 us -> none
    all_to_all x8 -> x4, waiting for transfers between devices: 101 us -> 43.7 us  [the longest x2 21.9 us: to_places(): lax.all_to_all(value, 'seq', split_axis=2, concat_axis=2, tiled=True)]
    all_gather x6 -> x0, waiting for transfers between devices: 55.9 us -> none  [the longest x1 55.8 us: collect(): lax.all_gather(wide[2], 'seq', axis=0, tiled=True)]
  transfers between devices with their start and end apart: 29 -> 4, of which waited for: 19 -> 2; matrix products, arithmetic and copies ran while one was open for 26% -> 2% of each run, Pallas kernels for 0% -> 53%
where the time goes in v1:
time: 798 us; the launch traced here: 797 us
  Pallas kernels  686 us (86%)
  waiting for transfers between devices  43.7 us (5%)
  local copies, waits for them, and re-layouts  36.9 us (5%)
  starting transfers between devices  23.6 us (3%)
    pallas_call x2, Pallas kernels, reduce_all(): pl.pallas_call(functools.partial(reduce_kernel, seq_count, dp_count, plan...  360 us
    pallas_call x1, Pallas kernels, gather_all(): pl.pallas_call(functools.partial(gather_kernel, seq_count, dp_count, plan...  151 us
    pallas_call x2, Pallas kernels, attend_backward(): pl.pallas_call(functools.partial(attend_backward_kernel, spatial, tokens)...  71.8 us
    pallas_call x1, Pallas kernels, hidden_layer(): pl.pallas_call(hidden_kernel, out_shape=(shape((tokens, width), low), sha...  58 us
    pallas_call x2, Pallas kernels, attend_forward(): pl.pallas_call(functools.partial(attend_forward_kernel, spatial, tokens),...  46.1 us
    all_to_all x2, waiting for transfers between devices, to_places(): lax.all_to_all(value, 'seq', split_axis=2, concat_axis=2, tiled=True)  21.9 us
    all_to_all x2, waiting for transfers between devices, to_frames(): lax.all_to_all(value, 'seq', split_axis=1, concat_axis=1, tiled=True)  21.9 us
  transfers between devices with their start and end apart: 4, of which 2 were waited for; matrix products, arithmetic and copies ran while one was open for 2% of the time, Pallas kernels for 53%

profile of v1, /device:TPU:0, one launch (start us, length us, event | category | flops | bytes accessed | tf_op | source)
XLA Modules:
  0.0 796.7 jit_solution(5495840365988318590)
XLA Ops:
  1.4 2.2 concatenate.11
  4.2 150.7 %gather_weights.1 = (bf16[2,4,2,2,64,1536]{5,4,3,2,1,0:T(8,128)(2,1)}, bf16[2,4,2,2,64,512]{5,4,3,2,1,0:T(8,128)(2,1)}, bf16[2,4,2,2,64,1536]{5,4,3,2,1,0:T(8,12...) custom-call(bf16[64,1536]{1,0:T(8,128)(2,1)} %refs_0_.1, ...), custom_call_target="tpu_custom_call" | custom-call | tf_op jit(solution)/shard_map/gather_weights/pallas_call | solution.py:291
  157.5 1.4 fusion.1.refs_1_.refs_2_
  158.9 22.9 %space_forward.1 = (bf16[512,1024]{1,0:T(8,128)(2,1)}, bf16[512,3072]{1,0:T(8,128)(2,1)}, bf16[32,256,256]{2,1,0:T(8,128)(2,1)}, bf16[512,1024]{1,0:T(8,128)(2,1)}) custom-call(bf16[512,1024]{1,0:T(8,128)(2,1)} %bitcast.64, f32[2,1024]{1,0:T(2,128)} %fusion.1.refs_1_.refs_2_, f32[1,1024]{1,0:T(1,128)} %slice.91.refs_2_.refs_3_, ...), custom_call_target="tpu_custom_call" | custom-call | tf_op jit(solution)/shard_map/space_forward/pallas_call | solution.py:564
  181.8 2.5 copy.55
  184.3 3.8 all-to-all-start
  189.2 21.9 %all-to-all-done = bf16[2,1,16,16,1024]{4,3,0,1,2:T(8,128)(2,1)S(1)} async-done(((bf16[2,1,16,16,1024]{4,3,0,1,2:T(8,128)(2,1)}), bf16[2,1,16,16,1024]{4,3,0,1,2:T(8,128)(2,1)S(1)}, u32[]{:S(2)}, u32[]{:S(2)}) %all-to-all-start) | async-done | bytes 1048608 | tf_op jit(solution)/shard_map/all_to_all | solution.py:1209
  211.1 6.9 all-to-all-start.1
  225.1 23.3 %time_forward.1 = (f32[512,1024]{1,0:T(8,128)}, bf16[512,3072]{1,0:T(8,128)(2,1)}, bf16[32,256,256]{2,1,0:T(8,128)(2,1)}, bf16[512,1024]{1,0:T(8,128)(2,1)}) custom-call(bf16[512,1024]{1,0:T(8,128)(2,1)} %bitcast.51, f32[2,256,256]{2,1,0:T(8,128)} %and_convert_fusion.refs_1_, f32[1,1024]{1,0:T(1,128)} %slice.95.refs_2_, f32[1,1024]{1,0:T(1,128)} %slice.97.refs_3_, ...), custom_call_target="tpu_custom_call" | custom-call | tf_op jit(solution)/shard_map/time_forward/pallas_call | solution.py:564
  249.5 58.0 %hidden_layer.1 = (bf16[512,1024]{1,0:T(8,128)(2,1)}, f32[512,1024]{1,0:T(8,128)}, bf16[2,1024,2048]{2,1,0:T(8,128)(2,1)}, bf16[2,4096,512]{2,1,0:T(8,128)(2,1)}...) custom-call(f32[512,1024]{1,0:T(8,128)} %get-tuple-element.60.stream, ...), custom_call_target="tpu_custom_call" | custom-call | tf_op jit(solution)/shard_map/hidden_layer/pallas_call | solution.py:797
  307.5 36.0 %time_backward.1 = (bf16[512,1024]{1,0:T(8,128)(2,1)}, bf16[2,1024,1536]{2,1,0:T(8,128)(2,1)}, bf16[2,1024,512]{2,1,0:T(8,128)(2,1)}, f32[1,1024]{1,0:T(1,128)}, f32[1,1024]{1,0:T(1,128)}) custom-call(f32[512,1024]{1,0:T(8,128)} %get-tuple-element.64.refs_0_, bf16[512,1024]{1,0:T(8,128)(2,1)} %bitcast.52, f32[1,1024]{1,0:T(1,128)} %slice.95.refs_2_, ...), custom_call_target="tpu_custom_call" | custom-call | tf_op jit(solution)/shard_map/time_backward/pallas_call | solution.py:656
  343.5 2.4 copy.63
  345.9 6.0 all-to-all-start.3
  353.0 21.9 %all-to-all-done.3 = bf16[2,16,1,16,1024]{4,3,0,2,1:T(8,128)(2,1)S(1)} async-done(((bf16[2,16,1,16,1024]{4,3,0,2,1:T(8,128)(2,1)}), bf16[2,16,1,16,1024]{4,3,0,2,1:T(8,128)(2,1)S(1)}, u32[]{:S(2)}, u32[]{:S(2)}) %all-to-all-start.3) | async-done | bytes 1048608 | tf_op jit(solution)/shard_map/all_to_all | solution.py:1214
  374.8 6.9 all-to-all-start.2
  382.0 176.2 %reduce_gradients.3 = (f32[64,2048]{1,0:T(8,128)}, f32[256,512]{1,0:T(8,128)}) custom-call(bf16[2,4,2,2,64,2048]{5,4,3,2,1,0:T(8,128)(2,1)} %bitcast.55, bf16[2,4,2,2,256,512]{5,4,3,2,1,0:T(8,128)(2,1)} %bitcast.56), custom_call_target="tpu_custom_call" | custom-call | tf_op jit(solution)/shard_map/reduce_gradients/pallas_call | solution.py:1133
  559.2 35.9 %space_backward.1 = (bf16[512,1024]{1,0:T(8,128)(2,1)}, bf16[2,1024,1536]{2,1,0:T(8,128)(2,1)}, bf16[2,1024,512]{2,1,0:T(8,128)(2,1)}, f32[1,1024]{1,0:T(1,128)}, f32[1,1024]{1,0:T(1,128)}, /*index=5*/f32[2,1024]{1,0:T(2,128)}) custom-call(bf16[512,1024]{1,0:T(8,128)(2,1)} %bitcast.66, bf16[512,1024]{1,0:T(8,128)(2,1)} %bitcast.65, ...), custom_call_target="tpu_custom_call" | custom-call | tf_op jit(solution)/shard_map/space_backward/pallas_call | solution.py:656
  598.6 183.5 %reduce_gradients.2 = (f32[64,1536]{1,0:T(8,128)}, f32[64,512]{1,0:T(8,128)}, f32[64,1536]{1,0:T(8,128)}, f32[64,512]{1,0:T(8,128)}, f32[32,128]{1,0:T(8,128)}) custom-call(bf16[2,4,2,2,64,1536]{5,4,3,2,1,0:T(8,128)(2,1)} %bitcast.62, bf16[2,4,2,2,64,512]{5,4,3,2,1,0:T(8,128)(2,1)} %bitcast.68, bf16[2,4,2,2,64,1536]{5,4,3,2,1,0:T(8,128)(2,1)} %bitcast.61, ...), custom_call_target="tpu_custom_call" | custom-call | tf_op jit(solution)/shard_map/reduce_gradients/pallas_call | solution.py:1133
  783.0 1.3 slice.109
  786.1 1.3 fusion.5
  788.5 1.8 copy.83
  790.3 1.6 copy.84
  791.8 1.8 copy.85
  793.6 1.6 copy.86
  (81 shorter events, 24.2 us)
Async XLA Ops:
  181.8 6.4 copy-start
  181.8 36.2 %copy-start.10 = (s32[2,1]{0,1:T(1,128)S(1)}, s32[2,1]{0,1:T(1,128)}, u32[]{:S(2)}) copy-start(s32[2,1]{0,1:T(1,128)} %param.17) | copy-start | bytes 28
  184.3 26.8 %all-to-all-start = ((bf16[2,1,16,16,1024]{4,3,0,1,2:T(8,128)(2,1)}), bf16[2,1,16,16,1024]{4,3,0,1,2:T(8,128)(2,1)S(1)}, u32[]{:S(2)}, u32[]{:S(2)}) async-start(bf16[2,1,16,16,1024]{4,3,0,1,2:T(8,128)(2,1)} %copy.55), calls=%async_computation | async-start | bytes 2097152 | tf_op jit(solution)/shard_map/all_to_all | solution.py:1209
  211.1 37.3 %all-to-all-start.1 = ((bf16[2,1,16,16,1024]{4,3,0,1,2:T(8,128)(2,1)}), bf16[2,1,16,16,1024]{4,3,0,1,2:T(8,128)(2,1)S(1)}, u32[]{:S(2)}, u32[]{:S(2)}) async-start(bf16[2,1,16,16,1024]{4,3,0,1,2:T(8,128)(2,1)} %copy.57), calls=%async_computation.1 | async-start | bytes 2097152 | tf_op jit(solution)/shard_map/all_to_all | solution.py:1209
  343.4 8.5 %copy-start.1 = (bf16[512,1024]{1,0:T(8,128)(2,1)S(1)}, bf16[512,1024]{1,0:T(8,128)(2,1)}, u32[]{:S(2)}) copy-start(bf16[512,1024]{1,0:T(8,128)(2,1)} %get-tuple-element.63) | copy-start | bytes 3145732
  343.4 38.3 %copy-start.9 = (f32[1,1024]{1,0:T(1,128)S(1)}, f32[1,1024]{1,0:T(1,128)}, u32[]{:S(2)}) copy-start(f32[1,1024]{1,0:T(1,128)} %get-tuple-element.78) | copy-start | bytes 12292
  343.4 38.3 %copy-start.8 = (f32[1,1024]{1,0:T(1,128)S(1)}, f32[1,1024]{1,0:T(1,128)}, u32[]{:S(2)}) copy-start(f32[1,1024]{1,0:T(1,128)} %get-tuple-element.81) | copy-start | bytes 12292
  343.5 38.3 %copy-start.7 = (f32[1,1024]{1,0:T(1,128)S(1)}, f32[1,1024]{1,0:T(1,128)}, u32[]{:S(2)}) copy-start(f32[1,1024]{1,0:T(1,128)} %get-tuple-element.79) | copy-start | bytes 12292
  343.5 38.3 %copy-start.6 = (f32[1,1024]{1,0:T(1,128)S(1)}, f32[1,1024]{1,0:T(1,128)}, u32[]{:S(2)}) copy-start(f32[1,1024]{1,0:T(1,128)} %get-tuple-element.82) | copy-start | bytes 12292
  343.5 38.3 %copy-start.5 = (f32[1,1024]{1,0:T(1,128)S(1)}, f32[1,1024]{1,0:T(1,128)}, u32[]{:S(2)}) copy-start(f32[1,1024]{1,0:T(1,128)} %get-tuple-element.84) | copy-start | bytes 12292
  343.5 38.3 %copy-start.4 = (f32[1,4096]{1,0:T(1,128)S(1)}, f32[1,4096]{1,0:T(1,128)}, u32[]{:S(2)}) copy-start(f32[1,4096]{1,0:T(1,128)} %get-tuple-element.85) | copy-start | bytes 49156
  345.9 28.9 %all-to-all-start.3 = ((bf16[2,16,1,16,1024]{4,3,0,2,1:T(8,128)(2,1)}), bf16[2,16,1,16,1024]{4,3,0,2,1:T(8,128)(2,1)S(1)}, u32[]{:S(2)}, u32[]{:S(2)}) async-start(bf16[2,16,1,16,1024]{4,3,0,2,1:T(8,128)(2,1)} %copy.63), calls=%async_computation.3 | async-start | bytes 2097152 | tf_op jit(solution)/shard_map/all_to_all | solution.py:1214
  374.8 412.6 %all-to-all-start.2 = ((bf16[2,16,1,16,1024]{4,3,0,2,1:T(8,128)(2,1)}), bf16[2,16,1,16,1024]{4,3,0,2,1:T(8,128)(2,1)S(1)}, u32[]{:S(2)}, u32[]{:S(2)}) async-start(bf16[2,16,1,16,1024]{4,3,0,2,1:T(8,128)(2,1)} %copy.61), calls=%async_computation.2 | async-start | bytes 2097152 | tf_op jit(solution)/shard_map/all_to_all | solution.py:1214
  559.2 37.3 %copy-start.11 = (s32[2,1]{0,1:T(1,128)S(1)}, s32[2,1]{0,1:T(1,128)}, u32[]{:S(2)}) copy-start(s32[2,1]{0,1:T(1,128)} %param.18) | copy-start | bytes 28
  782.2 13.0 %copy-start.3 = (f32[64,2048]{1,0:T(8,128)S(1)}, f32[64,2048]{1,0:T(8,128)}, u32[]{:S(2)}) copy-start(f32[64,2048]{1,0:T(8,128)} %get-tuple-element.179) | copy-start | bytes 1572868
  782.2 13.8 %copy-start.2 = (f32[256,512]{1,0:T(8,128)S(1)}, f32[256,512]{1,0:T(8,128)}, u32[]{:S(2)}) copy-start(f32[256,512]{1,0:T(8,128)} %get-tuple-element.180) | copy-start | bytes 1572868

commit v2 on v1

--- a/solution.py
+++ b/solution.py
@@ -36,13 +36,15 @@
         pl.when(condition)(action)
 
 
-def entry_barrier(place):
+def entry_barrier(place, change=None):
     barrier = pltpu.get_barrier_semaphore()
 
     def greet(device):
         pl.semaphore_signal(barrier, inc=1, device_id=device, device_id_type=MESH)
 
     count = 1
+    if change is not None:
+        count = count + change.greet()
     greet(place.sibling())
     for axis in ("x", "y", "z"):
         here, size = place.at[axis], place.size[axis]
@@ -373,7 +375,20 @@
     shift_out[...] = jnp.sum(shift_sum, axis=0, keepdims=True)
 
 
-def project(rows, weight, emit, tile_max=512):
+def chunks(count, step, units):
+    units = max(u for u in range(1, min(units, count) + 1) if count % u == 0)
+    each = count // units
+    for unit in range(units):
+        loop(each, lambda index, unit=unit: step(unit * each + index))
+        yield
+
+
+def drain(work):
+    for _ in work:
+        pass
+
+
+def project(rows, weight, emit, tile_max=512, units=1):
     parts, _, size = weight.shape
     tile = tile_of(size, tile_max)
     for part in range(parts):
@@ -383,10 +398,10 @@
             columns = pl.ds(pl.multiple_of(part * size + index * tile, 128), tile)
             emit(columns, dot(rows[...], weight[part, :, inner]))
 
-        loop(size // tile, step)
-
-
-def project_back(grad, weight, emit, tile_max=512):
+        yield from chunks(size // tile, step, units)
+
+
+def project_back(grad, weight, emit, tile_max=512, units=1):
     parts, depth, size = weight.shape
     tile = tile_of(depth, tile_max)
 
@@ -398,22 +413,28 @@
             total = term if total is None else total + term
         emit(inner, total)
 
-    loop(depth // tile, step)
-
-
-def outer(rows, grad, out, tile_max=512):
+    yield from chunks(depth // tile, step, units)
+
+
+def outer(rows, grad, out, stage, sems, units=1):
     parts, depth, size = out.shape
-    tile = tile_of(depth, tile_max)
+    tile = stage.shape[2]
+
+    def leave(index, slot):
+        return pltpu.make_async_copy(stage.at[slot], out.at[:, at_rows(index, tile), :], sems.at[slot])
 
     def step(index):
-        inner = at_rows(index, tile)
-        left = rows[:, inner]
+        slot = lax.rem(index, 2)
+        pl.when(index >= 2)(lambda: leave(index - 2, slot).wait())
+        left = rows[:, at_rows(index, tile)]
         for part in range(parts):
-            out[part, inner, :] = dot(
-                left, grad[:, part * size : (part + 1) * size], TN
-            ).astype(out.dtype)
-
-    loop(depth // tile, step)
+            stage[slot, part] = dot(left, grad[:, part * size : (part + 1) * size], TN).astype(out.dtype)
+        leave(index, slot).start()
+
+    count = depth // tile
+    yield from chunks(count, step, units)
+    leave(count - 2, (count - 2) % 2).wait()
+    leave(count - 1, (count - 1) % 2).wait()
 
 
 def head_mask(shape, axis, head):
@@ -438,7 +459,7 @@
     ]
 
 
-def attention_forward(packed, allowed, probs, mixed, tokens):
+def attention_forward(packed, allowed, probs, mixed, tokens, units=1):
     width = mixed.shape[1]
 
     def step(index):
@@ -459,10 +480,10 @@
             total = term if total is None else total + term
         mixed[rows, q_at] = total.T.astype(jnp.bfloat16)
 
-    loop(mixed.shape[0] // tokens * (width // 128), step)
-
-
-def attention_backward(packed, probs, grad, packed_grad, tokens):
+    yield from chunks(mixed.shape[0] // tokens * (width // 128), step, units)
+
+
+def attention_backward(packed, probs, grad, packed_grad, tokens, units=1):
     width = grad.shape[1]
 
     def step(index):
@@ -493,7 +514,7 @@
         packed_grad[rows, k_at] = key_grad.astype(jnp.bfloat16)
         packed_grad[rows, v_at] = value_grad.astype(jnp.bfloat16)
 
-    loop(grad.shape[0] // tokens * (width // 128), step)
+    yield from chunks(grad.shape[0] // tokens * (width // 128), step, units)
 
 
 class Fetch:
@@ -533,8 +554,8 @@
     def emit(columns, value):
         packed[:, columns] = value.astype(jnp.bfloat16)
 
-    project(normed, v_in, emit)
-    attention_forward(packed, allowed, probs, mixed, tokens)
+    drain(project(normed, v_in, emit))
+    drain(attention_forward(packed, allowed, probs, mixed, tokens))
     second.wait()
 
     def emit_out(columns, value):
@@ -546,7 +567,7 @@
         else:
             out[:, columns] = (stream[:, columns].astype(jnp.float32) + value).astype(out.dtype)
 
-    project(mixed, v_out, emit_out)
+    drain(project(mixed, v_out, emit_out))
 
 
 def vmem(count):
@@ -582,16 +603,11 @@
     )(stream, extra, gain, shift, w_in, w_out)
 
 
-def attend_backward_kernel(spatial, tokens, *refs):
-    if spatial:
-        (up, stream, row_pair, gain, shift, packed_h, probs_h, mixed, w_in_h, w_out_h,
-         down, w_in_grad, w_out_grad, gain_out, shift_out, sums, *rest) = refs
-        read = spatial_reader(stream, row_pair, tokens)
-    else:
-        (up, stream, gain, shift, packed_h, probs_h, mixed, w_in_h, w_out_h,
-         down, w_in_grad, w_out_grad, gain_out, shift_out, *rest) = refs
-        read = lambda rows: stream[rows, :].astype(jnp.float32)
-    normed, up_low, mixed_grad, packed_grad, normed_grad, packed, probs, w_in, w_out, sems = rest
+def attend_backward_work(spatial, tokens, up, stream, extra, gain, shift, packed_h, probs_h, mixed, w_in_h, w_out_h,
+                         down, w_in_grad, w_out_grad, gain_out, shift_out, sums,
+                         normed, up_low, mixed_grad, packed_grad, normed_grad, packed, probs, w_in, w_out,
+                         in_stage, out_stage, sems):
+    read = spatial_reader(stream, extra, tokens) if spatial else (lambda rows: stream[rows, :].astype(jnp.float32))
     fetches = [
         Fetch(src, dst, sems.at[i]).start()
         for i, (src, dst) in enumerate(
@@ -605,74 +621,59 @@
 
     loop(up.shape[0] // ROWS, lower)
     norm_forward(read, gain, shift, normed)
+    yield
     fetches[0].wait()
 
     def emit_mixed(columns, value):
         mixed_grad[:, columns] = value.astype(jnp.bfloat16)
 
-    project_back(up_low, w_out, emit_mixed)
-    outer(mixed, up_low, w_out_grad)
+    yield from project_back(up_low, w_out, emit_mixed, units=2)
+    yield from outer(mixed, up_low, w_out_grad, out_stage, sems.at[pl.ds(4, 2)], units=2)
     fetches[1].wait()
     fetches[2].wait()
-    attention_backward(packed, probs, mixed_grad, packed_grad, tokens)
+    yield from attention_backward(packed, probs, mixed_grad, packed_grad, tokens, units=8)
     fetches[3].wait()
-    outer(normed, packed_grad, w_in_grad)
+    yield from outer(normed, packed_grad, w_in_grad, in_stage, sems.at[pl.ds(6, 2)], units=4)
 
     def emit_normed(columns, value):
         normed_grad[:, columns] = value
 
-    project_back(packed_grad, w_in, emit_normed)
+    yield from project_back(packed_grad, w_in, emit_normed, 256, units=4)
+    block = down.shape[1]
+
+    def put(index, value):
+        down[pl.ds(index * (ROWS // block), ROWS // block)] = value.reshape(-1, block, value.shape[1]).astype(down.dtype)
+
     if spatial:
         sums[...] = jnp.zeros_like(sums)
 
         def write(index, rows, value):
-            down[rows, :] = value.astype(down.dtype)
+            put(index, value)
             micro = rows.start // tokens
             sums[pl.ds(micro, 1), :] += jnp.sum(fold8(value), axis=0, keepdims=True)
     else:
 
         def write(index, rows, value):
-            down[rows, :] = value.astype(down.dtype)
+            put(index, value)
 
     norm_backward(
         read, gain, normed_grad, lambda rows: up[rows, :].astype(jnp.float32), write, gain_out, shift_out
     )
-
-
-def attend_backward(spatial, tokens, up, stream, extra, gain, shift, packed, probs, mixed, w_in, w_out):
-    total, width = stream.shape
-    low, full = jnp.bfloat16, jnp.float32
-    shape = jax.ShapeDtypeStruct
-    outs = [
-        shape((total, width), low),
-        shape(w_in.shape, low),
-        shape(w_out.shape, low),
-        shape((1, width), full),
-        shape((1, width), full),
-    ]
-    if spatial:
-        outs.append(shape((total // tokens, width), full))
-    front = (up, stream) + ((extra,) if spatial else ()) + (gain, shift)
-    return pl.pallas_call(
-        functools.partial(attend_backward_kernel, spatial, tokens),
-        out_shape=tuple(outs),
-        in_specs=vmem(len(front)) + hbm(2) + vmem(1) + hbm(2),
-        out_specs=vmem(len(outs)),
-        scratch_shapes=[
-            pltpu.VMEM((total, width), low),
-            pltpu.VMEM((total, width), low),
-            pltpu.VMEM((total, width), low),
-            pltpu.VMEM((total, 3 * width), low),
-            pltpu.VMEM((total, width), full),
-            pltpu.VMEM(packed.shape, low),
-            pltpu.VMEM(probs.shape, low),
-            pltpu.VMEM(w_in.shape, low),
-            pltpu.VMEM(w_out.shape, low),
-            pltpu.SemaphoreType.DMA((4,)),
-        ],
-        compiler_params=pltpu.CompilerParams(vmem_limit_bytes=VMEM_LIMIT),
-        name="space_backward" if spatial else "time_backward",
-    )(*front, packed, probs, mixed, w_in, w_out)
+    yield
+
+
+END = object()
+
+
+def weave(work, events, ratio):
+    due = 0.0
+    for event in events:
+        event()
+        due += ratio
+        while due >= 1:
+            due -= 1
+            next(work, END)
+    drain(work)
 
 
 GELU_A = 0.7978845608028654
@@ -712,72 +713,29 @@
         active[:, columns] = act.astype(low)
         slope[:, columns] = rate.astype(low)
 
-    project(normed, w_up, emit_expand, 256)
+    drain(project(normed, w_up, emit_expand, 256))
     second.wait()
 
     def emit_out(columns, value):
         end = stream[:, columns] + value + down_bias[:, columns]
         out[:, columns] = (end * live[...]).astype(out.dtype)
 
-    project(active, w_down, emit_out, 256)
+    drain(project(active, w_down, emit_out, 256))
 
     def emit_active(columns, value):
         grad = value * slope[:, columns].astype(jnp.float32)
         up_bias_out[:, columns] = jnp.sum(grad, axis=0, keepdims=True)
         expand_low[:, columns] = grad.astype(low)
 
-    project_back(end_low, w_down, emit_active, 256)
-
-    hidden, size = w_down.shape[1], w_down.shape[2]
-    tile = down_stage.shape[2]
-
-    def send_down(index, slot):
-        return pltpu.make_async_copy(
-            down_stage.at[slot], down_grad_h.at[:, at_rows(index, tile), :], sems.at[2 + slot]
-        )
-
-    def step_down(index):
-        slot = lax.rem(index, 2)
-        pl.when(index >= 2)(lambda: send_down(index - 2, slot).wait())
-        left = active[:, at_rows(index, tile)]
-        for part in range(parts):
-            down_stage[slot, part] = dot(
-                left, end_low[:, part * size : (part + 1) * size], TN
-            ).astype(low)
-        send_down(index, slot).start()
-
-    count = hidden // tile
-    loop(count, step_down)
-    send_down(count - 2, (count - 2) % 2).wait()
-    send_down(count - 1, (count - 1) % 2).wait()
-
-    size_up = w_up.shape[2]
-    tile_up = up_stage.shape[2]
-
-    def send_up(index, slot):
-        return pltpu.make_async_copy(
-            up_stage.at[slot], up_grad_h.at[:, at_rows(index, tile_up), :], sems.at[4 + slot]
-        )
-
-    def step_up(index):
-        slot = lax.rem(index, 2)
-        pl.when(index >= 2)(lambda: send_up(index - 2, slot).wait())
-        left = normed[:, at_rows(index, tile_up)]
-        for part in range(parts):
-            up_stage[slot, part] = dot(
-                left, expand_low[:, part * size_up : (part + 1) * size_up], TN
-            ).astype(low)
-        send_up(index, slot).start()
-
-    count_up = width // tile_up
-    loop(count_up, step_up)
+    drain(project_back(end_low, w_down, emit_active, 256))
+
+    drain(outer(active, end_low, down_grad_h, down_stage, sems.at[pl.ds(2, 2)]))
+    drain(outer(normed, expand_low, up_grad_h, up_stage, sems.at[pl.ds(4, 2)]))
 
     def emit_normed(columns, value):
         normed_grad[:, columns] = value
 
-    project_back(expand_low, w_up, emit_normed, 256)
-    send_up(count_up - 2, (count_up - 2) % 2).wait()
-    send_up(count_up - 1, (count_up - 1) % 2).wait()
+    drain(project_back(expand_low, w_up, emit_normed, 256))
 
     def write(index, rows, value):
         down[rows, :] = value
@@ -840,14 +798,16 @@
         self.ticks = 1 + self.third_ticks + n2 + (1 if n1 == 2 else n1)
 
     @staticmethod
-    def scratch(n, sizes, rows, columns, dtype):
-        n1, n2, n3 = n
+    def scratch(order, sizes, rows, columns, dtype):
+        size = dict(zip(("y", "z", "x"), sizes))
+        n1, n2, n3 = [size[axis] for axis in order]
+        left = (n2, n1) if n3 == 2 else tuple(size[a] for a in ("y", "z", "x") if a != order[2])
         slots = lambda count: 1 if count == 2 else count + 1
         return (
             [
                 pltpu.VMEM(sizes + (rows, columns), dtype),
                 pltpu.VMEM(sizes + (rows, columns), dtype),
-                pltpu.VMEM((slots(n3), n2, n1, rows, columns), dtype),
+                pltpu.VMEM((slots(n3),) + left + (rows, columns), dtype),
                 pltpu.VMEM((slots(n2), n1, rows, columns), dtype),
                 pltpu.VMEM((slots(n1), rows, columns), dtype),
             ],
@@ -932,7 +892,8 @@
                         2, self.third_sems.at[0, 0, second], self.block(slice(None), second, other),
                         self.from_third.at[0, second], other, self.third_sems.at[1, 0, second],
                     )
-        now = now - 1
+            return
+        now = now - 2
         if not self.pair:
             if now < n3:
                 self.line(2, now)
@@ -942,8 +903,6 @@
         now = now - n2
         if 0 <= now and now < (1 if n1 == 2 else n1):
             self.line(0, now)
-        if now == (1 if n1 == 2 else n1):
-            pass
 
     def stage_ref(self, stage, index):
         if stage == 2:
@@ -1084,54 +1043,67 @@
     return plan
 
 
-def run_pieces(pieces, offsets, skew, work=()):
+def piece_events(pieces, offsets, skew):
     events = []
     for i, piece in enumerate(pieces):
         for e in range(piece.ticks + 1):
-            own = offsets[piece.order[2]] if isinstance(offsets, dict) else offsets
+            own = offsets[piece.order[2]]
             when_at = own[e] if e < len(own) else own[-1] + e - len(own) + 1
             events.append((when_at + i * skew, i, e))
     events.sort()
-    for _, i, e in events:
-        pieces[i].tick(e)
-
-
-def reduce_kernel(seq_count, dp_count, plan, offsets, skew, count, *refs):
+    return [functools.partial(pieces[i].tick, e) for _, i, e in events]
+
+
+LATE = (0, 1, 6, 7, 8, 9, 10)
+OFFSETS = {"x": LATE, "y": LATE, "z": (0, 1, 2, 3, 4, 5, 6, 7, 8)}
+PER_PIECE = 9
+
+
+def weight_orders(index):
+    third = ("x", "z", "y") if index % 2 == 0 else ("y", "z", "x")
+    first = ("x", "y", "z") if index % 2 == 0 else ("y", "x", "z")
+    return (("z", "x", "y"), ("z", "y", "x"), first, third)
+
+
+def reduce_plan(partials, seq_count, dp_count, parts=4):
+    sizes = (dp_count, 4, seq_count // 8)
+    blocked, outs, scratch = [], [], []
+    for p in partials:
+        rows = p.shape[1] // seq_count
+        blocked.append(p.reshape(sizes + (2, rows, p.shape[2])))
+        outs.append(jax.ShapeDtypeStruct((rows, p.shape[2]), jnp.float32))
+    plan = split_plan([o.shape[0] for o in outs], parts, weight_orders)
+    for index, first, rows, order in plan:
+        bufs, sems = Reduce.scratch(
+            order, sizes, rows, outs[index].shape[1], partials[index].dtype
+        )
+        scratch += bufs + sems
+    return plan, blocked, outs, scratch
+
+
+def reduce_pieces(place, plan, partials, outs, scratch):
+    pieces = []
+    for number, (index, first, rows, order) in enumerate(plan):
+        own = scratch[PER_PIECE * number : PER_PIECE * number + PER_PIECE]
+        pieces.append(Reduce(place, order, partials[index], pl.ds(first, rows), outs[index], own[:5], own[5:]))
+    return pieces
+
+
+def reduce_kernel(seq_count, dp_count, plan, count, *refs):
     partials, outs, rest = refs[:count], refs[count : 2 * count], refs[2 * count :]
     place = Place(seq_count, dp_count)
     entry_barrier(place)
-    pieces = []
-    for number, (index, first, rows, order) in enumerate(plan):
-        own = rest[9 * number : 9 * number + 9]
-        pieces.append(Reduce(place, order, partials[index], pl.ds(first, rows), outs[index], own[:5], own[5:]))
-    run_pieces(pieces, offsets, skew)
+    pieces = reduce_pieces(place, plan, partials, outs, rest)
+    for event in piece_events(pieces, OFFSETS, 0):
+        event()
     for piece in pieces:
         piece.finish_send()
 
 
-def weight_orders(index):
-    if index in (0, 1, 4):
-        return (("z", "x", "y"), ("z", "y", "x"), ("x", "y", "z"), ("x", "z", "y"))
-    return (("z", "x", "y"), ("z", "y", "x"), ("y", "x", "z"), ("y", "z", "x"))
-
-
-def reduce_all(partials, seq_count, dp_count, parts=2, offsets=(0, 1, 3, 4, 5, 6, 7), skew=1, collective_id=0, orders=weight_orders):
-    size = {"z": 4, "x": seq_count // 8, "y": dp_count}
-    sizes = (dp_count, 4, size["x"])
-    scratch = []
-    blocked, outs = [], []
-    for p in partials:
-        rows = p.shape[1] // seq_count
-        blocked.append(p.reshape((dp_count, 4, size["x"], 2, rows, p.shape[2])))
-        outs.append(jax.ShapeDtypeStruct((rows, p.shape[2]), jnp.float32))
-    plan = split_plan([o.shape[0] for o in outs], parts, orders)
-    for index, first, rows, order in plan:
-        bufs, sems = Reduce.scratch(
-            [size[a] for a in order], sizes, rows, outs[index].shape[1], partials[index].dtype
-        )
-        scratch += bufs + sems
+def reduce_all(partials, seq_count, dp_count, collective_id):
+    plan, blocked, outs, scratch = reduce_plan(partials, seq_count, dp_count)
     return pl.pallas_call(
-        functools.partial(reduce_kernel, seq_count, dp_count, plan, offsets, skew, len(partials)),
+        functools.partial(reduce_kernel, seq_count, dp_count, plan, len(partials)),
         out_shape=outs,
         in_specs=hbm(len(partials)),
         out_specs=vmem(len(partials)),
@@ -1141,6 +1113,154 @@
         ),
         name="reduce_gradients",
     )(*blocked)
+
+
+class Exchange:
+    def __init__(self, place, src, dst, sems, micro, seq_count, forward):
+        self.place, self.src, self.dst, self.sems = place, src, dst, sems
+        self.micro, self.count, self.forward = micro, seq_count, forward
+        self.each = src.shape[0] // (micro * seq_count)
+        self.me = lax.axis_index("seq")
+
+    def indices(self, peer):
+        frames = self.count * self.each
+        out = []
+        for micro in range(self.micro):
+            for f in range(self.each):
+                by_frame = (micro * self.each + f) * self.count
+                if self.forward:
+                    out.append((by_frame + peer, micro * frames + self.me * self.each + f))
+                else:
+                    out.append((micro * frames + peer * self.each + f, by_frame + self.me))
+        return out
+
+    def greet(self):
+        barrier = pltpu.get_barrier_semaphore()
+
+        def one(step):
+            peer = lax.rem(self.me + step + 1, self.count)
+            pl.semaphore_signal(
+                barrier, inc=1, device_id=(lax.axis_index("dp"), peer), device_id_type=MESH
+            )
+
+        loop(self.count - 1, one)
+        return self.count - 1
+
+    def start(self):
+        for here, there in self.indices(self.me):
+            pltpu.make_async_copy(self.src.at[here], self.dst.at[there], self.sems.at[2]).start()
+
+        def one(step):
+            peer = lax.rem(self.me + step + 1, self.count)
+            for here, there in self.indices(peer):
+                pltpu.make_async_remote_copy(
+                    src_ref=self.src.at[here], dst_ref=self.dst.at[there],
+                    send_sem=self.sems.at[0], recv_sem=self.sems.at[1],
+                    device_id=(lax.axis_index("dp"), peer), device_id_type=MESH,
+                ).start()
+
+        loop(self.count - 1, one)
+
+    def finish(self):
+        own = self.micro * self.each
+        most = self.dst.at[pl.ds(0, own * (self.count - 1))]
+        pltpu.make_async_copy(most, most, self.sems.at[1]).wait()
+        pltpu.make_async_copy(most, most, self.sems.at[0]).wait()
+        few = self.dst.at[pl.ds(0, own)]
+        pltpu.make_async_copy(few, few, self.sems.at[2]).wait()
+
+
+def attend_backward_kernel(spatial, tokens, micro, seq_count, dp_count, plan, counts, ratio, *refs):
+    fronts, count, outs_count = counts
+    refs = list(refs)
+    take = lambda n: [refs.pop(0) for _ in range(n)]
+    if spatial:
+        up, stream, extra, gain, shift = take(5)
+    else:
+        (up, stream, gain, shift), extra = take(4), None
+    packed_h, probs_h, mixed, w_in_h, w_out_h = take(5)
+    partials = take(count)
+    arrived = None if spatial else take(1)[0]
+    down, w_in_grad, w_out_grad, gain_out, shift_out = take(5) if spatial else [None] + take(4)
+    sums = take(1)[0] if spatial else None
+    outs = take(count)
+    own = take(12)
+    if not spatial:
+        down = take(1)[0]
+        change_sems = take(1)[0]
+    place = Place(seq_count, dp_count)
+    change = None if spatial else Exchange(place, down, arrived, change_sems, micro, seq_count, False)
+    entry_barrier(place, change)
+    pieces = reduce_pieces(place, plan, partials, outs, refs)
+    work = attend_backward_work(
+        spatial, tokens, up, stream, extra, gain, shift, packed_h, probs_h, mixed, w_in_h, w_out_h,
+        down, w_in_grad, w_out_grad, gain_out, shift_out, sums, *own
+    )
+
+    def all_work():
+        yield from work
+        if change is not None:
+            change.start()
+            yield
+
+    weave(all_work(), piece_events(pieces, OFFSETS, 0), ratio)
+    if change is not None:
+        change.finish()
+    for piece in pieces:
+        piece.finish_send()
+
+
+def attend_backward(spatial, tokens, block, micro, seq_count, dp_count, partials, ratio, collective_id,
+                    up, stream, extra, gain, shift, packed, probs, mixed, w_in, w_out):
+    total, width = stream.shape
+    low, full = jnp.bfloat16, jnp.float32
+    shape = jax.ShapeDtypeStruct
+    plan, blocked, sums_out, scratch = reduce_plan(partials, seq_count, dp_count)
+    down = shape((total // block, block, width), low)
+    outs = [
+        down,
+        shape(w_in.shape, low),
+        shape(w_out.shape, low),
+        shape((1, width), full),
+        shape((1, width), full),
+    ]
+    specs = (vmem(1) if spatial else hbm(1)) + hbm(2) + vmem(2)
+    if spatial:
+        outs.append(shape((total // tokens, width), full))
+        specs += vmem(1)
+    front = (up, stream) + ((extra,) if spatial else ()) + (gain, shift)
+    own = [
+        pltpu.VMEM((total, width), low),
+        pltpu.VMEM((total, width), low),
+        pltpu.VMEM((total, width), low),
+        pltpu.VMEM((total, 3 * width), low),
+        pltpu.VMEM((total, width), full),
+        pltpu.VMEM(packed.shape, low),
+        pltpu.VMEM(probs.shape, low),
+        pltpu.VMEM(w_in.shape, low),
+        pltpu.VMEM(w_out.shape, low),
+        pltpu.VMEM((2, dp_count, 128, w_in.shape[2]), low),
+        pltpu.VMEM((2, dp_count, 128, w_out.shape[2]), low),
+        pltpu.SemaphoreType.DMA((8,)),
+    ]
+    if not spatial:
+        own += [pltpu.VMEM(down.shape, low), pltpu.SemaphoreType.DMA((3,))]
+    result = pl.pallas_call(
+        functools.partial(
+            attend_backward_kernel, spatial, tokens, micro, seq_count, dp_count, plan,
+            (len(front), len(partials), len(outs)), ratio,
+        ),
+        out_shape=tuple(outs + sums_out),
+        in_specs=vmem(len(front)) + hbm(2) + vmem(1) + hbm(2) + hbm(len(partials)),
+        out_specs=specs + vmem(len(partials)),
+        scratch_shapes=own + scratch,
+        compiler_params=pltpu.CompilerParams(
+            collective_id=collective_id, has_side_effects=True, vmem_limit_bytes=VMEM_LIMIT
+        ),
+        name="space_backward" if spatial else "time_backward",
+    )(*front, packed, probs, mixed, w_in, w_out, *blocked)
+    return result[: len(outs)], result[len(outs) :]
+
 
 ACTIONS = 8
 FRAMES = 16
@@ -1227,12 +1347,14 @@
         stream_two, end_grad, live, gain[2], shift[2], up_bias, down_bias, w_hin, w_hout
     )
     layer_out = to_frames(out).reshape(frames_in.shape)
-    one_grad, tin_grad, tout_grad, gain_two, shift_two = attend_backward(
-        False, group, two_grad, stream_one, None, gain[1], shift[1], packed_two, probs_two, mixed_two, w_tin, w_tout
+    (one_grad, tin_grad, tout_grad, gain_two, shift_two), hidden_sums = attend_backward(
+        False, group, places, micro, seq_count, dp_count, [hin_grad, hout_grad], 0.5, 2,
+        two_grad, stream_one, None, gain[1], shift[1], packed_two, probs_two, mixed_two, w_tin, w_tout,
     )
-    one_grad = to_frames(one_grad)
-    in_grad, sin_grad, sout_grad, gain_one, shift_one, sums = attend_backward(
-        True, spatial, one_grad, frames_flat, row_pair, gain[0], shift[0], packed_one, probs_one, mixed_one, w_sin, w_sout
+    one_grad = one_grad.reshape(tokens, width)
+    (in_grad, sin_grad, sout_grad, gain_one, shift_one, sums), time_sums = attend_backward(
+        True, spatial, 16, micro, seq_count, dp_count, [tin_grad, tout_grad], 0.5, 3,
+        one_grad, frames_flat, row_pair, gain[0], shift[0], packed_one, probs_one, mixed_one, w_sin, w_sout,
     )
     table_grad = lax.dot_general(onehot, sums, (((0,), (0,)), ((), ())), precision=lax.Precision.HIGHEST)
 
@@ -1243,18 +1365,14 @@
     rows = jnp.concatenate([rows, up_grad.reshape(seq_count, up_rows, cut)], axis=1)
     rows = jnp.pad(rows, ((0, 0), (0, 32 - used), (0, 128 - cut))).astype(low).reshape(1, seq_count * 32, 128)
     rows = jnp.broadcast_to(rows, (dp_count,) + rows.shape[1:])
-    first = reduce_all([hin_grad, hout_grad], seq_count, dp_count, collective_id=2)
-    second = reduce_all([sin_grad, sout_grad, tin_grad, tout_grad, rows], seq_count, dp_count, collective_id=3)
-    small = second[4][:, :cut]
+    space_sums = reduce_all([sin_grad, sout_grad, rows], seq_count, dp_count, collective_id=4)
+    small = space_sums[2][:, :cut]
     return (
         layer_out,
         in_grad.reshape(frames_in.shape),
-        second[0],
-        second[1],
-        second[2],
-        second[3],
-        first[0],
-        first[1],
+        *space_sums[:2],
+        *time_sums,
+        *hidden_sums,
         small[0:3],
         small[3:6],
         small[15:used].reshape(-1),

time: 798 us -> 599 us (0.75)
  Pallas kernels: 686 us -> 515 us
  waiting for transfers between devices: 43.7 us -> 21.9 us
    pallas_call x2 -> x1, Pallas kernels: 360 us -> 57.7 us  [reduce_all(): pl.pallas_call(functools.partial(reduce_kernel, seq_count, dp_count, plan...]
    pallas_call x2, Pallas kernels: 71.8 us -> 201 us  [attend_backward(): pl.pallas_call(functools.partial(attend_backward_kernel, spatial, tokens,...]
    all_to_all x2 -> x1, waiting for transfers between devices: 21.9 us -> 0.01 us  [to_frames(): lax.all_to_all(value, 'seq', split_axis=1, concat_axis=1, tiled=True)]
  transfers between devices with their start and end apart: 4 -> 3, of which waited for: 2 -> 1; matrix products, arithmetic and copies ran while one was open for 2% -> 3% of each run, Pallas kernels for 53% -> 48%
where the time goes in v2:
time: 599 us; the launch traced here: 592 us
  Pallas kernels  515 us (86%)
  local copies, waits for them, and re-layouts  31.8 us (5%)
  waiting for transfers between devices  21.9 us (4%)
  starting transfers between devices  17.3 us (3%)
    pallas_call x2, Pallas kernels, attend_backward(): pl.pallas_call(functools.partial(attend_backward_kernel, spatial, tokens,...  201 us
    pallas_call x1, Pallas kernels, gather_all(): pl.pallas_call(functools.partial(gather_kernel, seq_count, dp_count, plan...  151 us
    pallas_call x1, Pallas kernels, hidden_layer(): pl.pallas_call(hidden_kernel, out_shape=(shape((tokens, width), low), sha...  59.5 us
    pallas_call x1, Pallas kernels, reduce_all(): pl.pallas_call(functools.partial(reduce_kernel, seq_count, dp_count, plan...  57.7 us
    pallas_call x2, Pallas kernels, attend_forward(): pl.pallas_call(functools.partial(attend_forward_kernel, spatial, tokens),...  46.1 us
    all_to_all x2, waiting for transfers between devices, to_places(): lax.all_to_all(value, 'seq', split_axis=2, concat_axis=2, tiled=True)  21.9 us
  transfers between devices with their start and end apart: 3, of which 1 were waited for; matrix products, arithmetic and copies ran while one was open for 3% of the time, Pallas kernels for 48%

profile of v2, /device:TPU:0, one launch (start us, length us, event | category | flops | bytes accessed | tf_op | source)
XLA Modules:
  0.0 592.3 jit_solution(2431352389974102158)
XLA Ops:
  1.4 2.2 concatenate.11
  4.2 150.7 %gather_weights.1 = (bf16[2,4,2,2,64,1536]{5,4,3,2,1,0:T(8,128)(2,1)}, bf16[2,4,2,2,64,512]{5,4,3,2,1,0:T(8,128)(2,1)}, bf16[2,4,2,2,64,1536]{5,4,3,2,1,0:T(8,12...) custom-call(bf16[64,1536]{1,0:T(8,128)(2,1)} %refs_0_.1, ...), custom_call_target="tpu_custom_call" | custom-call | tf_op jit(solution)/shard_map/gather_weights/pallas_call | solution.py:293
  157.5 1.4 fusion.1.refs_1_.refs_2_
  158.9 22.9 %space_forward.1 = (bf16[512,1024]{1,0:T(8,128)(2,1)}, bf16[512,3072]{1,0:T(8,128)(2,1)}, bf16[32,256,256]{2,1,0:T(8,128)(2,1)}, bf16[512,1024]{1,0:T(8,128)(2,1)}) custom-call(bf16[512,1024]{1,0:T(8,128)(2,1)} %bitcast.62, f32[2,1024]{1,0:T(2,128)} %fusion.1.refs_1_.refs_2_, f32[1,1024]{1,0:T(1,128)} %slice.91.refs_2_.refs_3_, ...), custom_call_target="tpu_custom_call" | custom-call | tf_op jit(solution)/shard_map/space_forward/pallas_call | solution.py:585
  181.8 2.5 copy.53
  184.3 3.8 all-to-all-start
  188.1 1.0 copy.55
  189.2 21.9 %all-to-all-done = bf16[2,1,16,16,1024]{4,3,0,1,2:T(8,128)(2,1)S(1)} async-done(((bf16[2,1,16,16,1024]{4,3,0,1,2:T(8,128)(2,1)}), bf16[2,1,16,16,1024]{4,3,0,1,2:T(8,128)(2,1)S(1)}, u32[]{:S(2)}, u32[]{:S(2)}) %all-to-all-start) | async-done | bytes 1048608 | tf_op jit(solution)/shard_map/all_to_all | solution.py:1329
  211.1 7.3 %all-to-all-start.1 = ((bf16[2,1,16,16,1024]{4,3,0,1,2:T(8,128)(2,1)}), bf16[2,1,16,16,1024]{4,3,0,1,2:T(8,128)(2,1)S(1)}, u32[]{:S(2)}, u32[]{:S(2)}) async-start(bf16[2,1,16,16,1024]{4,3,0,1,2:T(8,128)(2,1)} %copy.55), calls=%async_computation.1 | async-start | bytes 2097152 | tf_op jit(solution)/shard_map/all_to_all | solution.py:1329
  224.6 1.0 copy.54
  225.6 23.3 %time_forward.1 = (f32[512,1024]{1,0:T(8,128)}, bf16[512,3072]{1,0:T(8,128)(2,1)}, bf16[32,256,256]{2,1,0:T(8,128)(2,1)}, bf16[512,1024]{1,0:T(8,128)(2,1)}) custom-call(bf16[512,1024]{1,0:T(8,128)(2,1)} %bitcast.50, f32[2,256,256]{2,1,0:T(8,128)} %and_convert_fusion.refs_1_, f32[1,1024]{1,0:T(1,128)} %slice.95.refs_2_, f32[1,1024]{1,0:T(1,128)} %slice.97.refs_3_, ...), custom_call_target="tpu_custom_call" | custom-call | tf_op jit(solution)/shard_map/time_forward/pallas_call | solution.py:585
  248.9 1.1 copy.56
  249.9 59.5 %hidden_layer.1 = (bf16[512,1024]{1,0:T(8,128)(2,1)}, f32[512,1024]{1,0:T(8,128)}, bf16[2,1024,2048]{2,1,0:T(8,128)(2,1)}, bf16[2,4096,512]{2,1,0:T(8,128)(2,1)}...) custom-call(f32[512,1024]{1,0:T(8,128)} %get-tuple-element.60.stream, ...), custom_call_target="tpu_custom_call" | custom-call | tf_op jit(solution)/shard_map/hidden_layer/pallas_call | solution.py:755
  309.4 2.4 copy.59
  311.8 6.1 %all-to-all-start.2 = ((bf16[2,16,1,16,1024]{4,3,0,2,1:T(8,128)(2,1)}), bf16[2,16,1,16,1024]{4,3,0,2,1:T(8,128)(2,1)S(1)}, u32[]{:S(2)}, u32[]{:S(2)}) async-start(bf16[2,16,1,16,1024]{4,3,0,2,1:T(8,128)(2,1)} %copy.59), calls=%async_computation.2 | async-start | bytes 2097152 | tf_op jit(solution)/shard_map/all_to_all | solution.py:1334
  317.9 122.7 %time_backward.1 = (bf16[32,16,1024]{2,1,0:T(8,128)(2,1)}, bf16[2,1024,1536]{2,1,0:T(8,128)(2,1)}, bf16[2,1024,512]{2,1,0:T(8,128)(2,1)}, f32[1,1024]{1,0:T(1,12...) custom-call(f32[512,1024]{1,0:T(8,128)} %get-tuple-element.64.refs_0_, bf16[512,1024]{1,0:T(8,128)(2,1)} %bitcast.51, ...), custom_call_target="tpu_custom_call" | custom-call | tf_op jit(solution)/shard_map/time_backward/pallas_call | solution.py:1248
  440.7 77.9 %space_backward.1 = (bf16[32,16,1024]{2,1,0:T(8,128)(2,1)}, bf16[2,1024,1536]{2,1,0:T(8,128)(2,1)}, bf16[2,1024,512]{2,1,0:T(8,128)(2,1)}, f32[1,1024]{1,0:T(1,1...) custom-call(bf16[512,1024]{1,0:T(8,128)(2,1)} %bitcast.68, ...), custom_call_target="tpu_custom_call" | custom-call | tf_op jit(solution)/shard_map/space_backward/pallas_call | solution.py:1248
  520.2 1.0 convolution_convert_fusion
  522.4 57.7 %reduce_gradients.1 = (f32[64,1536]{1,0:T(8,128)}, f32[64,512]{1,0:T(8,128)}, f32[32,128]{1,0:T(8,128)}) custom-call(bf16[2,4,2,2,64,1536]{5,4,3,2,1,0:T(8,128)(2,1)} %bitcast.60, bf16[2,4,2,2,64,512]{5,4,3,2,1,0:T(8,128)(2,1)} %bitcast.66, bf16[2,4,2,2,32,128]{5,4,3,2,1,0:T(8,128)(2,1)} %broadcast_in_dim.8.refs_2_), custom_call_target="tpu_custom_call" | custom-call | tf_op jit(solution)/shard_map/reduce_gradients/pallas_call | solution.py:1105
  580.9 1.3 slice.109
  582.8 1.2 slice_bitcast_fusion.1
  584.0 1.3 fusion.5
  585.4 1.0 copy.60
  586.5 1.0 copy.80
  (85 shorter events, 18.5 us)
Async XLA Ops:
  181.8 6.4 %copy-start = (bf16[2,1,256,1024]{3,2,1,0:T(8,128)(2,1)S(1)}, bf16[2,1,256,1024]{3,2,1,0:T(8,128)(2,1)}, u32[]{:S(2)}) copy-start(bf16[2,1,256,1024]{3,2,1,0:T(8,128)(2,1)} %param.16) | copy-start | bytes 3145732
  181.8 36.6 %copy-start.14 = (s32[2,1]{0,1:T(1,128)S(1)}, s32[2,1]{0,1:T(1,128)}, u32[]{:S(2)}) copy-start(s32[2,1]{0,1:T(1,128)} %param.17) | copy-start | bytes 28
  184.3 26.8 %all-to-all-start = ((bf16[2,1,16,16,1024]{4,3,0,1,2:T(8,128)(2,1)}), bf16[2,1,16,16,1024]{4,3,0,1,2:T(8,128)(2,1)S(1)}, u32[]{:S(2)}, u32[]{:S(2)}) async-start(bf16[2,1,16,16,1024]{4,3,0,1,2:T(8,128)(2,1)} %copy.53), calls=%async_computation | async-start | bytes 2097152 | tf_op jit(solution)/shard_map/all_to_all | solution.py:1329
  211.1 37.8 %all-to-all-start.1 = ((bf16[2,1,16,16,1024]{4,3,0,1,2:T(8,128)(2,1)}), bf16[2,1,16,16,1024]{4,3,0,1,2:T(8,128)(2,1)S(1)}, u32[]{:S(2)}, u32[]{:S(2)}) async-start(bf16[2,1,16,16,1024]{4,3,0,1,2:T(8,128)(2,1)} %copy.55), calls=%async_computation.1 | async-start | bytes 2097152 | tf_op jit(solution)/shard_map/all_to_all | solution.py:1329
  311.8 273.6 %all-to-all-start.2 = ((bf16[2,16,1,16,1024]{4,3,0,2,1:T(8,128)(2,1)}), bf16[2,16,1,16,1024]{4,3,0,2,1:T(8,128)(2,1)S(1)}, u32[]{:S(2)}, u32[]{:S(2)}) async-start(bf16[2,16,1,16,1024]{4,3,0,2,1:T(8,128)(2,1)} %copy.59), calls=%async_computation.2 | async-start | bytes 2097152 | tf_op jit(solution)/shard_map/all_to_all | solution.py:1334
  440.6 79.4 %copy-start.13 = (f32[1,1024]{1,0:T(1,128)S(1)}, f32[1,1024]{1,0:T(1,128)}, u32[]{:S(2)}) copy-start(f32[1,1024]{1,0:T(1,128)} %get-tuple-element.80) | copy-start | bytes 12292
  440.6 79.4 %copy-start.12 = (f32[1,1024]{1,0:T(1,128)S(1)}, f32[1,1024]{1,0:T(1,128)}, u32[]{:S(2)}) copy-start(f32[1,1024]{1,0:T(1,128)} %get-tuple-element.83) | copy-start | bytes 12292
  440.6 79.4 %copy-start.11 = (f32[1,1024]{1,0:T(1,128)S(1)}, f32[1,1024]{1,0:T(1,128)}, u32[]{:S(2)}) copy-start(f32[1,1024]{1,0:T(1,128)} %get-tuple-element.81) | copy-start | bytes 12292
  440.6 79.4 %copy-start.10 = (f32[1,1024]{1,0:T(1,128)S(1)}, f32[1,1024]{1,0:T(1,128)}, u32[]{:S(2)}) copy-start(f32[1,1024]{1,0:T(1,128)} %get-tuple-element.84) | copy-start | bytes 12292
  440.6 79.4 %copy-start.9 = (f32[1,1024]{1,0:T(1,128)S(1)}, f32[1,1024]{1,0:T(1,128)}, u32[]{:S(2)}) copy-start(f32[1,1024]{1,0:T(1,128)} %get-tuple-element.86) | copy-start | bytes 12292
  440.6 79.4 %copy-start.8 = (f32[1,4096]{1,0:T(1,128)S(1)}, f32[1,4096]{1,0:T(1,128)}, u32[]{:S(2)}) copy-start(f32[1,4096]{1,0:T(1,128)} %get-tuple-element.87) | copy-start | bytes 49156
  440.7 79.6 %copy-start.15 = (s32[2,1]{0,1:T(1,128)S(1)}, s32[2,1]{0,1:T(1,128)}, u32[]{:S(2)}) copy-start(s32[2,1]{0,1:T(1,128)} %param.18) | copy-start | bytes 28
  522.4 64.1 %copy-start.1 = (bf16[32,16,1024]{2,1,0:T(8,128)(2,1)S(1)}, bf16[32,16,1024]{2,1,0:T(8,128)(2,1)}, u32[]{:S(2)}) copy-start(bf16[32,16,1024]{2,1,0:T(8,128)(2,1)} %get-tuple-element.76) | copy-start | bytes 3145732
  580.1 8.8 %copy-start.4 = (f32[64,1536]{1,0:T(8,128)S(1)}, f32[64,1536]{1,0:T(8,128)}, u32[]{:S(2)}) copy-start(f32[64,1536]{1,0:T(8,128)} %get-tuple-element.177) | copy-start | bytes 1179652
  580.1 10.2 %copy-start.3 = (f32[64,2048]{1,0:T(8,128)S(1)}, f32[64,2048]{1,0:T(8,128)}, u32[]{:S(2)}) copy-start(f32[64,2048]{1,0:T(8,128)} %get-tuple-element.179) | copy-start | bytes 1572868
  580.1 10.9 %copy-start.2 = (f32[256,512]{1,0:T(8,128)S(1)}, f32[256,512]{1,0:T(8,128)}, u32[]{:S(2)}) copy-start(f32[256,512]{1,0:T(8,128)} %get-tuple-element.180) | copy-start | bytes 1572868
  585.4 2.0 copy-start.5
  585.4 2.8 copy-start.7
  585.4 4.2 copy-start.6

commit v3 on v2

--- a/solution.py
+++ b/solution.py
@@ -247,58 +247,43 @@
                 self.to_sibling(second, third)().wait_send()
 
 
-ORDERS = (("x", "z", "y"), ("y", "z", "x"))
-ORDERS_LOW = (("z", "x", "y"), ("z", "y", "x"))
-
-
-def piece_plan(weights):
+def split_plan(heights, parts_of, orders_of):
     plan = []
-    for index in range(weights):
-        orders = ORDERS if index % 2 == 0 else ORDERS_LOW
-        for half in range(2):
-            plan.append((index, half, orders[half]))
+    for index, height in enumerate(heights):
+        parts = min(parts_of, height // 16)
+        rows = height // parts
+        for part in range(parts):
+            plan.append((index, part * rows, rows, orders_of(index)[part]))
     return plan
 
 
-def gather_kernel(seq_count, dp_count, plan, skew, count, *refs):
-    shards, wholes, sems = refs[:count], refs[count : 2 * count], refs[2 * count :]
-    place = Place(seq_count, dp_count)
-    entry_barrier(place)
+def gather_orders(index):
+    if index % 2 == 0:
+        return (("x", "z", "y"), ("y", "z", "x"))
+    return (("z", "x", "y"), ("z", "y", "x"))
+
+
+PER_GATHER = 5
+
+
+def gather_plan(shards, seq_count, dp_count, parts=2):
+    size = {"z": 4, "x": seq_count // 8, "y": dp_count}
+    plan = split_plan([s.shape[0] for s in shards], parts, gather_orders)
+    scratch = []
+    for _, _, _, order in plan:
+        scratch += list(Gather.sem_shapes([size[a] for a in order]))
+    outs = [jax.ShapeDtypeStruct((dp_count, 4, size["x"], 2) + s.shape, s.dtype) for s in shards]
+    return plan, outs, scratch
+
+
+def gather_pieces(place, plan, shards, wholes, scratch):
     pieces = []
-    for number, (index, half, order) in enumerate(plan):
-        rows = shards[index].shape[0] // 2
+    for number, (index, first, rows, order) in enumerate(plan):
         pieces.append(
-            Gather(place, order, shards[index], wholes[index], pl.ds(half * rows, rows),
-                   sems[5 * number : 5 * number + 5])
+            Gather(place, order, shards[index], wholes[index], pl.ds(first, rows),
+                   scratch[PER_GATHER * number : PER_GATHER * number + PER_GATHER])
         )
-    last = max(p.ticks + i * skew for i, p in enumerate(pieces))
-    for now in range(last + 1):
-        for i, piece in enumerate(pieces):
-            if 0 <= now - i * skew <= piece.ticks:
-                piece.tick(now - i * skew)
-    for piece in pieces:
-        piece.finish_recv()
-        piece.finish_send()
-
-
-def gather_all(shards, seq_count, dp_count, skew=1, collective_id=0):
-    plan = piece_plan(len(shards))
-    size = {"z": 4, "x": seq_count // 8, "y": dp_count}
-    scratch = []
-    for index, half, order in plan:
-        scratch += list(Gather.sem_shapes([size[a] for a in order]))
-    out_shape = [
-        jax.ShapeDtypeStruct((dp_count, 4, size["x"], 2) + s.shape, s.dtype) for s in shards
-    ]
-    return pl.pallas_call(
-        functools.partial(gather_kernel, seq_count, dp_count, plan, skew, len(shards)),
-        out_shape=out_shape,
-        in_specs=[pl.BlockSpec(memory_space=pltpu.HBM)] * len(shards),
-        out_specs=[pl.BlockSpec(memory_space=pltpu.HBM)] * len(shards),
-        scratch_shapes=scratch,
-        compiler_params=pltpu.CompilerParams(collective_id=collective_id, has_side_effects=True),
-        name="gather_weights",
-    )(*shards)
+    return pieces
 
 D_EPS = 1e-05
 NEG = -1e30
@@ -308,7 +293,7 @@
 NT = (((1,), (1,)), ((), ()))
 TN = (((0,), (0,)), ((), ()))
 ROWS = 32
-VMEM_LIMIT = 60 * 1024 * 1024
+VMEM_LIMIT = 63 * 1024 * 1024
 
 
 def dot(left, right, dims=(((1,), (0,)), ((), ()))):
@@ -417,21 +402,26 @@
 
 
 def outer(rows, grad, out, stage, sems, units=1):
-    parts, depth, size = out.shape
-    tile = stage.shape[2]
+    parts, _, across, _, size_r, size = out.shape
+    chips = stage.shape[2]
+    tile = chips * 2 * size_r
 
     def leave(index, slot):
-        return pltpu.make_async_copy(stage.at[slot], out.at[:, at_rows(index, tile), :], sems.at[slot])
+        first = index * chips
+        return pltpu.make_async_copy(
+            stage.at[slot], out.at[:, first // across, pl.ds(lax.rem(first, across), chips)], sems.at[slot]
+        )
 
     def step(index):
         slot = lax.rem(index, 2)
         pl.when(index >= 2)(lambda: leave(index - 2, slot).wait())
         left = rows[:, at_rows(index, tile)]
         for part in range(parts):
-            stage[slot, part] = dot(left, grad[:, part * size : (part + 1) * size], TN).astype(out.dtype)
+            value = dot(left, grad[:, part * size : (part + 1) * size], TN)
+            stage[slot, part] = value.reshape(chips, 2, size_r, size).astype(out.dtype)
         leave(index, slot).start()
 
-    count = depth // tile
+    count = rows.shape[1] // tile
     yield from chunks(count, step, units)
     leave(count - 2, (count - 2) % 2).wait()
     leave(count - 1, (count - 1) % 2).wait()
@@ -537,37 +527,23 @@
     return read
 
 
-def attend_forward_kernel(spatial, tokens, *refs):
-    if spatial:
-        stream, row_pair, gain, shift, w_in, w_out, out, packed, probs, mixed, *rest = refs
-        allowed = None
-        read = spatial_reader(stream, row_pair, tokens)
-    else:
-        stream, allowed, gain, shift, w_in, w_out, out, packed, probs, mixed, *rest = refs
-        read = lambda rows: stream[rows, :].astype(jnp.float32)
-    normed, v_in, v_out, sems = rest
-    first = Fetch(w_in, v_in, sems.at[0]).start()
-    second = Fetch(w_out, v_out, sems.at[1]).start()
+def attend_forward_work(read, base, allowed, gain, shift, v_in, v_out, ready_in, ready_out, put,
+                        packed, probs, mixed, normed, tokens):
     norm_forward(read, gain, shift, normed)
-    first.wait()
+    ready_in()
+    yield
 
     def emit(columns, value):
         packed[:, columns] = value.astype(jnp.bfloat16)
 
-    drain(project(normed, v_in, emit))
-    drain(attention_forward(packed, allowed, probs, mixed, tokens))
-    second.wait()
+    yield from project(normed, v_in, emit, units=3)
+    yield from attention_forward(packed, allowed, probs, mixed, tokens, units=8)
+    ready_out()
 
     def emit_out(columns, value):
-        if spatial:
-            for micro in range(stream.shape[0] // tokens):
-                rows = slice(micro * tokens, (micro + 1) * tokens)
-                base = stream[rows, columns].astype(jnp.float32) + row_pair[micro : micro + 1, columns]
-                out[rows, columns] = (base + value[rows]).astype(out.dtype)
-        else:
-            out[:, columns] = (stream[:, columns].astype(jnp.float32) + value).astype(out.dtype)
-
-    drain(project(mixed, v_out, emit_out))
+        put(columns, base(columns) + value)
+
+    yield from project(mixed, v_out, emit_out, units=2)
 
 
 def vmem(count):
@@ -578,34 +554,9 @@
     return [pl.BlockSpec(memory_space=pltpu.HBM)] * count
 
 
-def attend_forward(spatial, tokens, stream, extra, gain, shift, w_in, w_out):
-    total, width = stream.shape
-    heads = total // tokens * HEADS
-    low = jnp.bfloat16
-    return pl.pallas_call(
-        functools.partial(attend_forward_kernel, spatial, tokens),
-        out_shape=(
-            jax.ShapeDtypeStruct((total, width), low if spatial else jnp.float32),
-            jax.ShapeDtypeStruct((total, 3 * width), low),
-            jax.ShapeDtypeStruct((heads, tokens, tokens), low),
-            jax.ShapeDtypeStruct((total, width), low),
-        ),
-        in_specs=vmem(4) + hbm(2),
-        out_specs=vmem(4),
-        scratch_shapes=[
-            pltpu.VMEM((total, width), low),
-            pltpu.VMEM(w_in.shape, low),
-            pltpu.VMEM(w_out.shape, low),
-            pltpu.SemaphoreType.DMA((2,)),
-        ],
-        compiler_params=pltpu.CompilerParams(vmem_limit_bytes=VMEM_LIMIT),
-        name="space_forward" if spatial else "time_forward",
-    )(stream, extra, gain, shift, w_in, w_out)
-
-
 def attend_backward_work(spatial, tokens, up, stream, extra, gain, shift, packed_h, probs_h, mixed, w_in_h, w_out_h,
                          down, w_in_grad, w_out_grad, gain_out, shift_out, sums,
-                         normed, up_low, mixed_grad, packed_grad, normed_grad, packed, probs, w_in, w_out,
+                         up_low, mixed_grad, packed_grad, normed_grad, packed, probs, w_in, w_out,
                          in_stage, out_stage, sems):
     read = spatial_reader(stream, extra, tokens) if spatial else (lambda rows: stream[rows, :].astype(jnp.float32))
     fetches = [
@@ -620,15 +571,17 @@
         up_low[rows, :] = up[rows, :].astype(jnp.bfloat16)
 
     loop(up.shape[0] // ROWS, lower)
+    yield
+    fetches[0].wait()
+
+    def emit_mixed(columns, value):
+        mixed_grad[:, columns] = value.astype(jnp.bfloat16)
+
+    yield from project_back(up_low, w_out, emit_mixed, units=2)
+    yield from outer(mixed, up_low, w_out_grad, out_stage, sems.at[pl.ds(4, 2)], units=2)
+    normed = up_low
     norm_forward(read, gain, shift, normed)
     yield
-    fetches[0].wait()
-
-    def emit_mixed(columns, value):
-        mixed_grad[:, columns] = value.astype(jnp.bfloat16)
-
-    yield from project_back(up_low, w_out, emit_mixed, units=2)
-    yield from outer(mixed, up_low, w_out_grad, out_stage, sems.at[pl.ds(4, 2)], units=2)
     fetches[1].wait()
     fetches[2].wait()
     yield from attention_backward(packed, probs, mixed_grad, packed_grad, tokens, units=8)
@@ -665,14 +618,18 @@
 END = object()
 
 
-def weave(work, events, ratio):
-    due = 0.0
-    for event in events:
-        event()
-        due += ratio
-        while due >= 1:
-            due -= 1
-            next(work, END)
+def weave(work, ticks, units, last=()):
+    held = -1
+    for now, events in enumerate(ticks):
+        for event in events:
+            event()
+        for _ in range(units[min(now, len(units) - 1)]):
+            if held > now:
+                break
+            step = next(work, END)
+            held = -1 if step is END or step is None else last[step]
+            if held <= now:
+                held = -1
     drain(work)
 
 
@@ -688,24 +645,23 @@
     return value * half, slope
 
 
-def hidden_kernel(stream, cotangent, live, gain, shift, up_bias, down_bias, w_up_h, w_down_h,
-                  out, down, up_grad_h, down_grad_h, gain_out, shift_out, up_bias_out, down_bias_out,
-                  normed, end_low, active, slope, expand_low, normed_grad, w_up, w_down, up_stage, down_stage, sems):
+def hidden_kernel(micro, seq_count, dp_count, stream, live, gain, shift, up_bias, down_bias, cotangent_h, w_up_h, w_down_h,
+                  layer_out, down, up_grad_h, down_grad_h, gain_out, shift_out, up_bias_out, down_bias_out,
+                  normed, end_low, active, slope, expand_low, normed_grad, w_up, w_down, up_stage, down_stage,
+                  cotangent, out, sems, end_sems, home_sems):
     low = jnp.bfloat16
+    place = Place(seq_count, dp_count)
+    end = Exchange(place, cotangent_h, cotangent, end_sems, micro, seq_count, True)
+    home = Exchange(place, out, layer_out, home_sems, micro, seq_count, False)
+    exchange_barrier(end)
+    end.start()
+    block = out.shape[1]
     first = Fetch(w_up_h, w_up, sems.at[0]).start()
     second = Fetch(w_down_h, w_down, sems.at[1]).start()
     tokens, width = stream.shape
     parts = w_up.shape[0]
     norm_forward(lambda rows: stream[rows, :], gain, shift, normed)
 
-    def lower(index, total):
-        rows = at_rows(index, ROWS)
-        value = cotangent[rows, :].astype(jnp.float32) * live[rows, :]
-        end_low[rows, :] = value.astype(low)
-        return total + fold8(value)
-
-    total = lax.fori_loop(0, tokens // ROWS, lower, jnp.zeros((8, width), jnp.float32))
-    down_bias_out[...] = jnp.sum(total, axis=0, keepdims=True)
     first.wait()
 
     def emit_expand(columns, value):
@@ -717,10 +673,25 @@
     second.wait()
 
     def emit_out(columns, value):
-        end = stream[:, columns] + value + down_bias[:, columns]
-        out[:, columns] = (end * live[...]).astype(out.dtype)
+        ended = stream[:, columns] + value + down_bias[:, columns]
+        out[:, :, columns] = (ended * live[...]).astype(low).reshape(tokens // block, block, -1)
 
     drain(project(active, w_down, emit_out, 256))
+    home.start()
+    end.finish()
+
+    def upstream(rows):
+        part = cotangent[pl.ds(rows.start // block, ROWS // block)].astype(jnp.float32).reshape(ROWS, width)
+        return part * live[rows, :]
+
+    def lower(index, total):
+        rows = at_rows(index, ROWS)
+        value = upstream(rows)
+        end_low[rows, :] = value.astype(low)
+        return total + fold8(value)
+
+    total = lax.fori_loop(0, tokens // ROWS, lower, jnp.zeros((8, width), jnp.float32))
+    down_bias_out[...] = jnp.sum(total, axis=0, keepdims=True)
 
     def emit_active(columns, value):
         grad = value * slope[:, columns].astype(jnp.float32)
@@ -740,32 +711,41 @@
     def write(index, rows, value):
         down[rows, :] = value
 
-    def upstream(rows):
-        return cotangent[rows, :].astype(jnp.float32) * live[rows, :]
-
     norm_backward(lambda rows: stream[rows, :], gain, normed_grad, upstream, write, gain_out, shift_out)
-
-
-def hidden_layer(stream, cotangent, live, gain, shift, up_bias, down_bias, w_up, w_down):
+    home.finish()
+
+
+def blocks_of(weight, seq_count):
+    parts, depth, size = weight.shape
+    return jax.ShapeDtypeStruct((parts, 4, seq_count // 8, 2, depth // seq_count, size), jnp.bfloat16)
+
+
+def stage_of(blocks):
+    chips = max(1, 64 // blocks.shape[4])
+    return pltpu.VMEM((2, blocks.shape[0], chips) + blocks.shape[3:], jnp.bfloat16)
+
+
+def hidden_layer(micro, seq_count, dp_count, stream, live, gain, shift, up_bias, down_bias, cotangent, w_up, w_down):
     tokens, width = stream.shape
     hidden = up_bias.shape[1]
     parts = w_up.shape[0]
     low, full = jnp.bfloat16, jnp.float32
     shape = jax.ShapeDtypeStruct
+    up_blocks, down_blocks = blocks_of(w_up, seq_count), blocks_of(w_down, seq_count)
     return pl.pallas_call(
-        hidden_kernel,
+        functools.partial(hidden_kernel, micro, seq_count, dp_count),
         out_shape=(
-            shape((tokens, width), low),
+            shape(cotangent.shape, low),
             shape((tokens, width), full),
-            shape(w_up.shape, low),
-            shape(w_down.shape, low),
+            up_blocks,
+            down_blocks,
             shape((1, width), full),
             shape((1, width), full),
             shape((1, hidden), full),
             shape((1, width), full),
         ),
-        in_specs=vmem(7) + hbm(2),
-        out_specs=vmem(2) + hbm(2) + vmem(4),
+        in_specs=vmem(6) + hbm(3),
+        out_specs=hbm(1) + vmem(1) + hbm(2) + vmem(4),
         scratch_shapes=[
             pltpu.VMEM((tokens, width), low),
             pltpu.VMEM((tokens, width), low),
@@ -775,13 +755,19 @@
             pltpu.VMEM((tokens, width), full),
             pltpu.VMEM(w_up.shape, low),
             pltpu.VMEM(w_down.shape, low),
-            pltpu.VMEM((2, parts, 256, w_up.shape[2]), low),
-            pltpu.VMEM((2, parts, 256, w_down.shape[2]), low),
+            stage_of(up_blocks),
+            stage_of(down_blocks),
+            pltpu.VMEM(cotangent.shape, low),
+            pltpu.VMEM(cotangent.shape, low),
             pltpu.SemaphoreType.DMA((6,)),
+            pltpu.SemaphoreType.DMA((3,)),
+            pltpu.SemaphoreType.DMA((3,)),
         ],
-        compiler_params=pltpu.CompilerParams(vmem_limit_bytes=VMEM_LIMIT),
+        compiler_params=pltpu.CompilerParams(
+            collective_id=4, has_side_effects=True, vmem_limit_bytes=VMEM_LIMIT
+        ),
         name="hidden_layer",
-    )(stream, cotangent, live, gain, shift, up_bias, down_bias, w_up, w_down)
+    )(stream, live, gain, shift, up_bias, down_bias, cotangent, w_up, w_down)
 
 class Reduce:
     def __init__(self, place, order, partial_sum, rows, out, bufs, sems):
@@ -1033,29 +1019,23 @@
             when(condition, lambda copy=copy: copy().wait_send())
 
 
-def split_plan(heights, parts_of, orders_of):
-    plan = []
-    for index, height in enumerate(heights):
-        parts = min(parts_of, height // 16)
-        rows = height // parts
-        for part in range(parts):
-            plan.append((index, part * rows, rows, orders_of(index)[part]))
-    return plan
-
-
-def piece_events(pieces, offsets, skew):
-    events = []
-    for i, piece in enumerate(pieces):
+def by_time(timed):
+    times = sorted({entry[0] for entry in timed})
+    return [[entry[-1] for entry in timed if entry[0] == time] for time in times]
+
+
+def piece_ticks(pieces, offsets):
+    timed = []
+    for piece in pieces:
         for e in range(piece.ticks + 1):
             own = offsets[piece.order[2]]
             when_at = own[e] if e < len(own) else own[-1] + e - len(own) + 1
-            events.append((when_at + i * skew, i, e))
-    events.sort()
-    return [functools.partial(pieces[i].tick, e) for _, i, e in events]
-
-
-LATE = (0, 1, 6, 7, 8, 9, 10)
-OFFSETS = {"x": LATE, "y": LATE, "z": (0, 1, 2, 3, 4, 5, 6, 7, 8)}
+            timed.append((when_at, functools.partial(piece.tick, e)))
+    return by_time(timed)
+
+
+LATE = (0, 1, 4, 5, 6, 7, 8)
+OFFSETS = {"x": LATE, "y": LATE, "z": (0, 1, 1, 2, 3, 4, 5, 6, 7)}
 PER_PIECE = 9
 
 
@@ -1065,20 +1045,14 @@
     return (("z", "x", "y"), ("z", "y", "x"), first, third)
 
 
-def reduce_plan(partials, seq_count, dp_count, parts=4):
-    sizes = (dp_count, 4, seq_count // 8)
-    blocked, outs, scratch = [], [], []
-    for p in partials:
-        rows = p.shape[1] // seq_count
-        blocked.append(p.reshape(sizes + (2, rows, p.shape[2])))
-        outs.append(jax.ShapeDtypeStruct((rows, p.shape[2]), jnp.float32))
+def reduce_plan(blocked, parts=4):
+    outs = [jax.ShapeDtypeStruct(p.shape[4:], jnp.float32) for p in blocked]
     plan = split_plan([o.shape[0] for o in outs], parts, weight_orders)
+    scratch = []
     for index, first, rows, order in plan:
-        bufs, sems = Reduce.scratch(
-            order, sizes, rows, outs[index].shape[1], partials[index].dtype
-        )
+        bufs, sems = Reduce.scratch(order, blocked[index].shape[:3], rows, outs[index].shape[1], blocked[index].dtype)
         scratch += bufs + sems
-    return plan, blocked, outs, scratch
+    return plan, outs, scratch
 
 
 def reduce_pieces(place, plan, partials, outs, scratch):
@@ -1087,32 +1061,6 @@
         own = scratch[PER_PIECE * number : PER_PIECE * number + PER_PIECE]
         pieces.append(Reduce(place, order, partials[index], pl.ds(first, rows), outs[index], own[:5], own[5:]))
     return pieces
-
-
-def reduce_kernel(seq_count, dp_count, plan, count, *refs):
-    partials, outs, rest = refs[:count], refs[count : 2 * count], refs[2 * count :]
-    place = Place(seq_count, dp_count)
-    entry_barrier(place)
-    pieces = reduce_pieces(place, plan, partials, outs, rest)
-    for event in piece_events(pieces, OFFSETS, 0):
-        event()
-    for piece in pieces:
-        piece.finish_send()
-
-
-def reduce_all(partials, seq_count, dp_count, collective_id):
-    plan, blocked, outs, scratch = reduce_plan(partials, seq_count, dp_count)
-    return pl.pallas_call(
-        functools.partial(reduce_kernel, seq_count, dp_count, plan, len(partials)),
-        out_shape=outs,
-        in_specs=hbm(len(partials)),
-        out_specs=vmem(len(partials)),
-        scratch_shapes=scratch,
-        compiler_params=pltpu.CompilerParams(
-            collective_id=collective_id, has_side_effects=True, vmem_limit_bytes=VMEM_LIMIT
-        ),
-        name="reduce_gradients",
-    )(*blocked)
 
 
 class Exchange:
@@ -1170,67 +1118,164 @@
         pltpu.make_async_copy(few, few, self.sems.at[2]).wait()
 
 
-def attend_backward_kernel(spatial, tokens, micro, seq_count, dp_count, plan, counts, ratio, *refs):
-    fronts, count, outs_count = counts
-    refs = list(refs)
-    take = lambda n: [refs.pop(0) for _ in range(n)]
-    if spatial:
-        up, stream, extra, gain, shift = take(5)
-    else:
-        (up, stream, gain, shift), extra = take(4), None
-    packed_h, probs_h, mixed, w_in_h, w_out_h = take(5)
-    partials = take(count)
-    arrived = None if spatial else take(1)[0]
-    down, w_in_grad, w_out_grad, gain_out, shift_out = take(5) if spatial else [None] + take(4)
-    sums = take(1)[0] if spatial else None
-    outs = take(count)
-    own = take(12)
-    if not spatial:
-        down = take(1)[0]
-        change_sems = take(1)[0]
+def exchange_barrier(change):
+    pl.semaphore_wait(pltpu.get_barrier_semaphore(), change.greet())
+
+class Taker:
+    def __init__(self, refs):
+        self.refs = list(refs)
+
+    def __call__(self, count):
+        taken, self.refs = self.refs[:count], self.refs[count:]
+        return taken
+
+
+def batch_ticks(pieces, batches, stagger):
+    timed = []
+    for piece, batch in zip(pieces, batches):
+        for e in range(piece.ticks + 1):
+            timed.append((e + stagger[batch], batch, functools.partial(piece.tick, e)))
+    timed.sort(key=lambda entry: entry[:2])
+    times = sorted({entry[0] for entry in timed})
+    last = {batch: max(times.index(entry[0]) for entry in timed if entry[1] == batch) for batch in set(batches)}
+    return by_time(timed), last
+
+
+def forward_kernel(tokens, group, micro, seq_count, dp_count, plan, count, tuning, *refs):
+    batches, stagger, units = tuning
+    take = Taker(refs)
+    frames, onehot, allowed = take(3)
+    shards = take(count)
+    wholes = take(count)
+    stream_out, stream_two = take(2)
+    kept_one, kept_two = take(3), take(3)
+    small, table_rows, v_small, source, landed, normed, v_in, v_out, sems, one_sems = take(10)
     place = Place(seq_count, dp_count)
-    change = None if spatial else Exchange(place, down, arrived, change_sems, micro, seq_count, False)
-    entry_barrier(place, change)
-    pieces = reduce_pieces(place, plan, partials, outs, refs)
-    work = attend_backward_work(
-        spatial, tokens, up, stream, extra, gain, shift, packed_h, probs_h, mixed, w_in_h, w_out_h,
-        down, w_in_grad, w_out_grad, gain_out, shift_out, sums, *own
-    )
-
-    def all_work():
-        yield from work
-        if change is not None:
-            change.start()
-            yield
-
-    weave(all_work(), piece_events(pieces, OFFSETS, 0), ratio)
-    if change is not None:
-        change.finish()
+    one = Exchange(place, source, landed, one_sems, micro, seq_count, True)
+    entry_barrier(place, one)
+    pieces = gather_pieces(place, plan, shards, wholes, take.refs)
+    owners = [index for index, _, _, _ in plan]
+    ticks, last = batch_ticks(pieces, [batches[index] for index in owners], stagger)
+    across = seq_count // 8
+    total, width = frames.shape
+    cut = width // seq_count
+    block = source.shape[1]
+    low, full = jnp.bfloat16, jnp.float32
+
+    def arrived(*indices):
+        for piece, owner in zip(pieces, owners):
+            if owner in indices:
+                piece.finish_recv()
+
+    def fetch(index, into, sem):
+        rows = shards[index].shape[0]
+
+        def copy(shard):
+            src = wholes[index].at[:, shard // (2 * across), lax.rem(shard // 2, across), lax.rem(shard, 2)]
+            pltpu.make_async_copy(src, into.at[:, at_rows(shard, rows)], sem).start()
+
+        loop(seq_count, copy)
+        return lambda: pltpu.make_async_copy(into, into, sem).wait()
+
+    def space_read(rows):
+        return frames[rows, :].astype(full) + table_rows[pl.ds(rows.start // tokens, 1), :]
+
+    def space_base(columns):
+        rows = frames[:, columns].astype(full).reshape(total // tokens, tokens, -1)
+        return (rows + table_rows[:, columns][:, None, :]).reshape(total, -1)
+
+    def space_put(columns, value):
+        source[:, :, columns] = value.astype(low).reshape(total // block, block, -1)
+
+    def time_read(rows):
+        return landed[pl.ds(rows.start // block, ROWS // block)].astype(full).reshape(ROWS, width)
+
+    def time_base(columns):
+        return landed[:, :, columns].astype(full).reshape(total, -1)
+
+    def time_put(columns, value):
+        stream_two[:, columns] = value
+
+    def work():
+        yield 0
+        arrived(0, 1, 2)
+        ready_in, ready_out = fetch(1, v_in, sems.at[0]), fetch(2, v_out, sems.at[1])
+        Fetch(wholes[0].at[0], v_small, sems.at[2]).start().wait()
+        small[...] = jnp.zeros_like(small)
+        for shard in range(seq_count):
+            tile = pl.ds(shard * cut // 128 * 128, 128)
+            piece = v_small[shard // (2 * across), shard // 2 % across, shard % 2]
+            small[:, tile] = small[:, tile] + piece.astype(full)
+        rows = onehot[:, 0:1] * small[6:7, :]
+        for action in range(1, ACTIONS):
+            rows = rows + onehot[:, action : action + 1] * small[6 + action : 7 + action, :]
+        table_rows[...] = rows
+        yield
+        yield from attend_forward_work(
+            space_read, space_base, None, small.at[0:1], small.at[3:4], v_in, v_out, ready_in, ready_out,
+            space_put, *kept_one, normed, tokens,
+        )
+        one.start()
+        yield 1
+        arrived(3, 4)
+        ready_in, ready_out = fetch(3, v_in, sems.at[0]), fetch(4, v_out, sems.at[1])
+        yield
+        one.finish()
+        yield
+        yield from attend_forward_work(
+            time_read, time_base, allowed, small.at[1:2], small.at[4:5], v_in, v_out, ready_in, ready_out,
+            time_put, *kept_two, normed, group,
+        )
+
+    weave(work(), ticks, units, last)
+    leave = Fetch(landed, stream_out, sems.at[3]).start()
+    arrived(*range(5, count))
     for piece in pieces:
         piece.finish_send()
-
-
-def attend_backward(spatial, tokens, block, micro, seq_count, dp_count, partials, ratio, collective_id,
-                    up, stream, extra, gain, shift, packed, probs, mixed, w_in, w_out):
-    total, width = stream.shape
+    leave.wait()
+
+
+def forward(frames, onehot, allowed, shards, tokens, group, micro, seq_count, dp_count, block, tuning):
+    total, width = frames.shape
     low, full = jnp.bfloat16, jnp.float32
     shape = jax.ShapeDtypeStruct
-    plan, blocked, sums_out, scratch = reduce_plan(partials, seq_count, dp_count)
-    down = shape((total // block, block, width), low)
-    outs = [
-        down,
-        shape(w_in.shape, low),
-        shape(w_out.shape, low),
-        shape((1, width), full),
-        shape((1, width), full),
+    plan, wholes, scratch = gather_plan(shards, seq_count, dp_count)
+    heads = width // HDIM
+    kept = [
+        [shape((total, 3 * width), low), shape((total // size * heads, size, size), low), shape((total, width), low)]
+        for size in (tokens, group)
     ]
-    specs = (vmem(1) if spatial else hbm(1)) + hbm(2) + vmem(2)
-    if spatial:
-        outs.append(shape((total // tokens, width), full))
-        specs += vmem(1)
-    front = (up, stream) + ((extra,) if spatial else ()) + (gain, shift)
-    own = [
-        pltpu.VMEM((total, width), low),
+    blocks = (total // block, block, width)
+    count = len(shards)
+    result = pl.pallas_call(
+        functools.partial(forward_kernel, tokens, group, micro, seq_count, dp_count, plan, count, tuning),
+        out_shape=tuple(wholes + [shape(blocks, low), shape((total, width), full)] + kept[0] + kept[1]),
+        in_specs=vmem(3) + hbm(count),
+        out_specs=hbm(count + 1) + vmem(7),
+        scratch_shapes=[
+            pltpu.VMEM((32, width), full),
+            pltpu.VMEM((total // tokens, width), full),
+            pltpu.VMEM(wholes[0].shape[1:], low),
+            pltpu.VMEM(blocks, low),
+            pltpu.VMEM(blocks, low),
+            pltpu.VMEM((total, width), low),
+            pltpu.VMEM((dp_count, width, 3 * width // dp_count), low),
+            pltpu.VMEM((dp_count, width, width // dp_count), low),
+            pltpu.SemaphoreType.DMA((4,)),
+            pltpu.SemaphoreType.DMA((3,)),
+        ] + scratch,
+        compiler_params=pltpu.CompilerParams(
+            collective_id=1, has_side_effects=True, vmem_limit_bytes=VMEM_LIMIT
+        ),
+        name="forward",
+    )(frames, onehot, allowed, *shards)
+    wholes, rest = result[:count], result[count:]
+    return wholes, rest[0], rest[1], rest[2:5], rest[5:8]
+
+
+def backward_scratch(total, width, packed, probs, w_in, w_out, in_blocks, out_blocks):
+    low, full = jnp.bfloat16, jnp.float32
+    return [
         pltpu.VMEM((total, width), low),
         pltpu.VMEM((total, width), low),
         pltpu.VMEM((total, 3 * width), low),
@@ -1239,31 +1284,166 @@
         pltpu.VMEM(probs.shape, low),
         pltpu.VMEM(w_in.shape, low),
         pltpu.VMEM(w_out.shape, low),
-        pltpu.VMEM((2, dp_count, 128, w_in.shape[2]), low),
-        pltpu.VMEM((2, dp_count, 128, w_out.shape[2]), low),
+        stage_of(in_blocks),
+        stage_of(out_blocks),
         pltpu.SemaphoreType.DMA((8,)),
     ]
-    if not spatial:
-        own += [pltpu.VMEM(down.shape, low), pltpu.SemaphoreType.DMA((3,))]
-    result = pl.pallas_call(
+
+
+def time_backward_kernel(tokens, micro, seq_count, dp_count, plan, count, ratio, *refs):
+    take = Taker(refs)
+    up, stream, gain, shift, packed_h, probs_h, mixed, w_in_h, w_out_h = take(9)
+    partials = take(count)
+    arrived, w_in_grad, w_out_grad, gain_out, shift_out = take(5)
+    outs = take(count)
+    own = take(11)
+    down, change_sems = take(2)
+    place = Place(seq_count, dp_count)
+    change = Exchange(place, down, arrived, change_sems, micro, seq_count, False)
+    entry_barrier(place, change)
+    pieces = reduce_pieces(place, plan, partials, outs, take.refs)
+
+    def work():
+        yield from attend_backward_work(
+            False, tokens, up, stream, None, gain, shift, packed_h, probs_h, mixed, w_in_h, w_out_h,
+            down, w_in_grad, w_out_grad, gain_out, shift_out, None, *own
+        )
+        change.start()
+
+    weave(work(), piece_ticks(pieces, OFFSETS), ratio)
+    change.finish()
+    for piece in pieces:
+        piece.finish_send()
+
+
+def time_backward(tokens, block, micro, seq_count, dp_count, partials, ratio,
+                  up, stream, gain, shift, packed, probs, mixed, w_in, w_out):
+    total, width = stream.shape
+    low, full = jnp.bfloat16, jnp.float32
+    shape = jax.ShapeDtypeStruct
+    plan, sums_out, scratch = reduce_plan(partials)
+    blocks = (total // block, block, width)
+    in_blocks, out_blocks = blocks_of(w_in, seq_count), blocks_of(w_out, seq_count)
+    outs = [
+        shape(blocks, low), in_blocks, out_blocks, shape((1, width), full), shape((1, width), full)
+    ]
+    got = pl.pallas_call(
+        functools.partial(time_backward_kernel, tokens, micro, seq_count, dp_count, plan, len(partials), ratio),
+        out_shape=tuple(outs + sums_out),
+        in_specs=vmem(4) + hbm(2) + vmem(1) + hbm(2 + len(partials)),
+        out_specs=hbm(3) + vmem(2 + len(partials)),
+        scratch_shapes=backward_scratch(total, width, packed, probs, w_in, w_out, in_blocks, out_blocks)
+        + [pltpu.VMEM(blocks, low), pltpu.SemaphoreType.DMA((3,))]
+        + scratch,
+        compiler_params=pltpu.CompilerParams(
+            collective_id=2, has_side_effects=True, vmem_limit_bytes=VMEM_LIMIT
+        ),
+        name="time_backward",
+    )(up, stream, gain, shift, packed, probs, mixed, w_in, w_out, *partials)
+    return got[:5], got[5:]
+
+
+def space_backward_kernel(tokens, seq_count, dp_count, plans, counts, units, *refs):
+    take = Taker(refs)
+    up, stream, extra, gain, shift, packed_h, probs_h, mixed, w_in_h, w_out_h = take(10)
+    onehot, gain_two, gain_three, shift_two, shift_three, up_bias, down_bias = take(7)
+    partials = take(counts[0])
+    down, w_in_grad, w_out_grad = take(3)
+    outs = take(counts[0])
+    last_outs = take(3)
+    own = take(11)
+    gain_out, shift_out, sums, rows, small_part = take(5)
+    place = Place(seq_count, dp_count)
+    entry_barrier(place)
+    scratch = take(counts[1])
+    pieces = reduce_pieces(place, plans[0], partials, outs, scratch)
+    ends = reduce_pieces(place, plans[1], (w_in_grad, w_out_grad, small_part), last_outs, take.refs)
+    width, hidden = stream.shape[1], up_bias.shape[1]
+    low = jnp.bfloat16
+
+    def small_rows():
+        top = [gain_out, gain_two, gain_three, shift_out, shift_two, shift_three]
+        rows[...] = jnp.zeros_like(rows)
+        for at, row in enumerate(top):
+            rows[at : at + 1, :] = row[...]
+        for action in range(ACTIONS):
+            total = onehot[0:1, action : action + 1] * sums[0:1, :]
+            for frame in range(1, sums.shape[0]):
+                total = total + onehot[frame : frame + 1, action : action + 1] * sums[frame : frame + 1, :]
+            rows[6 + action : 7 + action, :] = total
+        rows[14:15, :] = down_bias[...]
+        across = seq_count // 8
+        lane_row = lax.broadcasted_iota(jnp.int32, (16, 128), 0)
+        for shard in range(seq_count):
+            tile = shard * (width // seq_count) // 128 * 128
+            first = rows[:, tile : tile + 128].astype(low)
+            second = jnp.zeros((16, 128), jnp.float32)
+            each = hidden // seq_count
+            for part in range(each // 128):
+                start = shard * each + part * 128
+                second = jnp.where(lane_row == part, up_bias[:, start : start + 128], second)
+            for part in range(dp_count):
+                at = (part, shard // (2 * across), shard // 2 % across, shard % 2)
+                small_part[at + (slice(0, 16),)] = first
+                small_part[at + (slice(16, 32),)] = second.astype(low)
+
+    def work():
+        yield from attend_backward_work(
+            True, tokens, up, stream, extra, gain, shift, packed_h, probs_h, mixed, w_in_h, w_out_h,
+            down, w_in_grad, w_out_grad, gain_out, shift_out, sums, *own
+        )
+        small_rows()
+        yield
+
+    weave(work(), piece_ticks(pieces, OFFSETS), units)
+    for events in piece_ticks(ends, OFFSETS):
+        for event in events:
+            event()
+    for piece in pieces + ends:
+        piece.finish_send()
+
+
+def space_backward(tokens, seq_count, dp_count, partials, units,
+                   up, stream, extra, gain, shift, packed, probs, mixed, w_in, w_out,
+                   onehot, gain_two, gain_three, shift_two, shift_three, up_bias, down_bias):
+    total, width = stream.shape
+    low, full = jnp.bfloat16, jnp.float32
+    shape = jax.ShapeDtypeStruct
+    in_blocks, out_blocks = blocks_of(w_in, seq_count), blocks_of(w_out, seq_count)
+    small = shape(in_blocks.shape[:4] + (32, 128), low)
+    plan, sums_out, scratch = reduce_plan(partials)
+    end_plan, end_out, end_scratch = reduce_plan([in_blocks, out_blocks, small])
+    outs = [shape((total // 16, 16, width), low), in_blocks, out_blocks]
+    count = len(partials)
+    got = pl.pallas_call(
         functools.partial(
-            attend_backward_kernel, spatial, tokens, micro, seq_count, dp_count, plan,
-            (len(front), len(partials), len(outs)), ratio,
+            space_backward_kernel, tokens, seq_count, dp_count, (plan, end_plan), (count, len(scratch)), units
         ),
-        out_shape=tuple(outs + sums_out),
-        in_specs=vmem(len(front)) + hbm(2) + vmem(1) + hbm(2) + hbm(len(partials)),
-        out_specs=specs + vmem(len(partials)),
-        scratch_shapes=own + scratch,
+        out_shape=tuple(outs + sums_out + end_out),
+        in_specs=vmem(5) + hbm(2) + vmem(1) + hbm(2) + vmem(7) + hbm(count),
+        out_specs=vmem(1) + hbm(2) + vmem(count + 3),
+        scratch_shapes=backward_scratch(total, width, packed, probs, w_in, w_out, in_blocks, out_blocks)
+        + [
+            pltpu.VMEM((1, width), full),
+            pltpu.VMEM((1, width), full),
+            pltpu.VMEM((total // tokens, width), full),
+            pltpu.VMEM((16, width), full),
+            pltpu.VMEM(small.shape, low),
+        ]
+        + scratch + end_scratch,
         compiler_params=pltpu.CompilerParams(
-            collective_id=collective_id, has_side_effects=True, vmem_limit_bytes=VMEM_LIMIT
+            collective_id=3, has_side_effects=True, vmem_limit_bytes=VMEM_LIMIT
         ),
-        name="space_backward" if spatial else "time_backward",
-    )(*front, packed, probs, mixed, w_in, w_out, *blocked)
-    return result[: len(outs)], result[len(outs) :]
-
+        name="space_backward",
+    )(up, stream, extra, gain, shift, packed, probs, mixed, w_in, w_out,
+      onehot, gain_two, gain_three, shift_two, shift_three, up_bias, down_bias, *partials)
+    return got[0], got[3 : 3 + count], got[3 + count :]
 
 ACTIONS = 8
 FRAMES = 16
+FORWARD = ((0, 0, 0, 1, 1, 2, 2), (0, 3, 6), (6,))
+TIME_UNITS = (7, 6, 6, 4)
+SPACE_UNITS = (6, 4, 4, 4, 4, 2)
 
 
 def body(
@@ -1297,19 +1477,10 @@
         [norm_gains, norm_shifts, action_table, bias_down[None], bias_up.reshape(up_rows, cut)], axis=0
     )
     used = small.shape[0]
-    small = jnp.pad(small, ((0, 32 - used), (0, 128 - cut)))
-    shards = [spatial_in, spatial_out, temporal_in, temporal_out, hidden_in, hidden_out, small]
-    wholes = gather_all(shards, seq_count, dp_count, skew=0, collective_id=1)
-    weights = [
-        whole.reshape(dp_count, shard.shape[0] * seq_count, shard.shape[1])
-        for whole, shard in zip(wholes[:6], shards)
-    ]
-    w_sin, w_sout, w_tin, w_tout, w_hin, w_hout = weights
-    small = wholes[6][0].reshape(seq_count, 32, 128)[:, :, :cut].astype(full)
-    rows = small[:, : used - up_rows].transpose(1, 0, 2).reshape(used - up_rows, width)
-    gain, shift = [rows[i : i + 1] for i in range(3)], [rows[i : i + 1] for i in range(3, 6)]
-    table, down_bias = rows[6:14], rows[14:15]
-    up_bias = small[:, used - up_rows : used].reshape(1, -1)
+    small = jnp.pad(small, ((0, 32 - used), (0, 0)))
+    lane = lax.rem(lax.axis_index("seq") * cut, 128)
+    small = lax.dynamic_update_slice(jnp.zeros((32, 128), low), small, (0, lane))
+    shards = [small, spatial_in, spatial_out, temporal_in, temporal_out, hidden_in, hidden_out]
 
     at = jnp.arange(group, dtype=jnp.int32)
     frame, place = at // places, at % places
@@ -1322,60 +1493,48 @@
     allowed = allowed.astype(full)
     live = alive.astype(full).reshape(tokens, 1)
     onehot = (actions.reshape(-1)[:, None] == jnp.arange(ACTIONS)[None, :]).astype(full)
+
+    frames_flat = frames_in.reshape(tokens, width)
+    blocks = (tokens // places, places, width)
+    wholes, stream_one, stream_two, kept_one, kept_two = forward(
+        frames_flat, onehot, allowed, shards, spatial, group, micro, seq_count, dp_count,
+        places, FORWARD,
+    )
+    w_sin, w_sout, w_tin, w_tout, w_hin, w_hout = [
+        whole.reshape(dp_count, shard.shape[0] * seq_count, shard.shape[1])
+        for whole, shard in zip(wholes[1:], shards[1:])
+    ]
+    small = wholes[0][0].reshape(seq_count // (128 // cut), 128 // cut, 32, 128).astype(full).sum(axis=1)
+    rows = small.transpose(1, 0, 2).reshape(32, width)
+    gain, shift = [rows[i : i + 1] for i in range(3)], [rows[i : i + 1] for i in range(3, 6)]
+    table, down_bias = rows[6:14], rows[14:15]
+    up_bias = rows[used - up_rows : used].reshape(up_rows, seq_count, cut).transpose(1, 0, 2).reshape(1, -1)
     row_pair = jnp.dot(onehot, table, precision=lax.Precision.HIGHEST)
-
-    def to_places(value):
-        value = value.reshape(micro, frame_count, seq_count, places, width)
-        value = lax.all_to_all(value, "seq", split_axis=2, concat_axis=2, tiled=True)
-        return value.transpose(0, 2, 1, 3, 4).reshape(tokens, width)
-
-    def to_frames(value):
-        value = value.reshape(micro, seq_count, frame_count, places, width)
-        value = lax.all_to_all(value, "seq", split_axis=1, concat_axis=1, tiled=True)
-        return value.transpose(0, 2, 1, 3, 4).reshape(tokens, width)
-
-    frames_flat = frames_in.reshape(tokens, width)
-    end_grad = to_places(cotangent)
-    stream_one, packed_one, probs_one, mixed_one = attend_forward(
-        True, spatial, frames_flat, row_pair, gain[0], shift[0], w_sin, w_sout
+    stream_one = stream_one.reshape(tokens, width)
+    layer_out, two_grad, hin_grad, hout_grad, gain_three, shift_three, up_grad, down_grad = hidden_layer(
+        micro, seq_count, dp_count, stream_two, live, gain[2], shift[2], up_bias, down_bias, cotangent.reshape(blocks),
+        w_hin, w_hout,
     )
-    stream_one = to_places(stream_one)
-    stream_two, packed_two, probs_two, mixed_two = attend_forward(
-        False, group, stream_one, allowed, gain[1], shift[1], w_tin, w_tout
+    (one_grad, tin_grad, tout_grad, gain_two, shift_two), hidden_sums = time_backward(
+        group, places, micro, seq_count, dp_count, [hin_grad, hout_grad], TIME_UNITS,
+        two_grad, stream_one, gain[1], shift[1], *kept_two, w_tin, w_tout,
     )
-    out, two_grad, hin_grad, hout_grad, gain_three, shift_three, up_grad, down_grad = hidden_layer(
-        stream_two, end_grad, live, gain[2], shift[2], up_bias, down_bias, w_hin, w_hout
+    in_grad, time_sums, (*space_sums, small) = space_backward(
+        spatial, seq_count, dp_count, [tin_grad, tout_grad], SPACE_UNITS,
+        one_grad.reshape(tokens, width), frames_flat, row_pair, gain[0], shift[0], *kept_one, w_sin, w_sout,
+        onehot, gain_two, gain_three, shift_two, shift_three, up_grad, down_grad,
     )
-    layer_out = to_frames(out).reshape(frames_in.shape)
-    (one_grad, tin_grad, tout_grad, gain_two, shift_two), hidden_sums = attend_backward(
-        False, group, places, micro, seq_count, dp_count, [hin_grad, hout_grad], 0.5, 2,
-        two_grad, stream_one, None, gain[1], shift[1], packed_two, probs_two, mixed_two, w_tin, w_tout,
-    )
-    one_grad = one_grad.reshape(tokens, width)
-    (in_grad, sin_grad, sout_grad, gain_one, shift_one, sums), time_sums = attend_backward(
-        True, spatial, 16, micro, seq_count, dp_count, [tin_grad, tout_grad], 0.5, 3,
-        one_grad, frames_flat, row_pair, gain[0], shift[0], packed_one, probs_one, mixed_one, w_sin, w_sout,
-    )
-    table_grad = lax.dot_general(onehot, sums, (((0,), (0,)), ((), ())), precision=lax.Precision.HIGHEST)
-
-    rows = jnp.concatenate(
-        [gain_one, gain_two, gain_three, shift_one, shift_two, shift_three, table_grad, down_grad], axis=0
-    )
-    rows = rows.reshape(used - up_rows, seq_count, cut).transpose(1, 0, 2)
-    rows = jnp.concatenate([rows, up_grad.reshape(seq_count, up_rows, cut)], axis=1)
-    rows = jnp.pad(rows, ((0, 0), (0, 32 - used), (0, 128 - cut))).astype(low).reshape(1, seq_count * 32, 128)
-    rows = jnp.broadcast_to(rows, (dp_count,) + rows.shape[1:])
-    space_sums = reduce_all([sin_grad, sout_grad, rows], seq_count, dp_count, collective_id=4)
-    small = space_sums[2][:, :cut]
+    up_sum = small[16 : 16 + bias_up.shape[0] // 128].reshape(-1)
+    small = lax.dynamic_slice(small, (0, lane), (16, cut))
     return (
-        layer_out,
+        layer_out.reshape(frames_in.shape),
         in_grad.reshape(frames_in.shape),
-        *space_sums[:2],
+        *space_sums,
         *time_sums,
         *hidden_sums,
         small[0:3],
         small[3:6],
-        small[15:used].reshape(-1),
+        up_sum,
         small[14],
         small[6:14],
     )

time: 599 us -> 519 us (0.87)
  Pallas kernels: 515 us -> 489 us
  waiting for transfers between devices: 21.9 us -> 0 us
  starting transfers between devices: 17.3 us -> 0 us
  local copies, waits for them, and re-layouts: 31.8 us -> 19.9 us
    pallas_call x7 -> x4, Pallas kernels: 515 us -> 489 us  [the longest x1 188 us: forward(): pl.pallas_call(functools.partial(forward_kernel, tokens, group, micro, se...]
    all_to_all x3 -> x0, waiting for transfers between devices: 21.9 us -> none  [the longest x2 21.9 us: to_places(): lax.all_to_all(value, 'seq', split_axis=2, concat_axis=2, tiled=True)]
    all_to_all x3 -> x0, starting transfers between devices: 17.3 us -> none  [the longest x2 11.2 us: to_places(): lax.all_to_all(value, 'seq', split_axis=2, concat_axis=2, tiled=True)]
  transfers between devices with their start and end apart: 3 -> 0, of which waited for: 1 -> 0; matrix products, arithmetic and copies ran while one was open for 3% -> 0% of each run, Pallas kernels for 48% -> 0%
where the time goes in v3:
time: 519 us; the launch traced here: 515 us
  Pallas kernels  489 us (94%)
  local copies, waits for them, and re-layouts  19.9 us (4%)
    pallas_call x1, Pallas kernels, forward(): pl.pallas_call(functools.partial(forward_kernel, tokens, group, micro, se...  188 us
    pallas_call x1, Pallas kernels, time_backward(): pl.pallas_call(functools.partial(time_backward_kernel, tokens, micro, seq...  126 us
    pallas_call x1, Pallas kernels, space_backward(): pl.pallas_call(functools.partial(space_backward_kernel, tokens, seq_count...  115 us
    pallas_call x1, Pallas kernels, hidden_layer(): pl.pallas_call(functools.partial(hidden_kernel, micro, seq_count, dp_coun...  59.3 us

profile of v3, /device:TPU:0, one launch (start us, length us, event | category | flops | bytes accessed | tf_op | source)
XLA Modules:
  0.0 515.2 jit_solution(13194960590194093683)
XLA Ops:
  0.7 1.3 fusion.4.refs_1_.refs_10_
  2.0 0.7 reshape.373
  2.8 0.7 convert_bitcast_fusion
  3.5 2.2 concatenate.3
  6.1 0.9 copy.41
  7.0 0.9 and_convert_fusion.refs_2_
  7.9 188.4 %forward.1 = (bf16[2,4,2,2,32,128]{5,4,3,2,1,0:T(8,128)(2,1)}, bf16[2,4,2,2,64,1536]{5,4,3,2,1,0:T(8,128)(2,1)}, bf16[2,4,2,2,64,512]{5,4,3,2,1,0:T(8,128)(2,1)}...) custom-call(bf16[512,1024]{1,0:T(8,128)(2,1)} %bitcast.51, ...), custom_call_target="tpu_custom_call" | custom-call | tf_op jit(solution)/shard_map/forward/pallas_call | solution.py:1250
  196.3 0.9 convert_reduce_fusion
  197.5 0.7 reshape.375.up_bias
  198.8 0.8 fusion.refs_2_
  199.6 59.3 %hidden_layer.1 = (bf16[32,16,1024]{2,1,0:T(8,128)(2,1)}, f32[512,1024]{1,0:T(8,128)}, bf16[2,4,2,2,64,2048]{5,4,3,2,1,0:T(8,128)(2,1)}, bf16[2,4,2,2,256,512]{5...) custom-call(f32[512,1024]{1,0:T(8,128)} %get-tuple-element.49.stream, ...), custom_call_target="tpu_custom_call" | custom-call | tf_op jit(solution)/shard_map/hidden_layer/pallas_call | solution.py:735
  258.9 126.3 %time_backward.1 = (bf16[32,16,1024]{2,1,0:T(8,128)(2,1)}, bf16[2,4,2,2,64,1536]{5,4,3,2,1,0:T(8,128)(2,1)}, bf16[2,4,2,2,64,512]{5,4,3,2,1,0:T(8,128)(2,1)}, f3...) custom-call(f32[512,1024]{1,0:T(8,128)} %get-tuple-element.54.refs_0_, ...), custom_call_target="tpu_custom_call" | custom-call | tf_op jit(solution)/shard_map/time_backward/pallas_call | solution.py:1330
  385.1 115.5 %space_backward.1 = (bf16[32,16,1024]{2,1,0:T(8,128)(2,1)}, bf16[2,4,2,2,64,1536]{5,4,3,2,1,0:T(8,128)(2,1)}, bf16[2,4,2,2,64,512]{5,4,3,2,1,0:T(8,128)(2,1)}, f...) custom-call(bf16[512,1024]{1,0:T(8,128)(2,1)} %bitcast.58, ...), custom_call_target="tpu_custom_call" | custom-call | tf_op jit(solution)/shard_map/space_backward/pallas_call | solution.py:1418
  500.6 1.4 dynamic-slice_bitcast_fusion
  502.0 1.2 slice_bitcast_fusion.1
  503.3 1.4 dynamic-slice.3
  504.7 1.4 fusion.7
  506.1 2.3 copy.60
  508.3 2.3 copy.61
  510.6 0.7 copy.62
  511.3 0.7 copy.63
  512.0 0.7 copy.64
  513.4 0.8 copy.66
  514.2 0.8 copy.67
  (30 shorter events, 1.8 us)
Async XLA Ops:
  0.6 198.1 %copy-start.7 = (s32[2,1]{0,1:T(1,128)S(1)}, s32[2,1]{0,1:T(1,128)}, u32[]{:S(2)}) copy-start(s32[2,1]{0,1:T(1,128)} %param.18) | copy-start | bytes 28
  5.9 2.0 copy-start.6
  500.6 10.0 %copy-start.3 = (f32[64,1536]{1,0:T(8,128)S(1)}, f32[64,1536]{1,0:T(8,128)}, u32[]{:S(2)}) copy-start(f32[64,1536]{1,0:T(8,128)} %get-tuple-element.152) | copy-start | bytes 1179652
  500.6 10.7 %copy-start.5 = (f32[64,512]{1,0:T(8,128)S(1)}, f32[64,512]{1,0:T(8,128)}, u32[]{:S(2)}) copy-start(f32[64,512]{1,0:T(8,128)} %get-tuple-element.153) | copy-start | bytes 393220
  500.6 11.4 %copy-start.2 = (f32[64,1536]{1,0:T(8,128)S(1)}, f32[64,1536]{1,0:T(8,128)}, u32[]{:S(2)}) copy-start(f32[64,1536]{1,0:T(8,128)} %get-tuple-element.154) | copy-start | bytes 1179652
  500.6 12.1 %copy-start.4 = (f32[64,512]{1,0:T(8,128)S(1)}, f32[64,512]{1,0:T(8,128)}, u32[]{:S(2)}) copy-start(f32[64,512]{1,0:T(8,128)} %get-tuple-element.155) | copy-start | bytes 393220
  500.6 12.8 %copy-start.1 = (f32[64,2048]{1,0:T(8,128)S(1)}, f32[64,2048]{1,0:T(8,128)}, u32[]{:S(2)}) copy-start(f32[64,2048]{1,0:T(8,128)} %get-tuple-element.156) | copy-start | bytes 1572868
  500.6 13.6 %copy-start = (f32[256,512]{1,0:T(8,128)S(1)}, f32[256,512]{1,0:T(8,128)}, u32[]{:S(2)}) copy-start(f32[256,512]{1,0:T(8,128)} %get-tuple-element.157) | copy-start | bytes 1572868

commit v4 on v3

--- a/solution.py
+++ b/solution.py
@@ -557,7 +557,7 @@
 def attend_backward_work(spatial, tokens, up, stream, extra, gain, shift, packed_h, probs_h, mixed, w_in_h, w_out_h,
                          down, w_in_grad, w_out_grad, gain_out, shift_out, sums,
                          up_low, mixed_grad, packed_grad, normed_grad, packed, probs, w_in, w_out,
-                         in_stage, out_stage, sems):
+                         in_stage, out_stage, sems, have_grads=None, have_normed=None):
     read = spatial_reader(stream, extra, tokens) if spatial else (lambda rows: stream[rows, :].astype(jnp.float32))
     fetches = [
         Fetch(src, dst, sems.at[i]).start()
@@ -587,11 +587,15 @@
     yield from attention_backward(packed, probs, mixed_grad, packed_grad, tokens, units=8)
     fetches[3].wait()
     yield from outer(normed, packed_grad, w_in_grad, in_stage, sems.at[pl.ds(6, 2)], units=4)
+    if have_grads is not None:
+        have_grads()
 
     def emit_normed(columns, value):
         normed_grad[:, columns] = value
 
     yield from project_back(packed_grad, w_in, emit_normed, 256, units=4)
+    if have_normed is not None:
+        have_normed()
     block = down.shape[1]
 
     def put(index, value):
@@ -1024,10 +1028,10 @@
     return [[entry[-1] for entry in timed if entry[0] == time] for time in times]
 
 
-def piece_ticks(pieces, offsets):
+def piece_ticks(pieces, offsets, begun=()):
     timed = []
     for piece in pieces:
-        for e in range(piece.ticks + 1):
+        for e in range(2 if piece in begun else 0, piece.ticks + 1):
             own = offsets[piece.order[2]]
             when_at = own[e] if e < len(own) else own[-1] + e - len(own) + 1
             timed.append((when_at, functools.partial(piece.tick, e)))
@@ -1036,6 +1040,7 @@
 
 LATE = (0, 1, 4, 5, 6, 7, 8)
 OFFSETS = {"x": LATE, "y": LATE, "z": (0, 1, 1, 2, 3, 4, 5, 6, 7)}
+END_OFFSETS = OFFSETS
 PER_PIECE = 9
 
 
@@ -1387,16 +1392,23 @@
                 small_part[at + (slice(0, 16),)] = first
                 small_part[at + (slice(16, 32),)] = second.astype(low)
 
+    matrices = [piece for piece, (index, _, _, _) in zip(ends, plans[1]) if index < 2]
+
+    def early(event):
+        for piece in matrices:
+            piece.tick(event)
+
     def work():
         yield from attend_backward_work(
             True, tokens, up, stream, extra, gain, shift, packed_h, probs_h, mixed, w_in_h, w_out_h,
-            down, w_in_grad, w_out_grad, gain_out, shift_out, sums, *own
+            down, w_in_grad, w_out_grad, gain_out, shift_out, sums, *own,
+            have_grads=lambda: early(0), have_normed=lambda: early(1),
         )
         small_rows()
         yield
 
     weave(work(), piece_ticks(pieces, OFFSETS), units)
-    for events in piece_ticks(ends, OFFSETS):
+    for events in piece_ticks(ends, END_OFFSETS, matrices):
         for event in events:
             event()
     for piece in pieces + ends:
@@ -1441,7 +1453,7 @@
 
 ACTIONS = 8
 FRAMES = 16
-FORWARD = ((0, 0, 0, 1, 1, 2, 2), (0, 3, 6), (6,))
+FORWARD = ((0, 0, 0, 1, 1, 2, 2), (0, 3, 6), (14,))
 TIME_UNITS = (7, 6, 6, 4)
 SPACE_UNITS = (6, 4, 4, 4, 4, 2)
 

time: 519 us -> 504 us (0.971)
  Pallas kernels: 489 us -> 474 us
    pallas_call x1, Pallas kernels: 188 us -> 173 us  [forward(): pl.pallas_call(functools.partial(forward_kernel, tokens, group, micro, se...]
where the time goes in v4:
time: 504 us; the launch traced here: 500 us
  Pallas kernels  474 us (94%)
  local copies, waits for them, and re-layouts  19.9 us (4%)
    pallas_call x1, Pallas kernels, forward(): pl.pallas_call(functools.partial(forward_kernel, tokens, group, micro, se...  173 us
    pallas_call x1, Pallas kernels, time_backward(): pl.pallas_call(functools.partial(time_backward_kernel, tokens, micro, seq...  126 us
    pallas_call x1, Pallas kernels, space_backward(): pl.pallas_call(functools.partial(space_backward_kernel, tokens, seq_count...  116 us
    pallas_call x1, Pallas kernels, hidden_layer(): pl.pallas_call(functools.partial(hidden_kernel, micro, seq_count, dp_coun...  59.5 us

profile of v4, /device:TPU:0, one launch (start us, length us, event | category | flops | bytes accessed | tf_op | source)
XLA Modules:
  0.0 500.2 jit_solution(13574123935617898692)
XLA Ops:
  0.7 1.3 fusion.4.refs_1_.refs_10_
  2.0 0.7 reshape.373
  2.8 0.7 convert_bitcast_fusion
  3.5 2.2 concatenate.3
  6.1 0.9 copy.41
  7.0 0.9 and_convert_fusion.refs_2_
  7.9 173.1 %forward.1 = (bf16[2,4,2,2,32,128]{5,4,3,2,1,0:T(8,128)(2,1)}, bf16[2,4,2,2,64,1536]{5,4,3,2,1,0:T(8,128)(2,1)}, bf16[2,4,2,2,64,512]{5,4,3,2,1,0:T(8,128)(2,1)}...) custom-call(bf16[512,1024]{1,0:T(8,128)(2,1)} %bitcast.51, ...), custom_call_target="tpu_custom_call" | custom-call | tf_op jit(solution)/shard_map/forward/pallas_call | solution.py:1255
  181.0 0.9 convert_reduce_fusion
  182.2 0.7 reshape.375.up_bias
  183.5 0.8 fusion.refs_2_
  184.3 59.5 %hidden_layer.1 = (bf16[32,16,1024]{2,1,0:T(8,128)(2,1)}, f32[512,1024]{1,0:T(8,128)}, bf16[2,4,2,2,64,2048]{5,4,3,2,1,0:T(8,128)(2,1)}, bf16[2,4,2,2,256,512]{5...) custom-call(f32[512,1024]{1,0:T(8,128)} %get-tuple-element.49.stream, ...), custom_call_target="tpu_custom_call" | custom-call | tf_op jit(solution)/shard_map/hidden_layer/pallas_call | solution.py:739
  243.8 125.6 %time_backward.1 = (bf16[32,16,1024]{2,1,0:T(8,128)(2,1)}, bf16[2,4,2,2,64,1536]{5,4,3,2,1,0:T(8,128)(2,1)}, bf16[2,4,2,2,64,512]{5,4,3,2,1,0:T(8,128)(2,1)}, f3...) custom-call(f32[512,1024]{1,0:T(8,128)} %get-tuple-element.54.refs_0_, ...), custom_call_target="tpu_custom_call" | custom-call | tf_op jit(solution)/shard_map/time_backward/pallas_call | solution.py:1335
  369.3 116.2 %space_backward.1 = (bf16[32,16,1024]{2,1,0:T(8,128)(2,1)}, bf16[2,4,2,2,64,1536]{5,4,3,2,1,0:T(8,128)(2,1)}, bf16[2,4,2,2,64,512]{5,4,3,2,1,0:T(8,128)(2,1)}, f...) custom-call(bf16[512,1024]{1,0:T(8,128)(2,1)} %bitcast.58, ...), custom_call_target="tpu_custom_call" | custom-call | tf_op jit(solution)/shard_map/space_backward/pallas_call | solution.py:1430
  485.6 1.4 dynamic-slice_bitcast_fusion
  487.0 1.2 slice_bitcast_fusion.1
  488.3 1.4 dynamic-slice.3
  489.6 1.4 fusion.7
  491.0 2.3 copy.60
  493.3 2.3 copy.61
  495.6 0.7 copy.62
  496.3 0.7 copy.63
  497.0 0.7 copy.64
  498.4 0.8 copy.66
  499.2 0.8 copy.67
  (30 shorter events, 1.8 us)
Async XLA Ops:
  0.6 182.8 %copy-start.7 = (s32[2,1]{0,1:T(1,128)S(1)}, s32[2,1]{0,1:T(1,128)}, u32[]{:S(2)}) copy-start(s32[2,1]{0,1:T(1,128)} %param.18) | copy-start | bytes 28
  5.9 2.0 copy-start.6
  485.6 10.0 %copy-start.3 = (f32[64,1536]{1,0:T(8,128)S(1)}, f32[64,1536]{1,0:T(8,128)}, u32[]{:S(2)}) copy-start(f32[64,1536]{1,0:T(8,128)} %get-tuple-element.152) | copy-start | bytes 1179652
  485.6 10.7 %copy-start.5 = (f32[64,512]{1,0:T(8,128)S(1)}, f32[64,512]{1,0:T(8,128)}, u32[]{:S(2)}) copy-start(f32[64,512]{1,0:T(8,128)} %get-tuple-element.153) | copy-start | bytes 393220
  485.6 11.4 %copy-start.2 = (f32[64,1536]{1,0:T(8,128)S(1)}, f32[64,1536]{1,0:T(8,128)}, u32[]{:S(2)}) copy-start(f32[64,1536]{1,0:T(8,128)} %get-tuple-element.154) | copy-start | bytes 1179652
  485.6 12.1 %copy-start.4 = (f32[64,512]{1,0:T(8,128)S(1)}, f32[64,512]{1,0:T(8,128)}, u32[]{:S(2)}) copy-start(f32[64,512]{1,0:T(8,128)} %get-tuple-element.155) | copy-start | bytes 393220
  485.6 12.8 %copy-start.1 = (f32[64,2048]{1,0:T(8,128)S(1)}, f32[64,2048]{1,0:T(8,128)}, u32[]{:S(2)}) copy-start(f32[64,2048]{1,0:T(8,128)} %get-tuple-element.156) | copy-start | bytes 1572868
  485.6 13.6 %copy-start = (f32[256,512]{1,0:T(8,128)S(1)}, f32[256,512]{1,0:T(8,128)}, u32[]{:S(2)}) copy-start(f32[256,512]{1,0:T(8,128)} %get-tuple-element.157) | copy-start | bytes 1572868

commit v5 on v4

--- a/solution.py
+++ b/solution.py
@@ -680,7 +680,7 @@
         ended = stream[:, columns] + value + down_bias[:, columns]
         out[:, :, columns] = (ended * live[...]).astype(low).reshape(tokens // block, block, -1)
 
-    drain(project(active, w_down, emit_out, 256))
+    drain(project(active, w_down, emit_out, 512))
     home.start()
     end.finish()
 
@@ -710,7 +710,7 @@
     def emit_normed(columns, value):
         normed_grad[:, columns] = value
 
-    drain(project_back(expand_low, w_up, emit_normed, 256))
+    drain(project_back(expand_low, w_up, emit_normed, 512))
 
     def write(index, rows, value):
         down[rows, :] = value

time: 504 us -> 503 us (level)
  no operation moved by 1% of the time
where the time goes in v5:
time: 503 us; the launch traced here: 500 us
  Pallas kernels  474 us (94%)
  local copies, waits for them, and re-layouts  19.9 us (4%)
    pallas_call x1, Pallas kernels, forward(): pl.pallas_call(functools.partial(forward_kernel, tokens, group, micro, se...  173 us
    pallas_call x1, Pallas kernels, time_backward(): pl.pallas_call(functools.partial(time_backward_kernel, tokens, micro, seq...  126 us
    pallas_call x1, Pallas kernels, space_backward(): pl.pallas_call(functools.partial(space_backward_kernel, tokens, seq_count...  116 us
    pallas_call x1, Pallas kernels, hidden_layer(): pl.pallas_call(functools.partial(hidden_kernel, micro, seq_count, dp_coun...  58.4 us

profile of v5, /device:TPU:0, one launch (start us, length us, event | category | flops | bytes accessed | tf_op | source)
XLA Modules:
  0.0 499.5 jit_solution(13349533940432182653)
XLA Ops:
  0.7 1.3 fusion.4.refs_1_.refs_10_
  2.0 0.7 reshape.373
  2.8 0.7 convert_bitcast_fusion
  3.5 2.2 concatenate.3
  6.1 0.9 copy.41
  7.0 0.9 and_convert_fusion.refs_2_
  7.9 173.1 %forward.1 = (bf16[2,4,2,2,32,128]{5,4,3,2,1,0:T(8,128)(2,1)}, bf16[2,4,2,2,64,1536]{5,4,3,2,1,0:T(8,128)(2,1)}, bf16[2,4,2,2,64,512]{5,4,3,2,1,0:T(8,128)(2,1)}...) custom-call(bf16[512,1024]{1,0:T(8,128)(2,1)} %bitcast.51, ...), custom_call_target="tpu_custom_call" | custom-call | tf_op jit(solution)/shard_map/forward/pallas_call | solution.py:1255
  181.0 0.9 convert_reduce_fusion
  182.2 0.7 reshape.375.up_bias
  183.5 0.8 fusion.refs_2_
  184.3 58.4 %hidden_layer.1 = (bf16[32,16,1024]{2,1,0:T(8,128)(2,1)}, f32[512,1024]{1,0:T(8,128)}, bf16[2,4,2,2,64,2048]{5,4,3,2,1,0:T(8,128)(2,1)}, bf16[2,4,2,2,256,512]{5...) custom-call(f32[512,1024]{1,0:T(8,128)} %get-tuple-element.49.stream, ...), custom_call_target="tpu_custom_call" | custom-call | tf_op jit(solution)/shard_map/hidden_layer/pallas_call | solution.py:739
  242.7 126.1 %time_backward.1 = (bf16[32,16,1024]{2,1,0:T(8,128)(2,1)}, bf16[2,4,2,2,64,1536]{5,4,3,2,1,0:T(8,128)(2,1)}, bf16[2,4,2,2,64,512]{5,4,3,2,1,0:T(8,128)(2,1)}, f3...) custom-call(f32[512,1024]{1,0:T(8,128)} %get-tuple-element.54.refs_0_, ...), custom_call_target="tpu_custom_call" | custom-call | tf_op jit(solution)/shard_map/time_backward/pallas_call | solution.py:1335
  368.8 116.1 %space_backward.1 = (bf16[32,16,1024]{2,1,0:T(8,128)(2,1)}, bf16[2,4,2,2,64,1536]{5,4,3,2,1,0:T(8,128)(2,1)}, bf16[2,4,2,2,64,512]{5,4,3,2,1,0:T(8,128)(2,1)}, f...) custom-call(bf16[512,1024]{1,0:T(8,128)(2,1)} %bitcast.58, ...), custom_call_target="tpu_custom_call" | custom-call | tf_op jit(solution)/shard_map/space_backward/pallas_call | solution.py:1430
  485.0 1.4 dynamic-slice_bitcast_fusion
  486.4 1.2 slice_bitcast_fusion.1
  487.7 1.4 dynamic-slice.3
  489.0 1.4 fusion.7
  490.4 2.3 copy.60
  492.7 2.3 copy.61
  494.9 0.7 copy.62
  495.7 0.7 copy.63
  496.3 0.7 copy.64
  497.8 0.8 copy.66
  498.6 0.8 copy.67
  (30 shorter events, 1.8 us)
Async XLA Ops:
  0.6 182.8 %copy-start.7 = (s32[2,1]{0,1:T(1,128)S(1)}, s32[2,1]{0,1:T(1,128)}, u32[]{:S(2)}) copy-start(s32[2,1]{0,1:T(1,128)} %param.18) | copy-start | bytes 28
  5.9 2.0 copy-start.6
  484.9 10.0 %copy-start.3 = (f32[64,1536]{1,0:T(8,128)S(1)}, f32[64,1536]{1,0:T(8,128)}, u32[]{:S(2)}) copy-start(f32[64,1536]{1,0:T(8,128)} %get-tuple-element.152) | copy-start | bytes 1179652
  484.9 10.7 %copy-start.5 = (f32[64,512]{1,0:T(8,128)S(1)}, f32[64,512]{1,0:T(8,128)}, u32[]{:S(2)}) copy-start(f32[64,512]{1,0:T(8,128)} %get-tuple-element.153) | copy-start | bytes 393220
  485.0 11.4 %copy-start.2 = (f32[64,1536]{1,0:T(8,128)S(1)}, f32[64,1536]{1,0:T(8,128)}, u32[]{:S(2)}) copy-start(f32[64,1536]{1,0:T(8,128)} %get-tuple-element.154) | copy-start | bytes 1179652
  485.0 12.1 %copy-start.4 = (f32[64,512]{1,0:T(8,128)S(1)}, f32[64,512]{1,0:T(8,128)}, u32[]{:S(2)}) copy-start(f32[64,512]{1,0:T(8,128)} %get-tuple-element.155) | copy-start | bytes 393220
  485.0 12.8 %copy-start.1 = (f32[64,2048]{1,0:T(8,128)S(1)}, f32[64,2048]{1,0:T(8,128)}, u32[]{:S(2)}) copy-start(f32[64,2048]{1,0:T(8,128)} %get-tuple-element.156) | copy-start | bytes 1572868
  485.0 13.6 %copy-start = (f32[256,512]{1,0:T(8,128)S(1)}, f32[256,512]{1,0:T(8,128)}, u32[]{:S(2)}) copy-start(f32[256,512]{1,0:T(8,128)} %get-tuple-element.157) | copy-start | bytes 1572868
